TPU v7x, 32 devices: a whole 2x2x4 slice. The times are simulated.
32 devices in a mesh: dp: 4 (over x, core), mp: 8 (over z, y).
Axes of the slice: x: 2, y: 2, z: 4, core: 2. Of those that a mesh axis runs over, the one named last changes fastest.
Arguments:
- stream_in: bfloat16 [32, 256, 2048], P('dp', 'mp'), may hold values from -6 to 6
- cotangent: float32 [32, 256, 2048], P('dp', 'mp'), may hold values from -6 to 6
- noise_table: float32 [32, 6, 2048], replicated, may hold values from -1.2 to 2.9, as said below
- timesteps: int32 [32], P('dp'), may hold values from 0 to 31
- bins: int32 [32], P('dp'), may hold values from 0 to 7
- counts: int32 [4], P('dp'), may hold values from 4 to 8, as said below
- w_qkv: float32 [2048, 3, 2048], P('dp', None, 'mp'), may hold values from -0.11932427 to 0.11932427
- w_out: float32 [2048, 2048], P('mp', 'dp'), may hold values from -0.5 to 0.5
- w_up: float32 [2048, 8192], P('dp', 'mp'), may hold values from -0.13258252 to 0.13258252
- w_down: float32 [8192, 2048], P('mp', 'dp'), may hold values from -0.0625 to 0.0625
- m_qkv: float32 [2048, 3, 2048], P('dp', None, 'mp'), may hold values from -0.00024414062 to 0.00024414062
- m_out: float32 [2048, 2048], P('mp', 'dp'), may hold values from -0.00024414062 to 0.00024414062
- m_up: float32 [2048, 8192], P('dp', 'mp'), may hold values from -0.00024414062 to 0.00024414062
- m_down: float32 [8192, 2048], P('mp', 'dp'), may hold values from -0.00024414062 to 0.00024414062
- v_qkv: float32 [2048, 3, 2048], P('dp', None, 'mp'), may hold values from 1.0450681e-09 to 4.172325e-09
- v_out: float32 [2048, 2048], P('mp', 'dp'), may hold values from 1.0450681e-09 to 4.172325e-09
- v_up: float32 [2048, 8192], P('dp', 'mp'), may hold values from 1.0450681e-09 to 4.172325e-09
- v_down: float32 [8192, 2048], P('mp', 'dp'), may hold values from 1.0450681e-09 to 4.172325e-09
Outputs:
- output: bfloat16 [32, 256, 2048], P('dp', 'mp')
- input_grad: float32 [32, 256, 2048], P('dp', 'mp')
- grad_norm: float32 [], replicated
- new_m_qkv: float32 [2048, 3, 2048], P('dp', None, 'mp')
- new_m_out: float32 [2048, 2048], P('mp', 'dp')
- new_m_up: float32 [2048, 8192], P('dp', 'mp')
- new_m_down: float32 [8192, 2048], P('mp', 'dp')
- new_v_qkv: float32 [2048, 3, 2048], P('dp', None, 'mp')
- new_v_out: float32 [2048, 2048], P('mp', 'dp')
- new_v_up: float32 [2048, 8192], P('dp', 'mp')
- new_v_down: float32 [8192, 2048], P('mp', 'dp')
- new_w_qkv: float32 [2048, 3, 2048], P('dp', None, 'mp')
- new_w_out: float32 [2048, 2048], P('mp', 'dp')
- new_w_up: float32 [2048, 8192], P('dp', 'mp')
- new_w_down: float32 [8192, 2048], P('mp', 'dp')
Inputs may be any that keep to these rules, and one draw needn't show every extreme that they name: `counts`: on every index of dp the live images fill its first slots; at least one index of dp has all 8 slots live in every draw. `noise_table`: rows 1, 2, 4, 5 of every timestep are positive.
All inputs are finite; a program needn't handle non-finite values.
Results may differ from a plain program's by a relative error of at most 0.022.
Values may be sent and summed in bfloat16 or wider, within the bound.
No kernel may reach another device: no remote copies, remote signals or barrier semaphores. Data moves between devices by JAX's collectives and lax.ppermute only.
A program may use at most 192 MiB of HBM per device.

v0:
```python
import jax
import jax.numpy as jnp
from jax import lax
from jax.sharding import PartitionSpec as P

HD = 128
BINS = 8
ADAM_STEP = 10


clip_limit = 1.0
beta_one = 0.9
beta_two = 0.95
learn_rate = 0.02
output_rate = 0.08
adam_epsilon = 1e-08
decay_rate = 0.01


def norm_rows(values):
    center = values - jnp.mean(values, axis=-1, keepdims=True)
    spread = jnp.mean(center * center, axis=-1, keepdims=True)
    return center * lax.rsqrt(spread + 1e-06)


def gelu_tanh(values):
    return jax.nn.gelu(values, approximate=True)


def adam_update(gradient, moment_one, moment_two, weight, factor, step_rate):
    clipped = gradient * factor
    new_one = beta_one * moment_one + (1.0 - beta_one) * clipped
    new_two = beta_two * moment_two + (1.0 - beta_two) * clipped * clipped
    corrected = new_one / (1.0 - beta_one**ADAM_STEP)
    root_two = jnp.sqrt(new_two / (1.0 - beta_two**ADAM_STEP))
    new_weight = weight - step_rate * (corrected / (root_two + adam_epsilon) + decay_rate * weight)
    return (new_one, new_two, new_weight)


def attention_probs(queries, keys_all):
    scores = jnp.einsum(
        "sqhe,skhe->shqk", queries, keys_all, preferred_element_type=jnp.float32
    ) * HD ** (-0.5)
    highest_precision = jnp.max(scores, axis=-1, keepdims=True)
    totals = jnp.sum(jnp.exp(scores - highest_precision), axis=-1, keepdims=True)
    return (scores, highest_precision + jnp.log(totals))


def forward(
    stream,
    modulation,
    complete_query_key_value,
    complete_out_weight,
    complete_up_weight,
    complete_down_weight,
):
    slot_count = stream.shape[0]
    attention_input = (norm_rows(stream) * modulation[:, 1:2] + modulation[:, 0:1]).astype(
        jnp.bfloat16
    )
    collected_rows = lax.all_gather(attention_input, "mp", axis=1, tiled=True)
    length = collected_rows.shape[1]
    heads_here = complete_query_key_value.shape[2] // HD
    projection_output = jnp.einsum(
        "ojb,bth->ojth",
        collected_rows,
        complete_query_key_value,
        preferred_element_type=jnp.float32,
    ).astype(jnp.bfloat16)
    queries = projection_output[:, :, 0].reshape(slot_count, length, heads_here, HD)
    keys_all = projection_output[:, :, 1].reshape(slot_count, length, heads_here, HD)
    values_all = projection_output[:, :, 2].reshape(slot_count, length, heads_here, HD)
    scores, log_total = attention_probs(queries, keys_all)
    attn_probs = jnp.exp(scores - log_total).astype(jnp.bfloat16)
    attention_result = jnp.einsum(
        "shqk,skhe->sqhe", attn_probs, values_all, preferred_element_type=jnp.float32
    ).astype(jnp.bfloat16)
    attention_result = attention_result.reshape(slot_count, length, heads_here * HD)
    attention_portion = jnp.einsum(
        "ybo,oh->ybh", attention_result, complete_out_weight, preferred_element_type=jnp.float32
    )
    attention_partial_sum = lax.psum_scatter(
        attention_portion, "mp", scatter_dimension=1, tiled=True
    )
    residual = stream + modulation[:, 2:3] * attention_partial_sum
    perceptron_input = (norm_rows(residual) * modulation[:, 4:5] + modulation[:, 3:4]).astype(
        jnp.bfloat16
    )
    perceptron_rows = lax.all_gather(perceptron_input, "mp", axis=1, tiled=True)
    expanded_preactivation = jnp.einsum(
        "bno,oj->bnj", perceptron_rows, complete_up_weight, preferred_element_type=jnp.float32
    )
    hidden_state = gelu_tanh(expanded_preactivation).astype(jnp.bfloat16)
    perceptron_portion = jnp.einsum(
        "ybo,oh->ybh", hidden_state, complete_down_weight, preferred_element_type=jnp.float32
    )
    perceptron_partial_sum = lax.psum_scatter(
        perceptron_portion.astype(jnp.bfloat16), "mp", scatter_dimension=1, tiled=True
    ).astype(jnp.float32)
    result = residual + modulation[:, 5:6] * perceptron_partial_sum
    kept = (
        collected_rows,
        queries,
        keys_all,
        values_all,
        log_total,
        attention_result,
        residual,
        perceptron_rows,
        expanded_preactivation,
        hidden_state,
    )
    return (result, kept)


def per_device(
    stream_in,
    cotangent,
    noise_table,
    timesteps,
    bins,
    counts,
    w_qkv,
    w_out,
    w_up,
    w_down,
    m_qkv,
    m_out,
    m_up,
    m_down,
    v_qkv,
    v_out,
    v_up,
    v_down,
):
    slot_count = stream_in.shape[0]
    table_rows = noise_table.shape[0]
    picks = (timesteps[:, None] == jnp.arange(table_rows)[None, :]).astype(jnp.float32)
    modulation = jnp.dot(
        picks, noise_table.reshape(table_rows, -1), precision=lax.Precision.HIGHEST
    ).reshape(slot_count, 6, -1)
    complete_query_key_value, complete_out_weight, complete_up_weight, complete_down_weight = (
        lax.all_gather(w_qkv.astype(jnp.bfloat16), "dp", axis=0, tiled=True),
        lax.all_gather(w_out.astype(jnp.bfloat16), "dp", axis=1, tiled=True),
        lax.all_gather(w_up.astype(jnp.bfloat16), "dp", axis=0, tiled=True),
        lax.all_gather(w_down.astype(jnp.bfloat16), "dp", axis=1, tiled=True),
    )
    stream = stream_in.astype(jnp.float32)
    result, kept = forward(
        stream,
        modulation,
        complete_query_key_value,
        complete_out_weight,
        complete_up_weight,
        complete_down_weight,
    )
    spare_result, kept = forward(
        stream,
        modulation,
        complete_query_key_value,
        complete_out_weight,
        complete_up_weight,
        complete_down_weight,
    )
    (
        collected_rows,
        queries,
        keys_all,
        values_all,
        log_total,
        attention_result,
        residual,
        perceptron_rows,
        expanded_preactivation,
        hidden_state,
    ) = kept
    output = result.astype(jnp.bfloat16)
    live = (jnp.arange(slot_count) < counts[0]).astype(jnp.float32)
    loss_scale = live * (bins.astype(jnp.float32) + 1.0) / BINS
    seed_grad = cotangent * loss_scale[:, None, None]
    mlp_grad = (modulation[:, 5:6] * seed_grad).astype(jnp.bfloat16)
    perceptron_gradient_rows = lax.all_gather(mlp_grad, "mp", axis=1, tiled=True)
    down_gradient = jnp.einsum(
        "xin,xie->ne", hidden_state, perceptron_gradient_rows, preferred_element_type=jnp.float32
    )
    hidden_grad = jnp.einsum(
        "wcb,pb->wcp",
        perceptron_gradient_rows,
        complete_down_weight,
        preferred_element_type=jnp.float32,
    )
    gelu_value, gelu_pull = jax.vjp(gelu_tanh, expanded_preactivation)
    expanded_gradient = gelu_pull(hidden_grad)[0].astype(jnp.bfloat16)
    up_gradient = jnp.einsum(
        "yna,ynz->az", perceptron_rows, expanded_gradient, preferred_element_type=jnp.float32
    )
    perceptron_input_gradient = jnp.einsum(
        "qhu,gu->qhg", expanded_gradient, complete_up_weight, preferred_element_type=jnp.float32
    )
    mlp_in_sum = lax.psum_scatter(
        perceptron_input_gradient.astype(jnp.bfloat16), "mp", scatter_dimension=1, tiled=True
    ).astype(jnp.float32)

    def second_norm(rows):
        return norm_rows(rows) * modulation[:, 4:5] + modulation[:, 3:4]

    norm_value, norm_pull = jax.vjp(second_norm, residual)
    residual_grad = seed_grad + norm_pull(mlp_in_sum)[0]
    attn_grad = (modulation[:, 2:3] * residual_grad).astype(jnp.bfloat16)
    attention_gradient_rows = lax.all_gather(attn_grad, "mp", axis=1, tiled=True)
    grad_out = jnp.einsum(
        "xin,xie->ne", attention_result, attention_gradient_rows, preferred_element_type=jnp.float32
    )
    length = attention_gradient_rows.shape[1]
    heads_here = complete_query_key_value.shape[2] // HD
    attended_grad = jnp.einsum(
        "wcb,pb->wcp",
        attention_gradient_rows,
        complete_out_weight,
        preferred_element_type=jnp.float32,
    ).astype(jnp.bfloat16)
    attended_grad = attended_grad.reshape(slot_count, length, heads_here, HD)
    scores, spare_total = attention_probs(queries, keys_all)
    attn_probs = jnp.exp(scores - log_total)
    values_grad = jnp.einsum(
        "shqk,sqhe->skhe",
        attn_probs.astype(jnp.bfloat16),
        attended_grad,
        preferred_element_type=jnp.float32,
    )
    probs_grad = jnp.einsum(
        "sqhe,skhe->shqk", attended_grad, values_all, preferred_element_type=jnp.float32
    )
    inner_sum = jnp.sum(attn_probs * probs_grad, axis=-1, keepdims=True)
    scores_grad = (attn_probs * (probs_grad - inner_sum)).astype(jnp.bfloat16)
    queries_grad = jnp.einsum(
        "shqk,skhe->sqhe", scores_grad, keys_all, preferred_element_type=jnp.float32
    ) * HD ** (-0.5)
    keys_grad = jnp.einsum(
        "shqk,sqhe->skhe", scores_grad, queries, preferred_element_type=jnp.float32
    ) * HD ** (-0.5)
    projection_output_gradient = (
        jnp.stack((queries_grad, keys_grad, values_grad), axis=2)
        .reshape(slot_count, length, 3, heads_here * HD)
        .astype(jnp.bfloat16)
    )
    grad_qkv = jnp.einsum(
        "kze,kzwg->ewg",
        collected_rows,
        projection_output_gradient,
        preferred_element_type=jnp.float32,
    )
    attn_in_grad = jnp.einsum(
        "yjvw,tvw->yjt",
        projection_output_gradient,
        complete_query_key_value,
        preferred_element_type=jnp.float32,
    )
    attn_in_sum = lax.psum_scatter(
        attn_in_grad.astype(jnp.bfloat16), "mp", scatter_dimension=1, tiled=True
    ).astype(jnp.float32)

    def first_norm(rows):
        return norm_rows(rows) * modulation[:, 1:2] + modulation[:, 0:1]

    first_value, first_pull = jax.vjp(first_norm, stream)
    input_grad = residual_grad + first_pull(attn_in_sum)[0]
    owned_qkv, owned_out, owned_up, owned_down = (
        lax.psum_scatter(
            grad_qkv.astype(jnp.bfloat16), "dp", scatter_dimension=0, tiled=True
        ).astype(jnp.float32),
        lax.psum_scatter(
            grad_out.astype(jnp.bfloat16), "dp", scatter_dimension=1, tiled=True
        ).astype(jnp.float32),
        lax.psum_scatter(
            up_gradient.astype(jnp.bfloat16), "dp", scatter_dimension=0, tiled=True
        ).astype(jnp.float32),
        lax.psum_scatter(
            down_gradient.astype(jnp.bfloat16), "dp", scatter_dimension=1, tiled=True
        ).astype(jnp.float32),
    )
    local_squares = (
        jnp.sum(owned_qkv * owned_qkv)
        + jnp.sum(owned_out * owned_out)
        + jnp.sum(owned_up * owned_up)
        + jnp.sum(owned_down * owned_down)
    )
    grad_norm = jnp.sqrt(lax.psum(local_squares, ("dp", "mp")))
    factor = jnp.minimum(1.0, clip_limit / (grad_norm + 1e-06))
    one_qkv, two_qkv, new_qkv = adam_update(owned_qkv, m_qkv, v_qkv, w_qkv, factor, learn_rate)
    one_out, two_out, new_out = adam_update(owned_out, m_out, v_out, w_out, factor, output_rate)
    one_up, two_up, new_up = adam_update(owned_up, m_up, v_up, w_up, factor, learn_rate)
    one_down, two_down, new_down = adam_update(
        owned_down, m_down, v_down, w_down, factor, learn_rate
    )
    return (
        output,
        input_grad,
        grad_norm,
        one_qkv,
        one_out,
        one_up,
        one_down,
        two_qkv,
        two_out,
        two_up,
        two_down,
        new_qkv,
        new_out,
        new_up,
        new_down,
    )


def solution(mesh):
    in_specs = (
        P("dp", "mp", None),
        P("dp", "mp", None),
        P(),
        P("dp"),
        P("dp"),
        P("dp"),
        P("dp", None, "mp"),
        P("mp", "dp"),
        P("dp", "mp"),
        P("mp", "dp"),
        P("dp", None, "mp"),
        P("mp", "dp"),
        P("dp", "mp"),
        P("mp", "dp"),
        P("dp", None, "mp"),
        P("mp", "dp"),
        P("dp", "mp"),
        P("mp", "dp"),
    )
    out_specs = (
        P("dp", "mp", None),
        P("dp", "mp", None),
        P(),
        P("dp", None, "mp"),
        P("mp", "dp"),
        P("dp", "mp"),
        P("mp", "dp"),
        P("dp", None, "mp"),
        P("mp", "dp"),
        P("dp", "mp"),
        P("mp", "dp"),
        P("dp", None, "mp"),
        P("mp", "dp"),
        P("dp", "mp"),
        P("mp", "dp"),
    )
    return jax.shard_map(
        per_device, mesh=mesh, in_specs=in_specs, out_specs=out_specs, check_vma=False
    )
```

profile of v0, /device:TPU:0, one launch (start us, length us, event | category | flops | bytes accessed | tf_op | source)
XLA Modules:
  0.0 1595.5 jit_solution(3651183792545015086)
XLA Ops:
  14.5 27.0 %all-gather.11.cloned.1.call-done = bf16[2048,3,256]{0,2,1:T(8,128)(2,1)} async-done(((bf16[512,3,256]{0,2,1:T(8,128)(2,1)}), bf16[2048,3,256]{0,2,1:T(8,128)(2,1)}) %all-gather.11.cloned.1.call-update) | async-done | bytes 3145744 | tf_op jit(solution)/shard_map/all_gather | solution.py:143
  41.5 127.7 %all-gather.9.cloned.1.call-done = bf16[8,256,2048]{2,1,0:T(8,128)(2,1)} async-done(((bf16[8,32,2048]{2,1,0:T(8,128)(2,1)}), bf16[8,256,2048]{2,1,0:T(8,128)(2,1)}) %all-gather.9.cloned.1.call-update) | async-done | bytes 8388624 | tf_op jit(solution)/shard_map/all_gather | solution.py:61
  169.2 10.1 fusion.28
  198.8 279.3 %reduce-scatter.9.cloned.1.call-done = f32[8,32,2048]{2,1,0:T(8,128)} async-done(((f32[8,256,2048]{2,1,0:T(8,128)}), f32[8,32,2048]{2,1,0:T(8,128)}) %reduce-scatter.9.cloned.1.call-update) | async-done | bytes 2097168 | tf_op jit(solution)/shard_map/reduce_scatter | solution.py:82
  489.7 23.9 %all-gather.17.cloned.1.call-done = bf16[2048,1024]{1,0:T(8,128)(2,1)} async-done(((bf16[512,1024]{1,0:T(8,128)(2,1)}), bf16[2048,1024]{1,0:T(8,128)(2,1)}) %all-gather.17.cloned.1.call-update) | async-done | bytes 4194320 | tf_op jit(solution)/shard_map/all_gather | solution.py:145
  513.7 127.8 %all-gather.15.cloned.1.call-done = bf16[8,256,2048]{2,1,0:T(8,128)(2,1)} async-done(((bf16[8,32,2048]{2,1,0:T(8,128)(2,1)}), bf16[8,256,2048]{2,1,0:T(8,128)(2,1)}) %all-gather.15.cloned.1.call-update) | async-done | bytes 8388624 | tf_op jit(solution)/shard_map/all_gather | solution.py:89
  641.5 14.4 fusion.14
  655.9 20.5 %all-gather.19.cloned.1.call-done = bf16[1024,2048]{1,0:T(8,128)(2,1)} async-done(((bf16[1024,512]{1,0:T(8,128)(2,1)}), bf16[1024,2048]{1,0:T(8,128)(2,1)}) %all-gather.19.cloned.1.call-update) | async-done | bytes 4194320 | tf_op jit(solution)/shard_map/all_gather | solution.py:146
  676.4 127.9 %all-gather.21.cloned.1.call-done = bf16[8,256,2048]{2,1,0:T(8,128)(2,1)} async-done(((bf16[8,32,2048]{2,1,0:T(8,128)(2,1)}), bf16[8,256,2048]{2,1,0:T(8,128)(2,1)}) %all-gather.21.cloned.1.call-update) | async-done | bytes 8388624 | tf_op jit(solution)/shard_map/all_gather | solution.py:182
  804.3 19.5 %fusion.6 = bf16[8,256,1024]{2,1,0:T(8,128)(2,1)S(1)} fusion(f32[8,256,1024]{2,1,0:T(8,128)} %fusion.14, bf16[8,256,2048]{2,1,0:T(8,128)(2,1)} %all-gather.21.cloned.1.call-done, bf16[1024,2048]{1,0:T(8,128)(2,1)} %all-gather.19.cloned.1.call-done), kind=kOutput, calls=%fused_computation.9 | convolution fusion | flops 8631877632 | bytes 25165824 | tf_op jit(solution)/shard_map/wcb,pb->wcp/dot_general | solution.py:186
  825.9 11.5 convolution_convert_fusion
  837.4 147.3 %reduce-scatter.13.cloned.1.call-done = bf16[8,32,2048]{2,1,0:T(8,128)(2,1)} async-done(((bf16[8,256,2048]{2,1,0:T(8,128)(2,1)}), bf16[8,32,2048]{2,1,0:T(8,128)(2,1)}) %reduce-scatter.13.cloned.1.call-update) | async-done | bytes 1048592 | tf_op jit(solution)/shard_map/reduce_scatter | solution.py:200
  991.8 14.0 bitcast_convert_fusion.2
  1005.9 16.3 %bitcast_convert_fusion.1 = bf16[1024,2048]{1,0:T(8,128)(2,1)} fusion(bf16[8,256,2048]{2,1,0:T(8,128)(2,1)} %all-gather.21.cloned.1.call-done, f32[8,256,1024]{2,1,0:T(8,128)} %fusion.14), kind=kOutput, calls=%fused_computation.14 | convolution fusion | flops 8610906112 | bytes 20971520 | tf_op jit(solution)/shard_map/xin,xie->ne/dot_general | solution.py:183
  1022.3 93.5 %all-gather.23.cloned.1.call-done = bf16[8,256,2048]{2,1,0:T(8,128)(2,1)} async-done(((bf16[8,32,2048]{2,1,0:T(8,128)(2,1)}), bf16[8,256,2048]{2,1,0:T(8,128)(2,1)}) %all-gather.23.cloned.1.call-update) | async-done | bytes 8388624 | tf_op jit(solution)/shard_map/all_gather | solution.py:210
  1145.4 11.1 bitcast_convert_fusion.3
  1157.7 10.9 bitcast_convert_fusion
  1168.7 16.4 %convolution_convert_fusion.1 = bf16[8,256,2048]{2,1,0:T(8,128)(2,1)} fusion(bf16[1024,2048]{1,0:T(8,128)(2,1)} %all-gather.19.cloned.1.call-done, f32[8,256,1024]{2,1,0:T(8,128)} %fusion.14), kind=kOutput, calls=%fused_computation.19 | convolution fusion | flops 8613003264 | bytes 20971520 | tf_op jit(solution)/shard_map/ybo,oh->ybh/dot_general | solution.py:94
  1187.7 20.5 %reduce-scatter.23.cloned.1.call-done = bf16[1024,512]{1,0:T(8,128)(2,1)} async-done(((bf16[1024,2048]{1,0:T(8,128)(2,1)}), bf16[1024,512]{1,0:T(8,128)(2,1)}) %reduce-scatter.23.cloned.1.call-update) | async-done | bytes 1048592 | tf_op jit(solution)/shard_map/reduce_scatter | solution.py:278
  1210.5 25.7 %reduce-scatter.19.cloned.1.call-done = bf16[256,512]{1,0:T(8,128)(2,1)} async-done(((bf16[256,2048]{1,0:T(8,128)(2,1)}), bf16[256,512]{1,0:T(8,128)(2,1)}) %reduce-scatter.19.cloned.1.call-update) | async-done | bytes 262160 | tf_op jit(solution)/shard_map/reduce_scatter | solution.py:272
  1237.9 38.8 %reduce-scatter.17.cloned.1.call-done = bf16[512,3,256]{2,0,1:T(8,128)(2,1)} async-done(((bf16[2048,3,256]{2,0,1:T(8,128)(2,1)}), bf16[512,3,256]{2,0,1:T(8,128)(2,1)}) %reduce-scatter.17.cloned.1.call-update) | async-done | bytes 786448 | tf_op jit(solution)/shard_map/reduce_scatter | solution.py:269
  1281.5 42.8 %psum.7 = f32[]{:T(128)} all-reduce(f32[]{:T(128)S(6)} %add.197), channel_id=1, replica_groups=mesh['dp'=4,'mp'=8] {'dp','mp'}, use_global_device_ids=true, to_apply=%region_23.0 | all-reduce | flops 1 | bytes 8 | tf_op jit(solution)/shard_map/psum | solution.py:288
  1342.2 88.0 %reduce-scatter.15.cloned.1.call-done = bf16[8,32,2048]{2,1,0:T(8,128)(2,1)} async-done(((bf16[8,256,2048]{2,1,0:T(8,128)(2,1)}), bf16[8,32,2048]{2,1,0:T(8,128)(2,1)}) %reduce-scatter.15.cloned.1.call-update) | async-done | bytes 1048592 | tf_op jit(solution)/shard_map/reduce_scatter | solution.py:259
  1432.8 149.4 %reduce-scatter.11.cloned.1.call-done = bf16[8,32,2048]{2,1,0:T(8,128)(2,1)} async-done(((bf16[8,256,2048]{2,1,0:T(8,128)(2,1)}), bf16[8,32,2048]{2,1,0:T(8,128)(2,1)}) %reduce-scatter.11.cloned.1.call-update) | async-done | bytes 1048592 | tf_op jit(solution)/shard_map/reduce_scatter | solution.py:97
  (212 shorter events, 110.9 us)
Async XLA Ops:
  7.2 34.2 %all-gather.11.cloned.1.call-start = ((), (), s32[]{:S(2)}) async-start(), calls=%async_computation.9 | async-start | bytes 3932160 | tf_op jit(solution)/shard_map/all_gather | solution.py:143
  10.0 159.2 %all-gather.9.cloned.1.call-start = ((), (), s32[]{:S(2)}) async-start(), calls=%async_computation.8 | async-start | bytes 9437184 | tf_op jit(solution)/shard_map/all_gather | solution.py:61
  12.0 474.4 %copy-start.40 = (f32[8,2048]{1,0:T(8,128)}, f32[8,2048]{1,0:T(8,128)S(1)}, u32[]{:S(2)}) copy-start(f32[8,2048]{1,0:T(8,128)S(1)} %get-tuple-element.34) | copy-start | bytes 196612
  12.0 977.6 %copy-start.26 = (f32[8,2048]{1,0:T(8,128)}, f32[8,2048]{1,0:T(8,128)S(1)}, u32[]{:S(2)}) copy-start(f32[8,2048]{1,0:T(8,128)S(1)} %get-tuple-element.36) | copy-start | bytes 196612
  13.6 172.7 %all-gather.13.cloned.1.call-start = ((), (), s32[]{:S(2)}) async-start(), calls=%async_computation.10 | async-start | bytes 1310720 | tf_op jit(solution)/shard_map/all_gather | solution.py:144
  14.4 463.7 %reduce-scatter.9.cloned.1.call-start = ((), (), s32[]{:S(2)}) async-start(), calls=%async_computation.11 | async-start | bytes 18874368 | tf_op jit(solution)/shard_map/reduce_scatter | solution.py:82
  195.9 317.7 %all-gather.17.cloned.1.call-start = ((), (), s32[]{:S(2)}) async-start(), calls=%async_computation.13 | async-start | bytes 5242880 | tf_op jit(solution)/shard_map/all_gather | solution.py:145
  198.7 442.7 %all-gather.15.cloned.1.call-start = ((), (), s32[]{:S(2)}) async-start(), calls=%async_computation.12 | async-start | bytes 9437184 | tf_op jit(solution)/shard_map/all_gather | solution.py:89
  480.1 509.6 %copy-start.43 = (f32[8,32]{1,0:T(8,128)}, f32[8,32]{1,0:T(8,128)S(1)}, u32[]{:S(2)}) copy-start(f32[8,32]{1,0:T(8,128)S(1)} %broadcast_multiply_fusion) | copy-start | bytes 3076
  480.4 509.3 %copy-start.47 = (f32[8,32]{1,0:T(8,128)}, f32[8,32]{1,0:T(8,128)S(1)}, u32[]{:S(2)}) copy-start(f32[8,32]{1,0:T(8,128)S(1)} %fusion.65) | copy-start | bytes 3076
  482.9 193.5 %all-gather.19.cloned.1.call-start = ((), (), s32[]{:S(2)}) async-start(), calls=%async_computation.14 | async-start | bytes 5242880 | tf_op jit(solution)/shard_map/all_gather | solution.py:146
  485.7 318.7 %all-gather.21.cloned.1.call-start = ((), (), s32[]{:S(2)}) async-start(), calls=%async_computation.16 | async-start | bytes 9437184 | tf_op jit(solution)/shard_map/all_gather | solution.py:182
  486.4 503.3 %copy-start.57 = (f32[8]{0:T(128)}, f32[8]{0:T(128)S(1)}, u32[]{:S(2)}) copy-start(f32[8]{0:T(128)S(1)} %fusion.67) | copy-start | bytes 100
  489.5 495.2 %reduce-scatter.13.cloned.1.call-start = ((), (), s32[]{:S(2)}) async-start(), calls=%async_computation.17 | async-start | bytes 9437184 | tf_op jit(solution)/shard_map/reduce_scatter | solution.py:200
  837.4 278.4 %all-gather.23.cloned.1.call-start = ((), (), s32[]{:S(2)}) async-start(), calls=%async_computation.18 | async-start | bytes 9437184 | tf_op jit(solution)/shard_map/all_gather | solution.py:210
  991.7 193.5 %reduce-scatter.21.cloned.1.call-start = ((), (), s32[]{:S(2)}) async-start(), calls=%async_computation.22 | async-start | bytes 5242880 | tf_op jit(solution)/shard_map/reduce_scatter | solution.py:275
  1005.8 202.3 %reduce-scatter.23.cloned.1.call-start = ((), (), s32[]{:S(2)}) async-start(), calls=%async_computation.23 | async-start | bytes 5242880 | tf_op jit(solution)/shard_map/reduce_scatter | solution.py:278
  1022.2 214.0 %reduce-scatter.19.cloned.1.call-start = ((), (), s32[]{:S(2)}) async-start(), calls=%async_computation.21 | async-start | bytes 1310720 | tf_op jit(solution)/shard_map/reduce_scatter | solution.py:272
  1145.4 131.3 %reduce-scatter.17.cloned.1.call-start = ((), (), s32[]{:S(2)}) async-start(), calls=%async_computation.20 | async-start | bytes 3932160 | tf_op jit(solution)/shard_map/reduce_scatter | solution.py:269
  1156.5 273.7 %reduce-scatter.15.cloned.1.call-start = ((), (), s32[]{:S(2)}) async-start(), calls=%async_computation.19 | async-start | bytes 9437184 | tf_op jit(solution)/shard_map/reduce_scatter | solution.py:259
  1168.7 413.5 %reduce-scatter.11.cloned.1.call-start = ((), (), s32[]{:S(2)}) async-start(), calls=%async_computation.15 | async-start | bytes 9437184 | tf_op jit(solution)/shard_map/reduce_scatter | solution.py:97
  1342.1 240.1 %copy-start.27 = (f32[8,2048]{1,0:T(8,128)S(1)}, f32[8,2048]{1,0:T(8,128)}, u32[]{:S(2)}) copy-start(f32[8,2048]{1,0:T(8,128)} %copy-done.26) | copy-start | bytes 196612
  1342.1 240.1 %copy-start.41 = (f32[8,2048]{1,0:T(8,128)S(1)}, f32[8,2048]{1,0:T(8,128)}, u32[]{:S(2)}) copy-start(f32[8,2048]{1,0:T(8,128)} %copy-done.40) | copy-start | bytes 196612
  1342.1 240.1 %copy-start.44 = (f32[8,32]{1,0:T(8,128)S(1)}, f32[8,32]{1,0:T(8,128)}, u32[]{:S(2)}) copy-start(f32[8,32]{1,0:T(8,128)} %copy-done.43) | copy-start | bytes 3076
  (55 other events, 2072.0 us)
Sparse Core Ops, SparseCore 0:
  10.2 31.2 all-gather.10
  44.2 124.9 all-gather.8
  171.3 14.8 all-gather.12
  196.1 281.9 reduce-scatter.8
  480.2 33.4 all-gather.16
  516.5 124.9 all-gather.14
  643.7 32.6 all-gather.18
  679.4 124.9 all-gather.20
  837.5 147.1 reduce-scatter.12
  991.8 123.9 all-gather.22
  1118.3 42.7 reduce-scatter.20
  1163.6 44.4 reduce-scatter.22
  1211.2 24.8 reduce-scatter.18
  1238.7 37.9 reduce-scatter.16
  1280.2 149.9 reduce-scatter.14
  1434.1 148.0 reduce-scatter.10
where the time goes:
time: 1600 us
  waiting for transfers between devices  1300 us (81%)
  matrix products  159 us (10%)
  other arithmetic  55.5 us (3%)
  blocking collectives  42.8 us (3%)
  between operations  20.1 us (1%)
  local copies, waits for them, and re-layouts  18 us (1%)
    reduce_scatter x1, waiting for transfers between devices, forward(): lax.psum_scatter(attention_portion, 'mp', scatter_dimension=1, tiled=True)  279 us
    reduce_scatter x1, waiting for transfers between devices, forward(): lax.psum_scatter(perceptron_portion.astype(jnp.bfloat16), 'mp', scatter_d...  149 us
    reduce_scatter x1, waiting for transfers between devices, per_device(): lax.psum_scatter(perceptron_input_gradient.astype(jnp.bfloat16), 'mp', sc...  147 us
    all_gather x1, waiting for transfers between devices, per_device(): lax.all_gather(mlp_grad, 'mp', axis=1, tiled=True)  128 us
    all_gather x1, waiting for transfers between devices, forward(): perceptron_rows = lax.all_gather(perceptron_input, 'mp', axis=1, tiled=True)  128 us
    all_gather x1, waiting for transfers between devices, forward(): collected_rows = lax.all_gather(attention_input, 'mp', axis=1, tiled=True)  128 us
    all_gather x1, waiting for transfers between devices, per_device(): lax.all_gather(attn_grad, 'mp', axis=1, tiled=True)  93.5 us
    reduce_scatter x1, waiting for transfers between devices, per_device(): lax.psum_scatter(attn_in_grad.astype(jnp.bfloat16), 'mp', scatter_dimensi...  88 us
  transfers between devices with their start and end apart: 16, of which 15 were waited for; matrix products, arithmetic and copies ran while one was open for 11% of the time, Pallas kernels for 0%

commit v1 on v0

v1 whole, which is shorter than its diff:
```python
import jax
import jax.numpy as jnp
from jax import lax
from jax.sharding import PartitionSpec as P

HD = 128
BINS = 8
ADAM_STEP = 10

clip_limit = 1.0
beta_one = 0.9
beta_two = 0.95
learn_rate = 0.02
output_rate = 0.08
adam_epsilon = 1e-08
decay_rate = 0.01

BF = jnp.bfloat16
F32 = jnp.float32


def norm_rows(values):
    center = values - jnp.mean(values, axis=-1, keepdims=True)
    spread = jnp.mean(center * center, axis=-1, keepdims=True)
    return center * lax.rsqrt(spread + 1e-06)


def gelu_tanh(values):
    return jax.nn.gelu(values, approximate=True)


def adam_update(gradient, moment_one, moment_two, weight, factor, step_rate):
    clipped = gradient * factor
    new_one = beta_one * moment_one + (1.0 - beta_one) * clipped
    new_two = beta_two * moment_two + (1.0 - beta_two) * clipped * clipped
    corrected = new_one / (1.0 - beta_one**ADAM_STEP)
    root_two = jnp.sqrt(new_two / (1.0 - beta_two**ADAM_STEP))
    new_weight = weight - step_rate * (corrected / (root_two + adam_epsilon) + decay_rate * weight)
    return (new_one, new_two, new_weight)


def after(value, *earlier):
    return lax.optimization_barrier((value, *earlier))[0]


def matmul(a, b, contract):
    return lax.dot_general(a, b, (contract, ((), ())), preferred_element_type=F32)


class Links:
    def __init__(self, n_dp, n_mp):
        self.X, self.H = n_dp // 2, n_mp // 4
        self.n_dp, self.n_mp = n_dp, n_mp

    def from_dp(self, v, jx, jc):
        pairs = []
        for dst in range(self.n_dp):
            x, c = divmod(dst, 2)
            pairs.append((((x + jx) % self.X) * 2 + (c ^ jc), dst))
        return lax.ppermute(v, "dp", pairs)

    def from_mp(self, v, jh, jp, jq):
        pairs = []
        for dst in range(self.n_mp):
            h, p, q = dst // 4, (dst // 2) % 2, dst % 2
            pairs.append((((h + jh) % self.H) * 4 + (p ^ jp) * 2 + (q ^ jq), dst))
        return lax.ppermute(v, "mp", pairs)

    def gather_blocks(self, w, h_dim, d_dim):
        pieces = {(0, 0, 0): w}
        for jh in range(1, self.H):
            pieces[jh, 0, 0] = self.from_mp(w, jh, 0, 0)
        for jh in range(self.H):
            for jx in range(1, self.X):
                pieces[jh, jx, 0] = self.from_dp(pieces[jh, 0, 0], jx, 0)
        for jh in range(self.H):
            for jx in range(self.X):
                pieces[jh, jx, 1] = self.from_dp(pieces[jh, jx, 0], 0, 1)
        return jnp.concatenate(
            [
                jnp.concatenate(
                    [pieces[jh, jx, jc] for jc in range(2) for jx in range(self.X)], axis=d_dim
                )
                for jh in range(self.H)
            ],
            axis=h_dim,
        )

    def reduce_blocks(self, g, h_dim, d_dim):
        half = g.shape[d_dim] // 2
        keep = lax.slice_in_dim(g, 0, half, axis=d_dim)
        sent = self.from_dp(lax.slice_in_dim(g, half, 2 * half, axis=d_dim), 0, 1)
        g = (keep.astype(F32) + sent.astype(F32)).astype(BF)
        width = half // self.X
        total = lax.slice_in_dim(g, 0, width, axis=d_dim).astype(F32)
        for jx in range(1, self.X):
            block = lax.slice_in_dim(g, jx * width, (jx + 1) * width, axis=d_dim)
            total = total + self.from_dp(block, -jx, 0).astype(F32)
        g = total.astype(BF)
        width = g.shape[h_dim] // self.H
        total = lax.slice_in_dim(g, 0, width, axis=h_dim).astype(F32)
        for jh in range(1, self.H):
            block = lax.slice_in_dim(g, jh * width, (jh + 1) * width, axis=h_dim)
            total = total + self.from_mp(block, -jh, 0, 0).astype(F32)
        return total

    def to_group(self, v):
        here = lax.axis_index("mp") // 4
        images = v.shape[0] // self.H
        parts = []
        for jh in range(self.H):
            chosen = lax.dynamic_slice_in_dim(v, ((here - jh) % self.H) * images, images, axis=0)
            parts.append(chosen if jh == 0 else self.from_mp(chosen, jh, 0, 0))
        return jnp.concatenate(parts, axis=1)

    def to_home(self, v):
        here = lax.axis_index("mp") // 4
        images = v.shape[0]
        tokens = v.shape[1] // self.H
        out = jnp.zeros((images * self.H, tokens, v.shape[2]), v.dtype)
        for jh in range(self.H):
            part = v[:, jh * tokens : (jh + 1) * tokens]
            part = part if jh == 0 else self.from_mp(part, -jh, 0, 0)
            out = lax.dynamic_update_slice_in_dim(
                out, part, ((here - jh) % self.H) * images, axis=0
            )
        return out

    def gather_tokens(self, v):
        half = v.shape[0] // 2
        a, b = v[:half], v[half:]
        pa, qb = self.from_mp(a, 0, 1, 0), self.from_mp(b, 0, 0, 1)
        qa, pb = self.from_mp(a, 0, 0, 1), self.from_mp(b, 0, 1, 0)
        da, db = self.from_mp(pa, 0, 0, 1), self.from_mp(qb, 0, 1, 0)
        return jnp.concatenate(
            [
                jnp.concatenate([a, qa, pa, da], axis=1),
                jnp.concatenate([b, qb, pb, db], axis=1),
            ],
            axis=0,
        )

    def reduce_tokens(self, v):
        images, length, width = v.shape
        half, t = images // 2, length // 4
        v = v.reshape(images, 2, 2, t, width)
        a, b = v[:half], v[half:]
        ra = self.from_mp(a[:, :, 1], 0, 0, 1)
        rb = self.from_mp(b[:, 1], 0, 1, 0)
        sa = (a[:, :, 0].astype(F32) + ra.astype(F32)).astype(BF)
        sb = (b[:, 0].astype(F32) + rb.astype(F32)).astype(BF)
        ta = self.from_mp(sa[:, 1], 0, 1, 0)
        tb = self.from_mp(sb[:, 1], 0, 0, 1)
        return jnp.concatenate(
            [
                sa[:, 0].astype(F32) + ta.astype(F32),
                sb[:, 0].astype(F32) + tb.astype(F32),
            ],
            axis=0,
        )

    def features_here(self, v):
        d = lax.axis_index("dp")
        x, c = d // 2, d % 2
        width = v.shape[-1] // self.n_dp
        return jnp.concatenate(
            [
                lax.dynamic_slice_in_dim(
                    v, (((x + jx) % self.X) * 2 + (c ^ jc)) * width, width, axis=v.ndim - 1
                )
                for jc in range(2)
                for jx in range(self.X)
            ],
            axis=-1,
        )

    def features_home(self, v):
        d = lax.axis_index("dp")
        x, c = d // 2, d % 2
        width = v.shape[-1] // self.n_dp
        return jnp.concatenate(
            [
                lax.dynamic_slice_in_dim(
                    v,
                    (((e % 2) ^ c) * self.X + (e // 2 - x) % self.X) * width,
                    width,
                    axis=v.ndim - 1,
                )
                for e in range(self.n_dp)
            ],
            axis=-1,
        )

    def total(self, v):
        step = 1
        while step < self.n_dp:
            v = v + lax.ppermute(v, "dp", [(i ^ step, i) for i in range(self.n_dp)])
            step *= 2
        step = 1
        while step < self.n_mp:
            v = v + lax.ppermute(v, "mp", [(i ^ step, i) for i in range(self.n_mp)])
            step *= 2
        return v


def per_device(
    links,
    stream_in,
    cotangent,
    noise_table,
    timesteps,
    bins,
    counts,
    w_qkv,
    w_out,
    w_up,
    w_down,
    m_qkv,
    m_out,
    m_up,
    m_down,
    v_qkv,
    v_out,
    v_up,
    v_down,
):
    H = links.H
    slots, _, D = stream_in.shape
    images = slots // H
    here = lax.axis_index("mp") // 4

    steps_here = lax.dynamic_slice_in_dim(timesteps, here * images, images)
    table_rows = noise_table.shape[0]
    picks = (steps_here[:, None] == jnp.arange(table_rows)[None, :]).astype(F32)
    modulation = jnp.dot(
        picks, noise_table.reshape(table_rows, -1), precision=lax.Precision.HIGHEST
    ).reshape(images, 6, D)
    modulation = links.features_here(modulation)
    shift_a, scale_a, gate_a, shift_f, scale_f, gate_f = (modulation[:, i : i + 1] for i in range(6))

    stream = links.to_group(links.features_here(stream_in)).astype(F32)

    block = w_qkv.shape[2]
    wq = links.gather_blocks(w_qkv.astype(BF).reshape(w_qkv.shape[0], 3 * block), 1, 0)
    wo = links.gather_blocks(w_out.astype(BF), 0, 1)
    wu = links.gather_blocks(w_up.astype(BF), 1, 0)
    wd = links.gather_blocks(w_down.astype(BF), 0, 1)

    live = jnp.arange(slots) < counts[0]
    loss_scale = live.astype(F32) * (bins.astype(F32) + 1.0) / BINS
    loss_scale = lax.dynamic_slice_in_dim(loss_scale, here * images, images)
    cot = links.to_group(links.features_here(cotangent.astype(BF))).astype(F32)
    dy = cot * loss_scale[:, None, None]

    def first_norm(rows):
        return norm_rows(rows) * scale_a + shift_a

    def second_norm(rows):
        return norm_rows(rows) * scale_f + shift_f

    a_rows = links.gather_tokens(first_norm(stream).astype(BF))
    length = a_rows.shape[1]
    rows = images * length
    a_rows = a_rows.reshape(rows, D)
    heads = H * block // HD
    qkv = matmul(a_rows, wq, ((1,), (0,))).astype(BF)
    qkv = qkv.reshape(images, length, H, 3, block)
    q = qkv[:, :, :, 0].reshape(images, length, heads, HD)
    k = qkv[:, :, :, 1].reshape(images, length, heads, HD)
    v = qkv[:, :, :, 2].reshape(images, length, heads, HD)
    scores = jnp.einsum("sqhe,skhe->shqk", q, k, preferred_element_type=F32) * HD ** (-0.5)
    top = jnp.max(scores, axis=-1, keepdims=True)
    lse = top + jnp.log(jnp.sum(jnp.exp(scores - top), axis=-1, keepdims=True))
    probs = jnp.exp(scores - lse)
    o = jnp.einsum("shqk,skhe->sqhe", probs.astype(BF), v, preferred_element_type=F32).astype(BF)
    o = o.reshape(rows, heads * HD)
    att = links.reduce_tokens(
        matmul(o, wo, ((1,), (0,))).astype(BF).reshape(images, length, D)
    )
    residual = stream + gate_a * att
    b_rows = links.gather_tokens(second_norm(residual).astype(BF)).reshape(rows, D)
    u = matmul(b_rows, wu, ((1,), (0,)))
    hidden = gelu_tanh(u).astype(BF)
    ff = links.reduce_tokens(
        matmul(hidden, wd, ((1,), (0,))).astype(BF).reshape(images, length, D)
    )
    output = links.features_home(links.to_home((residual + gate_f * ff).astype(BF)))

    df_rows = links.gather_tokens((gate_f * dy).astype(BF)).reshape(rows, D)
    g_down = matmul(hidden, df_rows, ((0,), (0,))).astype(BF)
    d_hidden = matmul(df_rows, wd, ((1,), (1,)))
    du = jax.vjp(gelu_tanh, u)[1](d_hidden)[0].astype(BF)
    g_up = matmul(b_rows, du, ((0,), (0,))).astype(BF)
    db = links.reduce_tokens(
        matmul(du, wu, ((1,), (1,))).astype(BF).reshape(images, length, D)
    )
    dr = dy + jax.vjp(second_norm, residual)[1](db)[0]
    datt = links.gather_tokens((gate_a * dr).astype(BF)).reshape(rows, D)
    g_out = matmul(o, datt, ((0,), (0,))).astype(BF)
    do = matmul(datt, wo, ((1,), (1,))).astype(BF).reshape(images, length, heads, HD)
    dv = jnp.einsum("shqk,sqhe->skhe", probs.astype(BF), do, preferred_element_type=F32)
    dp = jnp.einsum("sqhe,skhe->shqk", do, v, preferred_element_type=F32)
    ds = (probs * (dp - jnp.sum(probs * dp, axis=-1, keepdims=True))).astype(BF)
    dq = jnp.einsum("shqk,skhe->sqhe", ds, k, preferred_element_type=F32) * HD ** (-0.5)
    dk = jnp.einsum("shqk,sqhe->skhe", ds, q, preferred_element_type=F32) * HD ** (-0.5)
    dqkv = jnp.stack(
        [t.astype(BF).reshape(images, length, H, block) for t in (dq, dk, dv)], axis=3
    ).reshape(rows, H * 3 * block)
    g_qkv = matmul(a_rows, dqkv, ((0,), (0,))).astype(BF)
    da = links.reduce_tokens(
        matmul(dqkv, wq, ((1,), (1,))).astype(BF).reshape(images, length, D)
    )
    d_stream = dr + jax.vjp(first_norm, stream)[1](da)[0]
    input_grad = links.features_home(links.to_home(d_stream.astype(BF))).astype(F32)

    g_down = links.reduce_blocks(g_down, 0, 1)
    g_up = links.reduce_blocks(g_up, 1, 0)
    g_out = links.reduce_blocks(g_out, 0, 1)
    g_qkv = links.reduce_blocks(g_qkv, 1, 0).reshape(w_qkv.shape)
    squares = (
        jnp.sum(g_qkv * g_qkv)
        + jnp.sum(g_out * g_out)
        + jnp.sum(g_up * g_up)
        + jnp.sum(g_down * g_down)
    )
    grad_norm = jnp.sqrt(links.total(squares))
    factor = jnp.minimum(1.0, clip_limit / (grad_norm + 1e-06))
    one_qkv, two_qkv, new_qkv = adam_update(g_qkv, m_qkv, v_qkv, w_qkv, factor, learn_rate)
    one_out, two_out, new_out = adam_update(g_out, m_out, v_out, w_out, factor, output_rate)
    one_up, two_up, new_up = adam_update(g_up, m_up, v_up, w_up, factor, learn_rate)
    one_down, two_down, new_down = adam_update(g_down, m_down, v_down, w_down, factor, learn_rate)
    return (
        output,
        input_grad,
        grad_norm,
        one_qkv,
        one_out,
        one_up,
        one_down,
        two_qkv,
        two_out,
        two_up,
        two_down,
        new_qkv,
        new_out,
        new_up,
        new_down,
    )


def solution(mesh):
    links = Links(mesh.shape["dp"], mesh.shape["mp"])
    tokens, qkv = P("dp", "mp", None), P("dp", None, "mp")
    rows, columns = P("mp", "dp"), P("dp", "mp")
    weights = (qkv, rows, columns, rows)
    return jax.shard_map(
        lambda *args: per_device(links, *args),
        mesh=mesh,
        in_specs=(tokens, tokens, P(), P("dp"), P("dp"), P("dp")) + 3 * weights,
        out_specs=(tokens, tokens, P()) + 3 * weights,
        check_vma=False,
    )
```

time: 1600 us -> 904 us (0.56)
  waiting for transfers between devices: 1300 us -> 459 us
  starting transfers between devices: 0.88 us -> 81.2 us
  local copies, waits for them, and re-layouts: 18 us -> 67.6 us
  matrix products: 159 us -> 202 us
  blocking collectives: 42.8 us -> 0 us
  other arithmetic: 55.5 us -> 78.4 us
    reduce_scatter x8 -> x0, waiting for transfers between devices: 749 us -> none  [the longest x1 279 us: forward(): lax.psum_scatter(attention_portion, 'mp', scatter_dimension=1, tiled=True)]
    all_gather x8 -> x0, waiting for transfers between devices: 550 us -> none  [the longest x1 128 us: per_device(): lax.all_gather(mlp_grad, 'mp', axis=1, tiled=True)]
    ppermute x0 -> x89, waiting for transfers between devices: none -> 459 us  [the longest x52 350 us: from_mp(): return lax.ppermute(v, 'mp', pairs)]
    ppermute x0 -> x89, starting transfers between devices: none -> 81.2 us  [the longest x52 58 us: from_mp(): return lax.ppermute(v, 'mp', pairs)]
    dot_general x18, matrix products: 158 us -> 201 us  [the longest x12 193 us: matmul(): lax.dot_general(a, b, (contract, ((), ())), preferred_element_type=F32)]
    psum x1 -> x0, blocking collectives: 42.8 us -> none  [per_device(): grad_norm = jnp.sqrt(lax.psum(local_squares, ('dp', 'mp')))]
    slice x1 -> x34, local copies, waits for them, and re-layouts: 0.22 us -> 22.6 us  [the longest x4 7.57 us: reduce_blocks(): sent = self.from_dp(lax.slice_in_dim(g, half, 2 * half, axis=d_dim), 0, 1)]
    convert_element_type x8 -> x27, other arithmetic: 15.3 us -> 34.3 us  [the longest x4 13.7 us: reduce_blocks(): g = (keep.astype(F32) + sent.astype(F32)).astype(BF)]
  transfers between devices with their start and end apart: 16 -> 89, of which waited for: 15 -> 44; matrix products, arithmetic and copies ran while one was open for 11% -> 29% of each run, Pallas kernels for 0% -> 0%
where the time goes in v1:
time: 904 us; the launch traced here: 899 us
  waiting for transfers between devices  459 us (51%)
  matrix products  202 us (22%)
  starting transfers between devices  81.2 us (9%)
  other arithmetic  78.4 us (9%)
  local copies, waits for them, and re-layouts  67.6 us (7%)
  between operations  10.5 us (1%)
    ppermute x52, waiting for transfers between devices, from_mp(): return lax.ppermute(v, 'mp', pairs)  350 us
    dot_general x12, matrix products, matmul(): lax.dot_general(a, b, (contract, ((), ())), preferred_element_type=F32)  193 us
    ppermute x32, waiting for transfers between devices, from_dp(): return lax.ppermute(v, 'dp', pairs)  101 us
    ppermute x52, starting transfers between devices, from_mp(): return lax.ppermute(v, 'mp', pairs)  58 us
    unnamed x216, local copies, waits for them, and re-layouts  20.2 us
  transfers between devices with their start and end apart: 89, of which 44 were waited for; matrix products, arithmetic and copies ran while one was open for 29% of the time, Pallas kernels for 0%

profile of v1, /device:TPU:0, one launch (start us, length us, event | category | flops | bytes accessed | tf_op | source)
XLA Modules:
  0.0 898.8 jit_solution(12681335388546963966)
XLA Ops:
  18.4 52.5 %collective-permute-done = bf16[4,32,2048]{2,1,0:T(8,128)(2,1)S(1)} collective-permute-done((bf16[4,32,2048]{2,1,0:T(8,128)(2,1)}, bf16[4,32,2048]{2,1,0:T(8,128)(2,1)S(1)}, u32[]{:S(2)}, u32[]{:S(2)}) %collective-permute-start) | collective-permute-done | bytes 524320 | tf_op jit(solution)/shard_map/ppermute | solution.py:67
  89.7 10.7 %collective-permute-done.5 = bf16[2,64,2048]{2,1,0:T(8,128)(2,1)S(1)} collective-permute-done((bf16[2,64,2048]{2,1,0:T(8,128)(2,1)S(1)}, bf16[2,64,2048]{2,1,0:T(8,128)(2,1)S(1)}, u32[]{:S(2)}, u32[]{:S(2)}) %collective-permute-start.5) | collective-permute-done | bytes 524320 | tf_op jit(solution)/shard_map/ppermute | solution.py:67
  124.3 34.8 %convolution_convert_fusion.4 = bf16[1024,1536]{1,0:T(8,128)(2,1)} fusion(bf16[1024,2048]{1,0:T(8,128)(2,1)} %bitcast.241, bf16[512,768]{0,1:T(8,128)(2,1)} %copy-done.93, bf16[512,768]{0,1:T(8,128)(2,1)S(1)} %collective-permute-done.12, bf16[512,768]{0,1:T(8,128)(2,1)S(1)} %collective-permute-done.11, bf16[512,768]{0,1:T(8,128)(2,1)} %collective-permute-done.10, ...), kind=kOutput, calls=%fused_computation.30 | convolution fusion | flops 6494355456 | bytes 13631488 | tf_op jit(solution)/shard_map/dot_general | solution.py:47
  190.9 18.2 %collective-permute-done.50 = bf16[4,32,2048]{2,1,0:T(8,128)(2,1)S(1)} collective-permute-done((bf16[4,32,2048]{2,1,0:T(8,128)(2,1)S(1)}, bf16[4,32,2048]{2,1,0:T(8,128)(2,1)S(1)}, u32[]{:S(2)}, u32[]{:S(2)}) %collective-permute-start.50) | collective-permute-done | bytes 524320 | tf_op jit(solution)/shard_map/ppermute | solution.py:67
  210.6 13.0 %collective-permute-done.23 = bf16[2,2,64,2048]{3,2,0,1:T(8,128)(2,1)S(1)} collective-permute-done((bf16[2,2,64,2048]{3,2,0,1:T(8,128)(2,1)S(1)}, bf16[2,2,64,2048]{3,2,0,1:T(8,128)(2,1)S(1)}, u32[]{:S(2)}, u32[]{:S(2)}) %collective-permute-start.23) | collective-permute-done | bytes 1048608 | tf_op jit(solution)/shard_map/ppermute | solution.py:67
  225.2 10.0 %collective-permute-done.21 = bf16[2,2,64,2048]{3,2,0,1:T(8,128)(2,1)S(1)} collective-permute-done((bf16[2,2,64,2048]{3,2,0,1:T(8,128)(2,1)S(1)}, bf16[2,2,64,2048]{3,2,0,1:T(8,128)(2,1)S(1)}, u32[]{:S(2)}, u32[]{:S(2)}) %collective-permute-start.21) | collective-permute-done | bytes 1048608 | tf_op jit(solution)/shard_map/ppermute | solution.py:67
  262.2 17.7 %collective-permute-done.55 = bf16[2,64,2048]{2,1,0:T(8,128)(2,1)S(1)} collective-permute-done((bf16[2,64,2048]{2,1,0:T(8,128)(2,1)S(1)}, bf16[2,64,2048]{2,1,0:T(8,128)(2,1)S(1)}, u32[]{:S(2)}, u32[]{:S(2)}) %collective-permute-start.55) | collective-permute-done | bytes 524320 | tf_op jit(solution)/shard_map/ppermute | solution.py:67
  282.4 13.8 %collective-permute-done.52 = bf16[2,64,2048]{2,1,0:T(8,128)(2,1)S(1)} collective-permute-done((bf16[2,64,2048]{2,1,0:T(8,128)(2,1)S(1)}, bf16[2,64,2048]{2,1,0:T(8,128)(2,1)S(1)}, u32[]{:S(2)}, u32[]{:S(2)}) %collective-permute-start.52) | collective-permute-done | bytes 524320 | tf_op jit(solution)/shard_map/ppermute | solution.py:67
  348.5 15.3 %collective-permute-done.42 = bf16[1024,512]{1,0:T(8,128)(2,1)} collective-permute-done((bf16[1024,512]{1,0:T(8,128)(2,1)}, bf16[1024,512]{1,0:T(8,128)(2,1)}, u32[]{:S(2)}, u32[]{:S(2)}) %collective-permute-start.42) | collective-permute-done | bytes 1048608 | tf_op jit(solution)/shard_map/ppermute | solution.py:60
  363.8 17.3 %fusion.55 = f32[1024,2048]{1,0:T(8,128)} fusion(bf16[1024,2048]{1,0:T(8,128)(2,1)} %bitcast.243, bf16[512,1024]{1,0:T(8,128)(2,1)} %collective-permute-done.37, bf16[512,1024]{1,0:T(8,128)(2,1)} %collective-permute-done.36, bf16[512,1024]{1,0:T(8,128)(2,1)} %collective-permute-done.35, bf16[512,1024]{1,0:T(8,128)(2,1)} %collective-permute-done.34, ...), kind=kOutput, calls=%fused_computation.228 | convolution fusion | flops 8657043456 | bytes 20971520 | tf_op jit(solution)/shard_map/dot_general | solution.py:47
  381.1 15.7 %convolution_convert_fusion.1 = bf16[2048,2048]{1,0:T(8,128)(2,1)} fusion(bf16[1024,2048]{1,0:T(8,128)(2,1)} %bitcast.247, f32[1024,2048]{1,0:T(8,128)} %fusion.55), kind=kOutput, calls=%fused_computation.15 | convolution fusion | flops 8613003264 | bytes 20971520 | tf_op jit(solution)/shard_map/dot_general | solution.py:47
  396.8 26.7 %fusion.6 = bf16[1024,2048]{1,0:T(8,128)(2,1)} fusion(f32[1024,2048]{1,0:T(8,128)S(1)} %copy-done.96, bf16[1024,2048]{1,0:T(8,128)(2,1)S(1)} %bitcast.248, bf16[1024,512]{1,0:T(8,128)(2,1)} %collective-permute-done.44, bf16[1024,512]{1,0:T(8,128)(2,1)} %collective-permute-done.43, bf16[1024,512]{1,0:T(8,128)(2,1)} %collective-permute-done.42, ...), kind=kOutput, calls=%fused_computation.8 | convolution fusion | flops 8698986496 | bytes 25165824 | tf_op jit(solution)/shard_map/dot_general | solution.py:47
  423.5 22.3 %convolution_convert_fusion.5 = bf16[1024,2048]{1,0:T(8,128)(2,1)} fusion(bf16[1024,2048]{1,0:T(8,128)(2,1)} %fusion.6, bf16[512,1024]{1,0:T(8,128)(2,1)} %collective-permute-done.37, bf16[512,1024]{1,0:T(8,128)(2,1)} %collective-permute-done.36, bf16[512,1024]{1,0:T(8,128)(2,1)} %collective-permute-done.35, bf16[512,1024]{1,0:T(8,128)(2,1)} %collective-permute-done.34, ...), kind=kOutput, calls=%fused_computation.31 | convolution fusion | flops 8659140608 | bytes 16777216 | tf_op jit(solution)/shard_map/dot_general | solution.py:47
  452.0 27.6 %convolution_convert_fusion.6 = bf16[1024,2048]{1,0:T(8,128)(2,1)} fusion(f32[1024,2048]{1,0:T(8,128)} %fusion.55, bf16[1024,512]{1,0:T(8,128)(2,1)} %collective-permute-done.44, bf16[1024,512]{1,0:T(8,128)(2,1)} %collective-permute-done.43, bf16[1024,512]{1,0:T(8,128)(2,1)} %collective-permute-done.42, bf16[1024,512]{1,0:T(8,128)(2,1)} %collective-permute-done.41, ...), kind=kOutput, calls=%fused_computation.32 | convolution fusion | flops 8678014976 | bytes 20971520 | tf_op jit(solution)/shard_map/dot_general | solution.py:47
  490.6 18.1 %collective-permute-done.47 = bf16[2,2,64,2048]{3,2,0,1:T(8,128)(2,1)S(1)} collective-permute-done((bf16[2,2,64,2048]{3,2,0,1:T(8,128)(2,1)S(1)}, bf16[2,2,64,2048]{3,2,0,1:T(8,128)(2,1)S(1)}, u32[]{:S(2)}, u32[]{:S(2)}) %collective-permute-start.47) | collective-permute-done | bytes 1048608 | tf_op jit(solution)/shard_map/ppermute | solution.py:67
  512.9 9.5 %collective-permute-done.60 = bf16[2,64,2048]{2,1,0:T(8,128)(2,1)S(1)} collective-permute-done((bf16[2,64,2048]{2,1,0:T(8,128)(2,1)S(1)}, bf16[2,64,2048]{2,1,0:T(8,128)(2,1)S(1)}, u32[]{:S(2)}, u32[]{:S(2)}) %collective-permute-start.60) | collective-permute-done | bytes 524320 | tf_op jit(solution)/shard_map/ppermute | solution.py:67
  538.0 11.0 %convolution_convert_fusion.2 = bf16[2048,2048]{1,0:T(8,128)(2,1)S(1)} fusion(bf16[1024,2048]{1,0:T(8,128)(2,1)S(1)} %bitcast.244, bf16[1024,2048]{1,0:T(8,128)(2,1)} %fusion.6), kind=kOutput, calls=%fused_computation.16 | convolution fusion | flops 8594128896 | bytes 16777216 | tf_op jit(solution)/shard_map/dot_general | solution.py:47
  616.3 19.7 %convolution_convert_fusion.3 = bf16[1024,2048]{1,0:T(8,128)(2,1)S(1)} fusion(bf16[1024,1536]{0,1:T(8,128)(2,1)} %bitcast.253, bf16[512,768]{0,1:T(8,128)(2,1)} %copy-done.93, bf16[512,768]{0,1:T(8,128)(2,1)} %copy-done.91, bf16[512,768]{0,1:T(8,128)(2,1)S(1)} %copy-done.89, bf16[512,768]{0,1:T(8,128)(2,1)} %collective-permute-done.10, ...), kind=kOutput, calls=%fused_computation.29 | convolution fusion | flops 6494879744 | bytes 13631488 | tf_op jit(solution)/shard_map/dot_general | solution.py:47
  643.9 17.2 %collective-permute-done.69 = bf16[2,2,64,2048]{3,2,0,1:T(8,128)(2,1)S(1)} collective-permute-done((bf16[2,2,64,2048]{3,2,0,1:T(8,128)(2,1)S(1)}, bf16[2,2,64,2048]{3,2,0,1:T(8,128)(2,1)S(1)}, u32[]{:S(2)}, u32[]{:S(2)}) %collective-permute-start.69) | collective-permute-done | bytes 1048608 | tf_op jit(solution)/shard_map/ppermute | solution.py:67
  696.2 26.3 %collective-permute-done.77 = bf16[256,512]{1,0:T(8,128)(2,1)S(1)} collective-permute-done((bf16[256,512]{1,0:T(8,128)(2,1)S(1)}, bf16[256,512]{1,0:T(8,128)(2,1)S(1)}, u32[]{:S(2)}, u32[]{:S(2)}) %collective-permute-start.77) | collective-permute-done | bytes 262176 | tf_op jit(solution)/shard_map/ppermute | solution.py:67
  731.0 40.8 %collective-permute-done.82 = bf16[2048,512]{1,0:T(8,128)(2,1)S(1)} collective-permute-done((bf16[2048,512]{1,0:T(8,128)(2,1)S(1)}, bf16[2048,512]{1,0:T(8,128)(2,1)S(1)}, u32[]{:S(2)}, u32[]{:S(2)}) %collective-permute-start.82) | collective-permute-done | bytes 2097184 | tf_op jit(solution)/shard_map/ppermute | solution.py:60
  774.4 29.4 %collective-permute-done.73 = bf16[512,1536]{0,1:T(8,128)(2,1)S(1)} collective-permute-done((bf16[512,1536]{0,1:T(8,128)(2,1)S(1)}, bf16[512,1536]{0,1:T(8,128)(2,1)S(1)}, u32[]{:S(2)}, u32[]{:S(2)}) %collective-permute-start.73) | collective-permute-done | bytes 1572896 | tf_op jit(solution)/shard_map/ppermute | solution.py:60
  809.7 28.5 %collective-permute-done.83 = bf16[1024,512]{1,0:T(8,128)(2,1)S(1)} collective-permute-done((bf16[1024,512]{1,0:T(8,128)(2,1)S(1)}, bf16[1024,512]{1,0:T(8,128)(2,1)S(1)}, u32[]{:S(2)}, u32[]{:S(2)}) %collective-permute-start.83) | collective-permute-done | bytes 1048608 | tf_op jit(solution)/shard_map/ppermute | solution.py:67
  839.4 14.2 %collective-permute-done.74 = bf16[512,768]{0,1:T(8,128)(2,1)S(1)} collective-permute-done((bf16[512,768]{0,1:T(8,128)(2,1)S(1)}, bf16[512,768]{0,1:T(8,128)(2,1)S(1)}, u32[]{:S(2)}, u32[]{:S(2)}) %collective-permute-start.74) | collective-permute-done | bytes 786464 | tf_op jit(solution)/shard_map/ppermute | solution.py:67
  (528 shorter events, 378.1 us)
Async XLA Ops:
  3.3 74.1 %collective-permute-start.10 = (bf16[512,768]{0,1:T(8,128)(2,1)}, bf16[512,768]{0,1:T(8,128)(2,1)}, u32[]{:S(2)}, u32[]{:S(2)}) collective-permute-start(bf16[512,768]{0,1:T(8,128)(2,1)} %bitcast.6), channel_id=1, source_target_pairs={{4,0},{5,1},{6,2},{7,3},{0,4},{1,5},{2,6},{3,7},{12,8},{13,9},{14,... | collective-permute-start | bytes 2359304 | tf_op jit(solution)/shard_map/ppermute | solution.py:67
  7.4 78.6 %collective-permute-start.7 = (bf16[512,768]{0,1:T(8,128)(2,1)}, bf16[512,768]{0,1:T(8,128)(2,1)}, u32[]{:S(2)}, u32[]{:S(2)}) collective-permute-start(bf16[512,768]{0,1:T(8,128)(2,1)} %bitcast.6), channel_id=1, source_target_pairs={{16,0},{24,8},{0,16},{8,24},{17,1},{25,9},{1,17},{9,25},{18,2},{26... | collective-permute-start | bytes 2359304 | tf_op jit(solution)/shard_map/ppermute | solution.py:60
  13.8 57.1 %collective-permute-start = (bf16[4,32,2048]{2,1,0:T(8,128)(2,1)}, bf16[4,32,2048]{2,1,0:T(8,128)(2,1)S(1)}, u32[]{:S(2)}, u32[]{:S(2)}) collective-permute-start(bf16[4,32,2048]{2,1,0:T(8,128)(2,1)} %get-tuple-element.86), channel_id=1, source_target_pairs={{4,0},{5,1},{6,2},{7,3},{0,4},{1,5},{2,6},{3,7},{12,8},{13,9},{14,... | collective-permute-start | bytes 1572872 | tf_op jit(solution)/shard_map/ppermute | solution.py:67
  14.9 61.0 %collective-permute-start.17 = (bf16[256,512]{1,0:T(8,128)(2,1)}, bf16[256,512]{1,0:T(8,128)(2,1)}, u32[]{:S(2)}, u32[]{:S(2)}) collective-permute-start(bf16[256,512]{1,0:T(8,128)(2,1)} %convert_element_type.385), channel_id=1, source_target_pairs={{4,0},{5,1},{6,2},{7,3},{0,4},{1,5},{2,6},{3,7},{12,8},{13,9},{14,... | collective-permute-start | bytes 786440 | tf_op jit(solution)/shard_map/ppermute | solution.py:67
  120.6 60.4 %collective-permute-start.15 = (bf16[256,512]{1,0:T(8,128)(2,1)}, bf16[256,512]{1,0:T(8,128)(2,1)}, u32[]{:S(2)}, u32[]{:S(2)}) collective-permute-start(bf16[256,512]{1,0:T(8,128)(2,1)} %convert_element_type.385), channel_id=1, source_target_pairs={{8,0},{0,8},{24,16},{16,24},{9,1},{1,9},{25,17},{17,25},{10,2},{2,... | collective-permute-start | bytes 786440 | tf_op jit(solution)/shard_map/ppermute | solution.py:60
  120.6 128.3 %collective-permute-start.34 = (bf16[512,1024]{1,0:T(8,128)(2,1)}, bf16[512,1024]{1,0:T(8,128)(2,1)}, u32[]{:S(2)}, u32[]{:S(2)}) collective-permute-start(bf16[512,1024]{1,0:T(8,128)(2,1)} %convert_element_type.402), channel_id=1, source_target_pairs={{4,0},{5,1},{6,2},{7,3},{0,4},{1,5},{2,6},{3,7},{12,8},{13,9},{14,... | collective-permute-start | bytes 3145736 | tf_op jit(solution)/shard_map/ppermute | solution.py:67
  122.7 59.9 %collective-permute-start.19 = (bf16[256,512]{1,0:T(8,128)(2,1)}, bf16[256,512]{1,0:T(8,128)(2,1)}, u32[]{:S(2)}, u32[]{:S(2)}) collective-permute-start(bf16[256,512]{1,0:T(8,128)(2,1)} %collective-permute-done.17), channel_id=1, source_target_pairs={{8,0},{0,8},{24,16},{16,24},{9,1},{1,9},{25,17},{17,25},{10,2},{2,... | collective-permute-start | bytes 786440 | tf_op jit(solution)/shard_map/ppermute | solution.py:60
  122.8 59.7 %collective-permute-start.16 = (bf16[256,512]{1,0:T(8,128)(2,1)}, bf16[256,512]{1,0:T(8,128)(2,1)}, u32[]{:S(2)}, u32[]{:S(2)}) collective-permute-start(bf16[256,512]{1,0:T(8,128)(2,1)} %collective-permute-done.14), channel_id=1, source_target_pairs={{8,0},{0,8},{24,16},{16,24},{9,1},{1,9},{25,17},{17,25},{10,2},{2,... | collective-permute-start | bytes 786440 | tf_op jit(solution)/shard_map/ppermute | solution.py:60
  124.1 59.5 %collective-permute-start.20 = (bf16[256,512]{1,0:T(8,128)(2,1)}, bf16[256,512]{1,0:T(8,128)(2,1)}, u32[]{:S(2)}, u32[]{:S(2)}) collective-permute-start(bf16[256,512]{1,0:T(8,128)(2,1)} %collective-permute-done.18), channel_id=1, source_target_pairs={{8,0},{0,8},{24,16},{16,24},{9,1},{1,9},{25,17},{17,25},{10,2},{2,... | collective-permute-start | bytes 786440 | tf_op jit(solution)/shard_map/ppermute | solution.py:60
  181.0 69.6 %collective-permute-start.31 = (bf16[512,1024]{1,0:T(8,128)(2,1)}, bf16[512,1024]{1,0:T(8,128)(2,1)S(1)}, u32[]{:S(2)}, u32[]{:S(2)}) collective-permute-start(bf16[512,1024]{1,0:T(8,128)(2,1)} %convert_element_type.402), channel_id=1, source_target_pairs={{16,0},{24,8},{0,16},{8,24},{17,1},{25,9},{1,17},{9,25},{18,2},{26... | collective-permute-start | bytes 3145736 | tf_op jit(solution)/shard_map/ppermute | solution.py:60
  182.5 68.5 %collective-permute-start.32 = (bf16[512,1024]{1,0:T(8,128)(2,1)}, bf16[512,1024]{1,0:T(8,128)(2,1)S(1)}, u32[]{:S(2)}, u32[]{:S(2)}) collective-permute-start(bf16[512,1024]{1,0:T(8,128)(2,1)} %convert_element_type.402), channel_id=1, source_target_pairs={{8,0},{0,8},{24,16},{16,24},{9,1},{1,9},{25,17},{17,25},{10,2},{2,... | collective-permute-start | bytes 3145736 | tf_op jit(solution)/shard_map/ppermute | solution.py:60
  245.0 53.3 %collective-permute-start.41 = (bf16[1024,512]{1,0:T(8,128)(2,1)S(1)}, bf16[1024,512]{1,0:T(8,128)(2,1)}, u32[]{:S(2)}, u32[]{:S(2)}) collective-permute-start(bf16[1024,512]{1,0:T(8,128)(2,1)S(1)} %convert_element_type.404), channel_id=1, source_target_pairs={{4,0},{5,1},{6,2},{7,3},{0,4},{1,5},{2,6},{3,7},{12,8},{13,9},{14,... | collective-permute-start | bytes 3145736 | tf_op jit(solution)/shard_map/ppermute | solution.py:67
  261.7 60.5 %collective-permute-start.35 = (bf16[512,1024]{1,0:T(8,128)(2,1)}, bf16[512,1024]{1,0:T(8,128)(2,1)}, u32[]{:S(2)}, u32[]{:S(2)}) collective-permute-start(bf16[512,1024]{1,0:T(8,128)(2,1)} %collective-permute-done.34), channel_id=1, source_target_pairs={{16,0},{24,8},{0,16},{8,24},{17,1},{25,9},{1,17},{9,25},{18,2},{26... | collective-permute-start | bytes 3145736 | tf_op jit(solution)/shard_map/ppermute | solution.py:60
  347.4 49.4 %collective-permute-start.39 = (bf16[1024,512]{1,0:T(8,128)(2,1)S(1)}, bf16[1024,512]{1,0:T(8,128)(2,1)}, u32[]{:S(2)}, u32[]{:S(2)}) collective-permute-start(bf16[1024,512]{1,0:T(8,128)(2,1)S(1)} %copy-done.52), channel_id=1, source_target_pairs={{8,0},{0,8},{24,16},{16,24},{9,1},{1,9},{25,17},{17,25},{10,2},{2,... | collective-permute-start | bytes 3145736 | tf_op jit(solution)/shard_map/ppermute | solution.py:60
  348.0 48.8 %collective-permute-start.43 = (bf16[1024,512]{1,0:T(8,128)(2,1)}, bf16[1024,512]{1,0:T(8,128)(2,1)}, u32[]{:S(2)}, u32[]{:S(2)}) collective-permute-start(bf16[1024,512]{1,0:T(8,128)(2,1)} %collective-permute-done.41), channel_id=1, source_target_pairs={{8,0},{0,8},{24,16},{16,24},{9,1},{1,9},{25,17},{17,25},{10,2},{2,... | collective-permute-start | bytes 3145736 | tf_op jit(solution)/shard_map/ppermute | solution.py:60
  348.0 48.7 %collective-permute-start.40 = (bf16[1024,512]{1,0:T(8,128)(2,1)}, bf16[1024,512]{1,0:T(8,128)(2,1)}, u32[]{:S(2)}, u32[]{:S(2)}) collective-permute-start(bf16[1024,512]{1,0:T(8,128)(2,1)} %collective-permute-done.38), channel_id=1, source_target_pairs={{8,0},{0,8},{24,16},{16,24},{9,1},{1,9},{25,17},{17,25},{10,2},{2,... | collective-permute-start | bytes 3145736 | tf_op jit(solution)/shard_map/ppermute | solution.py:60
  553.6 113.3 %collective-permute-start.78 = (bf16[1024,2048]{1,0:T(8,128)(2,1)}, bf16[1024,2048]{1,0:T(8,128)(2,1)}, u32[]{:S(2)}, u32[]{:S(2)}) collective-permute-start(bf16[1024,2048]{1,0:T(8,128)(2,1)} %slice.446), channel_id=1, source_target_pairs={{8,0},{0,8},{24,16},{16,24},{9,1},{1,9},{25,17},{17,25},{10,2},{2,... | collective-permute-start | bytes 12582920 | tf_op jit(solution)/shard_map/ppermute | solution.py:60
  571.4 103.1 %collective-permute-start.81 = (bf16[2048,1024]{1,0:T(8,128)(2,1)}, bf16[2048,1024]{1,0:T(8,128)(2,1)}, u32[]{:S(2)}, u32[]{:S(2)}) collective-permute-start(bf16[2048,1024]{1,0:T(8,128)(2,1)} %slice.452), channel_id=1, source_target_pairs={{8,0},{0,8},{24,16},{16,24},{9,1},{1,9},{25,17},{17,25},{10,2},{2,... | collective-permute-start | bytes 12582920 | tf_op jit(solution)/shard_map/ppermute | solution.py:60
  674.5 52.6 %collective-permute-start.79 = (bf16[512,2048]{1,0:T(8,128)(2,1)}, bf16[512,2048]{1,0:T(8,128)(2,1)}, u32[]{:S(2)}, u32[]{:S(2)}) collective-permute-start(bf16[512,2048]{1,0:T(8,128)(2,1)} %slice.448), channel_id=1, source_target_pairs={{16,0},{24,8},{0,16},{8,24},{17,1},{25,9},{1,17},{9,25},{18,2},{26... | collective-permute-start | bytes 6291464 | tf_op jit(solution)/shard_map/ppermute | solution.py:60
  680.4 91.5 %collective-permute-start.82 = (bf16[2048,512]{1,0:T(8,128)(2,1)S(1)}, bf16[2048,512]{1,0:T(8,128)(2,1)S(1)}, u32[]{:S(2)}, u32[]{:S(2)}) collective-permute-start(bf16[2048,512]{1,0:T(8,128)(2,1)S(1)} %slice.454), channel_id=1, source_target_pairs={{16,0},{24,8},{0,16},{8,24},{17,1},{25,9},{1,17},{9,25},{18,2},{26... | collective-permute-start | bytes 6291464 | tf_op jit(solution)/shard_map/ppermute | solution.py:60
  694.8 109.0 %collective-permute-start.73 = (bf16[512,1536]{0,1:T(8,128)(2,1)S(1)}, bf16[512,1536]{0,1:T(8,128)(2,1)S(1)}, u32[]{:S(2)}, u32[]{:S(2)}) collective-permute-start(bf16[512,1536]{0,1:T(8,128)(2,1)S(1)} %slice.436), channel_id=1, source_target_pairs={{16,0},{24,8},{0,16},{8,24},{17,1},{25,9},{1,17},{9,25},{18,2},{26... | collective-permute-start | bytes 4718600 | tf_op jit(solution)/shard_map/ppermute | solution.py:60
  729.5 79.0 %collective-permute-start.80 = (bf16[512,1024]{1,0:T(8,128)(2,1)S(1)}, bf16[512,1024]{1,0:T(8,128)(2,1)S(1)}, u32[]{:S(2)}, u32[]{:S(2)}) collective-permute-start(bf16[512,1024]{1,0:T(8,128)(2,1)S(1)} %slice.450), channel_id=1, source_target_pairs={{4,0},{5,1},{6,2},{7,3},{0,4},{1,5},{2,6},{3,7},{12,8},{13,9},{14,... | collective-permute-start | bytes 3145736 | tf_op jit(solution)/shard_map/ppermute | solution.py:67
  772.8 65.4 %collective-permute-start.83 = (bf16[1024,512]{1,0:T(8,128)(2,1)S(1)}, bf16[1024,512]{1,0:T(8,128)(2,1)S(1)}, u32[]{:S(2)}, u32[]{:S(2)}) collective-permute-start(bf16[1024,512]{1,0:T(8,128)(2,1)S(1)} %slice.456), channel_id=1, source_target_pairs={{4,0},{5,1},{6,2},{7,3},{0,4},{1,5},{2,6},{3,7},{12,8},{13,9},{14,... | collective-permute-start | bytes 3145736 | tf_op jit(solution)/shard_map/ppermute | solution.py:67
  804.5 49.0 %collective-permute-start.74 = (bf16[512,768]{0,1:T(8,128)(2,1)S(1)}, bf16[512,768]{0,1:T(8,128)(2,1)S(1)}, u32[]{:S(2)}, u32[]{:S(2)}) collective-permute-start(bf16[512,768]{0,1:T(8,128)(2,1)S(1)} %slice.438), channel_id=1, source_target_pairs={{4,0},{5,1},{6,2},{7,3},{0,4},{1,5},{2,6},{3,7},{12,8},{13,9},{14,... | collective-permute-start | bytes 2359304 | tf_op jit(solution)/shard_map/ppermute | solution.py:67
  (168 other events, 4238.4 us)

commit v2 on v1

v2 whole, which is shorter than its diff:
```python
import jax
import jax.numpy as jnp
from jax import lax
from jax.experimental import pallas as pl
from jax.experimental.pallas import tpu as pltpu
from jax.sharding import Mesh
from jax.sharding import PartitionSpec as P

HD = 128
BINS = 8
ADAM_STEP = 10

clip_limit = 1.0
beta_one = 0.9
beta_two = 0.95
learn_rate = 0.02
output_rate = 0.08
adam_epsilon = 1e-08
decay_rate = 0.01

BF = jnp.bfloat16
F32 = jnp.float32


def norm_rows(values):
    center = values - jnp.mean(values, axis=-1, keepdims=True)
    spread = jnp.mean(center * center, axis=-1, keepdims=True)
    return center * lax.rsqrt(spread + 1e-06)


def gelu_tanh(values):
    return jax.nn.gelu(values, approximate=True)


def adam_update(gradient, moment_one, moment_two, weight, factor, step_rate):
    clipped = gradient * factor
    new_one = beta_one * moment_one + (1.0 - beta_one) * clipped
    new_two = beta_two * moment_two + (1.0 - beta_two) * clipped * clipped
    corrected = new_one / (1.0 - beta_one**ADAM_STEP)
    root_two = jnp.sqrt(new_two / (1.0 - beta_two**ADAM_STEP))
    new_weight = weight - step_rate * (corrected / (root_two + adam_epsilon) + decay_rate * weight)
    return (new_one, new_two, new_weight)


def sync(*values):
    return lax.optimization_barrier(values)


def dot(a, b, contract=(1, 0)):
    return lax.dot_general(
        a, b, (((contract[0],), (contract[1],)), ((), ())), preferred_element_type=F32
    )


def rows_of(ref, columns=slice(None)):
    value = ref[0, :, :, columns]
    return value.reshape(value.shape[0] * value.shape[1], value.shape[2])


def join_tokens(pieces, whole):
    for kind, two in enumerate(pieces):
        for r, ref in enumerate(two):
            t = ref.shape[1]
            whole[0, kind, r * t : (r + 1) * t] = ref[0]


def put_parts(value, columns, parts):
    half = value.shape[0] // (2 * len(parts))
    for kind, (keep, send) in enumerate(parts):
        keep[0, :, columns] = value[2 * kind * half : (2 * kind + 1) * half]
        send[0, :, columns] = value[(2 * kind + 1) * half : (2 * kind + 2) * half]


def softmax_rows(q, k):
    scores = dot(q, k, (1, 1)) * HD ** (-0.5)
    weights = jnp.exp(scores - jnp.max(scores, axis=-1, keepdims=True))
    return weights / jnp.sum(weights, axis=-1, keepdims=True)


def head_columns(jh, part, n, block):
    start = (jh * 3 + part) * block + n * HD
    return slice(start, start + HD)


class Pieces:
    def __init__(self, refs):
        self.refs, self.at = refs, 0

    def take(self, count):
        self.at += count
        return self.refs[self.at - count : self.at]

    def tokens(self):
        near_far = self.take(4)
        return near_far[:2], near_far[2:]

    def parts(self):
        a, b, c, d = self.take(4)
        return (a, b), (c, d)


class Separate:
    def __init__(self, refs, nd):
        self.refs, self.depth = refs, refs[0].shape[0]
        self.shape = refs[0].shape[1:]

    def block(self, jh, d, rows=slice(None), columns=slice(None)):
        core, x = divmod(d, self.depth)
        return self.refs[2 * jh + core][x, rows, columns]


def attention_kernel(nh, nd, gates, *refs):
    refs = Pieces(refs)
    tokens, weights = refs.tokens(), Separate(refs.take(2 * nh), nd)
    refs.take(gates)
    (a, qkv, o), parts = refs.take(3), refs.parts()
    join_tokens(tokens, a)
    depth, block = weights.shape[0], weights.shape[1] // 4
    width = 3 * block
    inward = (slice(None), slice(0, width))
    outward = (slice(None), slice(width, width + block))
    kinds, length = a.shape[1], a.shape[2]
    for jh in range(nh):
        total = dot(rows_of(a, slice(0, depth)), weights.block(jh, 0, *inward))
        for d in range(1, nd):
            total += dot(rows_of(a, slice(d * depth, (d + 1) * depth)), weights.block(jh, d, *inward))
        qkv[0, :, :, jh * width : (jh + 1) * width] = total.astype(BF).reshape(kinds, length, width)
    for kind in range(kinds):
        for jh in range(nh):
            for n in range(block // HD):
                q, k, v = (qkv[0, kind, :, head_columns(jh, i, n, block)] for i in range(3))
                out = dot(softmax_rows(q, k).astype(BF), v).astype(BF)
                o[0, kind, :, jh * block + n * HD : jh * block + (n + 1) * HD] = out
    for d in range(nd):
        total = dot(rows_of(o, slice(0, block)), weights.block(0, d, *outward), (1, 1))
        for jh in range(1, nh):
            total += dot(rows_of(o, slice(jh * block, (jh + 1) * block)), weights.block(jh, d, *outward), (1, 1))
        put_parts(total.astype(BF), slice(d * depth, (d + 1) * depth), parts)


def mlp_kernel(nh, nd, gates, *refs):
    refs = Pieces(refs)
    b_tokens, df_tokens = refs.tokens(), refs.tokens()
    wu, wd = (Separate(refs.take(2 * nh), nd) for _ in range(2))
    refs.take(gates)
    (b, df, hidden, du), parts = refs.take(4), refs.parts()
    join_tokens(b_tokens, b)
    join_tokens(df_tokens, df)
    depth, width = wu.shape
    kinds, length = b.shape[1], b.shape[2]
    chunk = min(width, 512)
    curve, cubic = 0.7978845608028654, 0.044715
    for jh in range(nh):
        for c in range(0, width, chunk):
            part = slice(c, c + chunk)
            u = dot(rows_of(b, slice(0, depth)), wu.block(jh, 0, columns=part))
            dh = dot(rows_of(df, slice(0, depth)), wd.block(jh, 0, part), (1, 1))
            for d in range(1, nd):
                cols = slice(d * depth, (d + 1) * depth)
                u += dot(rows_of(b, cols), wu.block(jh, d, columns=part))
                dh += dot(rows_of(df, cols), wd.block(jh, d, part), (1, 1))
            square = u * u
            t = jnp.tanh(curve * u * (1.0 + cubic * square))
            near = 0.5 * (1.0 + t)
            slope = near + 0.5 * u * (1.0 - t * t) * (curve * (1.0 + 3.0 * cubic * square))
            cols = slice(jh * width + c, jh * width + c + chunk)
            hidden[0, :, :, cols] = (u * near).astype(BF).reshape(kinds, length, chunk)
            du[0, :, :, cols] = (dh * slope).astype(BF).reshape(kinds, length, chunk)
    for d in range(nd):
        total = dot(rows_of(du, slice(0, width)), wu.block(0, d), (1, 1))
        for jh in range(1, nh):
            total += dot(rows_of(du, slice(jh * width, (jh + 1) * width)), wu.block(jh, d), (1, 1))
        put_parts(total.astype(BF), slice(d * depth, (d + 1) * depth), parts)


def down_kernel(nh, nd, gates, *refs):
    refs = Pieces(refs)
    (hidden,), wd = refs.take(1), Separate(refs.take(2 * nh), nd)
    refs.take(gates)
    parts = refs.parts()
    width, depth = wd.shape
    for d in range(nd):
        total = dot(rows_of(hidden, slice(0, width)), wd.block(0, d))
        for jh in range(1, nh):
            total += dot(rows_of(hidden, slice(jh * width, (jh + 1) * width)), wd.block(jh, d))
        put_parts(total.astype(BF), slice(d * depth, (d + 1) * depth), parts)


def attention_back_kernel(nh, nd, gates, *refs):
    refs = Pieces(refs)
    tokens, (qkv,) = refs.tokens(), refs.take(1)
    weights = Separate(refs.take(2 * nh), nd)
    refs.take(gates)
    (datt, dqkv), parts = refs.take(2), refs.parts()
    join_tokens(tokens, datt)
    depth, block = weights.shape[0], weights.shape[1] // 4
    width = 3 * block
    inward = (slice(None), slice(0, width))
    outward = (slice(None), slice(width, width + block))
    kinds, length = datt.shape[1], datt.shape[2]
    for jh in range(nh):
        do_all = dot(rows_of(datt, slice(0, depth)), weights.block(jh, 0, *outward))
        for d in range(1, nd):
            do_all += dot(rows_of(datt, slice(d * depth, (d + 1) * depth)), weights.block(jh, d, *outward))
        do_all = do_all.astype(BF)
        for kind in range(kinds):
            for n in range(block // HD):
                q, k, v = (qkv[0, kind, :, head_columns(jh, i, n, block)] for i in range(3))
                do = do_all[kind * length : (kind + 1) * length, n * HD : (n + 1) * HD]
                p = softmax_rows(q, k)
                dv = dot(p.astype(BF), do, (0, 0))
                dp = dot(do, v, (1, 1))
                ds = (p * (dp - jnp.sum(p * dp, axis=-1, keepdims=True))).astype(BF)
                dq = dot(ds, k) * HD ** (-0.5)
                dk = dot(ds, q, (0, 0)) * HD ** (-0.5)
                for i, value in enumerate((dq, dk, dv)):
                    dqkv[0, kind, :, head_columns(jh, i, n, block)] = value.astype(BF)
    for d in range(nd):
        total = dot(rows_of(dqkv, slice(0, width)), weights.block(0, d, *inward), (1, 1))
        for jh in range(1, nh):
            total += dot(rows_of(dqkv, slice(jh * width, (jh + 1) * width)), weights.block(jh, d, *inward), (1, 1))
        put_parts(total.astype(BF), slice(d * depth, (d + 1) * depth), parts)


def group_call(kernel, name, nh, nd, steps, blocked, whole, gates, outs):
    def cut(shape):
        zeros = (0,) * (len(shape) - 1)
        return pl.BlockSpec((1,) + tuple(shape[1:]), lambda i: (i,) + zeros)

    return pl.pallas_call(
        lambda *refs: kernel(nh, nd, len(gates), *refs),
        name=name,
        grid=(steps,),
        in_specs=[cut(v.shape) for v in blocked]
        + [pl.BlockSpec(memory_space=pltpu.VMEM)] * len(whole)
        + [pl.BlockSpec(memory_space=pl.ANY)] * len(gates),
        out_specs=[cut(s) for s in outs],
        out_shape=[jax.ShapeDtypeStruct(s, BF) for s in outs],
        compiler_params=pltpu.CompilerParams(vmem_limit_bytes=60 * 2**20),
        cost_estimate=pl.CostEstimate(flops=0, bytes_accessed=0, transcendentals=0),
    )(*blocked, *whole, *gates)


def pack_attention_weights(w_qkv, w_out):
    depth, _, block = w_qkv.shape

    def kernel(inward, outward, packed):
        for i in range(3):
            packed[:, i * block : (i + 1) * block] = inward[i].astype(BF)
        packed[:, 3 * block :] = outward[...].T.astype(BF)

    return pl.pallas_call(
        kernel,
        name="pack",
        out_shape=jax.ShapeDtypeStruct((depth, 4 * block), BF),
        compiler_params=pltpu.CompilerParams(vmem_limit_bytes=32 * 2**20),
    )(w_qkv.transpose(1, 0, 2), w_out)


def gradient(name, nh, nd, left, right, left_is_hidden, core):
    rows = left.shape[0]
    hidden, features = (left, right) if left_is_hidden else (right, left)
    h_width, d_width, half = hidden.shape[1] // nh, features.shape[1] // nd, nd // 2

    def kernel(left, right, out):
        out[...] = dot(left[...], right[...], (0, 0)).astype(BF)

    h_spec = pl.BlockSpec((rows, h_width), lambda jh, d: (0, jh))
    d_spec = pl.BlockSpec((rows, d_width), lambda jh, d: (0, core * half + d))
    if left_is_hidden:
        in_specs, out_spec = [h_spec, d_spec], pl.BlockSpec((h_width, d_width), lambda jh, d: (jh, d))
        shape = (nh * h_width, half * d_width)
    else:
        in_specs, out_spec = [d_spec, h_spec], pl.BlockSpec((d_width, h_width), lambda jh, d: (d, jh))
        shape = (half * d_width, nh * h_width)
    return pl.pallas_call(
        kernel,
        name=name,
        grid=(nh, half),
        in_specs=in_specs,
        out_specs=out_spec,
        out_shape=jax.ShapeDtypeStruct(shape, BF),
        compiler_params=pltpu.CompilerParams(vmem_limit_bytes=48 * 2**20),
        cost_estimate=pl.CostEstimate(flops=0, bytes_accessed=0, transcendentals=0),
    )(left, right)


class Links:
    everywhere = ("x", "core", "h")

    def __init__(self, n_dp, n_mp):
        self.X, self.H = n_dp // 2, n_mp // 4
        self.n_dp, self.n_mp = n_dp, n_mp

    def shifted(self, v, axis, size, offset, name):
        with jax.named_scope(f"{name}_{axis}"):
            return lax.ppermute(v, axis, [((dst + offset) % size, dst) for dst in range(size)])

    def from_core(self, v, name):
        return self.shifted(v, "core", 2, 1, name)

    def from_x(self, v, jx, name):
        return self.shifted(v, "x", self.X, jx, name)

    def from_h(self, v, jh, name):
        return self.shifted(v, "h", self.H, jh, name)

    def over_h(self, w, name):
        return [self.from_h(w, jh, name) for jh in range(1, self.H)]

    def over_x(self, w, name):
        return [self.from_x(w, jx, name) for jx in range(1, self.X)]

    def part(self, g, d, h, jx, far):
        width = g.shape[d] // self.X
        g = lax.slice_in_dim(g, jx * width, (jx + 1) * width, axis=d)
        width = g.shape[h] // self.H
        return lax.slice_in_dim(g, width if far else 0, g.shape[h] if far else width, axis=h)

    def send_x(self, g, d, h, far, name):
        return [self.from_x(self.part(g, d, h, jx, far), -jx, name) for jx in range(1, self.X)]

    def sum_x(self, g, d, h, far, received):
        return self.part(g, d, h, 0, far).astype(F32) + sum(v.astype(F32) for v in received)

    def send_h(self, g, h, name, rows=None):
        width = g.shape[h] // (self.H - 1)
        received = []
        for jh in range(1, self.H):
            block = lax.slice_in_dim(g, (jh - 1) * width, jh * width, axis=h)
            if rows is not None:
                size = block.shape[0] // 2
                block = block[rows * size : (rows + 1) * size]
            received.append(self.from_h(block, -jh, name))
        return received

    def for_groups(self, v):
        here = lax.axis_index("h")
        images = v.shape[0] // self.H
        return [
            lax.dynamic_slice_in_dim(v, ((here - jh) % self.H) * images, images, axis=0)
            for jh in range(self.H)
        ]

    def to_group(self, parts, name):
        return [self.from_h(parts[jh], jh, name) for jh in range(1, self.H)]

    def leave_group(self, v, name):
        tokens = v.shape[1] // self.H
        return [
            self.from_h(v[:, jh * tokens : (jh + 1) * tokens], -jh, name) for jh in range(1, self.H)
        ]

    def at_home(self, v, received):
        here = lax.axis_index("h")
        images = v.shape[0]
        tokens = v.shape[1] // self.H
        out = jnp.zeros((images * self.H, tokens, v.shape[2]), v.dtype)
        for jh, part in enumerate([v[:, :tokens], *received]):
            out = lax.dynamic_update_slice_in_dim(
                out, part, ((here - jh) % self.H) * images, axis=0
            )
        return self.features_home(out)

    def over(self, v, kind, late, name):
        return self.shifted(v, "p" if (kind == 0) != late else "q", 2, 1, f"{name}{kind}")

    def first_hop(self, v, name):
        half = v.shape[0] // 2
        own = [v[k * half : (k + 1) * half] for k in range(2)]
        return [(own[k], self.over(own[k], k, False, name)) for k in range(2)]

    def near(self, hops):
        return [jnp.concatenate(pair, axis=1) for pair in hops]

    def last_hop(self, near, name):
        return [self.over(near[k], k, True, name) for k in range(2)]

    def send_late(self, parts, name):
        return [self.over(parts[2 * k + 1], k, True, name) for k in range(2)]

    def onward(self, parts, got):
        t = parts[0].shape[1] // 2
        return [
            (parts[2 * k][:, t:].astype(F32) + got[k][:, t:].astype(F32)).astype(BF)
            for k in range(2)
        ]

    def send_on(self, onward, name):
        return [self.over(onward[k], k, False, name) for k in range(2)]

    def total_tokens(self, parts, got, last):
        t = parts[0].shape[1] // 2
        return jnp.concatenate(
            [
                parts[2 * k][:, :t].astype(F32) + got[k][:, :t].astype(F32) + last[k].astype(F32)
                for k in range(2)
            ],
            axis=0,
        )

    def features_here(self, v):
        x, c = lax.axis_index("x"), lax.axis_index("core")
        width = v.shape[-1] // self.n_dp
        return jnp.concatenate(
            [
                lax.dynamic_slice_in_dim(
                    v, (((x + jx) % self.X) * 2 + (c ^ jc)) * width, width, axis=v.ndim - 1
                )
                for jc in range(2)
                for jx in range(self.X)
            ],
            axis=-1,
        )

    def features_home(self, v):
        x, c = lax.axis_index("x"), lax.axis_index("core")
        width = v.shape[-1] // self.n_dp
        return jnp.concatenate(
            [
                lax.dynamic_slice_in_dim(
                    v,
                    (((e % 2) ^ c) * self.X + (e // 2 - x) % self.X) * width,
                    width,
                    axis=v.ndim - 1,
                )
                for e in range(self.n_dp)
            ],
            axis=-1,
        )

    def total(self, v):
        for axis, size in (("core", 2), ("q", 2), ("p", 2), ("x", self.X), ("h", self.H)):
            step = 1
            while step < size:
                with jax.named_scope("norm"):
                    v = v + lax.ppermute(v, axis, [(i ^ step, i) for i in range(size)])
                step *= 2
        return v


def per_device(
    links,
    stream_in,
    cotangent,
    noise_table,
    timesteps,
    bins,
    counts,
    w_qkv,
    w_out,
    w_up,
    w_down,
    m_qkv,
    m_out,
    m_up,
    m_down,
    v_qkv,
    v_out,
    v_up,
    v_down,
):
    H = links.H
    slots, _, D = stream_in.shape
    images = slots // H
    here = lax.axis_index("h")

    steps_here = lax.dynamic_slice_in_dim(timesteps, here * images, images)
    table_rows = noise_table.shape[0]
    picks = (steps_here[:, None] == jnp.arange(table_rows)[None, :]).astype(F32)
    modulation = jnp.dot(
        picks, noise_table.reshape(table_rows, -1), precision=lax.Precision.HIGHEST
    ).reshape(images, 6, D)
    modulation = links.features_here(modulation)
    shift_a, scale_a, gate_a, shift_f, scale_f, gate_f = (modulation[:, i : i + 1] for i in range(6))
    live = jnp.arange(slots) < counts[0]
    loss_scale = live.astype(F32) * (bins.astype(F32) + 1.0) / BINS
    loss_scale = lax.dynamic_slice_in_dim(loss_scale, here * images, images)

    def first_norm(rows):
        return norm_rows(rows) * scale_a + shift_a

    def second_norm(rows):
        return norm_rows(rows) * scale_f + shift_f

    block = w_qkv.shape[2]
    length = stream_in.shape[1] * H * 4
    steps = images // 2
    rows = images * length
    nh, nd = H, 2 * links.X
    heads = H * block
    hidden_width = H * w_up.shape[1]
    whole = lambda width: (steps, 2, length, width)
    parts = [(steps, length // 2, D)] * 4

    def flat(v):
        return v.reshape(rows, v.shape[-1])

    def call(kernel, name, blocked, weights, gates, outs):
        return list(
            group_call(kernel, name, nh, nd, steps, blocked, weights, gates, outs + parts)
        )

    def halves(w):
        size = w.shape[0] // 2
        return w[:size], w[size:]

    def joined(pair):
        return [jnp.concatenate(two, axis=0) for two in zip(*pair)]

    def add_core(keep, sent):
        return (keep.astype(F32) + sent.astype(F32)).astype(BF)

    stream_parts = links.for_groups(links.features_here(stream_in))
    packed = pack_attention_weights(w_qkv, w_out)
    up, down = w_up.astype(BF), w_down.astype(BF)
    stream_got = links.to_group(stream_parts, "stream")
    x_packed = links.over_x(packed, "wqo0")
    stream_parts, stream_got, x_packed, packed, up = sync(
        stream_parts, stream_got, x_packed, packed, up
    )

    stream = jnp.concatenate([stream_parts[0], *stream_got], axis=1).astype(F32)
    a_hops = links.first_hop(first_norm(stream).astype(BF), "a")
    packed_halves = halves(packed)
    far_one = links.over_h(packed_halves[0], "wqoA")
    x_up = links.over_x(up, "wu0")
    wqo = [jnp.stack([packed, *x_packed])]
    a_hops, wqo = sync(a_hops, wqo)
    wqo.append(links.from_core(wqo[0], "wqo0"))
    a_near = links.near(a_hops)
    a_near, far_one, x_up, wqo, packed_two, down = sync(
        a_near, far_one, x_up, wqo, packed_halves[1], down
    )

    a_far = links.last_hop(a_near, "a")
    far_two = links.over_h(packed_two, "wqoB")
    x_down = links.over_x(down, "wd0")
    cot_parts = links.for_groups(links.features_here(cotangent.astype(BF)))
    a_far, far_two, x_down, cot_parts = sync(a_far, far_two, x_down, cot_parts)

    packed_far = joined((far_one, far_two))
    x_far = [links.over_x(w, "wqo1") for w in packed_far]
    cot_got = links.to_group(cot_parts, "cot")
    wu = [jnp.stack([up, *x_up])]
    wu.append(links.from_core(wu[0], "wu0"))
    wd = [jnp.stack([down, *x_down])]
    wd, wu = sync(wd, wu)
    wd.append(links.from_core(wd[0], "wd0"))
    packed_far, x_far, cot_got, wu, wd, up = sync(packed_far, x_far, cot_got, wu, wd, up)

    cot = jnp.concatenate([cot_parts[0], *cot_got], axis=1).astype(F32)
    dy = cot * loss_scale[:, None, None]
    df_hops = links.first_hop((gate_f * dy).astype(BF), "df")
    for w, others in zip(packed_far, x_far):
        wqo.append(jnp.stack([w, *others]))
        wqo.append(links.from_core(wqo[-1], "wqo1"))
    up_halves = halves(up)
    up_one = links.over_h(up_halves[0], "wuA")
    df_near, wqo = sync(links.near(df_hops), wqo)

    df_far = links.last_hop(df_near, "df")
    a_rows, qkv, o, *att = call(
        attention_kernel,
        "attention",
        [a_near[0], a_far[0], a_near[1], a_far[1]],
        wqo,
        [],
        [whole(D), whole(3 * heads), whole(heads)],
    )
    df_far, att, up_one, up_two = sync(df_far, att, up_one, up_halves[1])

    att_got = links.send_late(att, "att")
    up_two = links.over_h(up_two, "wuB")
    att_got, up_two, down = sync(att_got, up_two, down)

    att_last = links.send_on(links.onward(att, att_got), "att")
    down_halves = halves(down)
    down_one = links.over_h(down_halves[0], "wdA")
    up_far = joined((up_one, up_two))
    x_up = [links.over_x(w, "wu1") for w in up_far]
    residual = stream + gate_a * links.total_tokens(att, att_got, att_last)
    b = second_norm(residual).astype(BF)
    b, down_one, up_far, x_up, down_two = sync(b, down_one, up_far, x_up, down_halves[1])

    b_hops = links.first_hop(b, "b")
    down_two = links.over_h(down_two, "wdB")
    for w, others in zip(up_far, x_up):
        wu.append(jnp.stack([w, *others]))
        wu.append(links.from_core(wu[-1], "wu1"))
    b_near, wu, down_one = sync(links.near(b_hops), wu, down_one)
    x_one = [links.over_x(w, "wdA1") for w in down_one]
    down_two, x_one, b_near = sync(down_two, x_one, b_near)

    b_far = links.last_hop(b_near, "b")
    x_two = [links.over_x(w, "wdB1") for w in down_two]
    for w, one, two in zip(joined((down_one, down_two)), x_one, x_two):
        wd.append(jnp.stack([w, *joined((one, two))]))
        wd.append(links.from_core(wd[-1], "wd1"))
    b_far, wd = sync(b_far, wd)

    b_rows, df_rows, hidden, du, *db = call(
        mlp_kernel,
        "mlp",
        [b_near[0], b_far[0], b_near[1], b_far[1], df_near[0], df_far[0], df_near[1], df_far[1]],
        wu + wd,
        [],
        [whole(D), whole(D), whole(hidden_width), whole(hidden_width)],
    )
    b_rows, df_rows, hidden, du, db = sync(b_rows, df_rows, hidden, du, db)

    db_got = links.send_late(db, "db")
    left, right = flat(hidden), flat(df_rows)
    g_send = gradient("g_down_send", nh, nd, left, right, True, 1)
    g_sent = links.from_core(g_send, "g_down")
    g_keep = gradient("g_down_keep", nh, nd, left, right, True, 0)
    db_got, g_sent, g_keep, b_rows, du = sync(db_got, g_sent, g_keep, b_rows, du)

    db_last = links.send_on(links.onward(db, db_got), "db")
    g_down = add_core(g_keep, g_sent)
    down_far = links.send_x(g_down, 1, 0, True, "g_downA")
    left, right = flat(b_rows), flat(du)
    g_send = gradient("g_up_send", nh, nd, left, right, False, 1)
    g_sent = links.from_core(g_send, "g_up")
    g_keep = gradient("g_up_keep", nh, nd, left, right, False, 0)
    dr = dy + jax.vjp(second_norm, residual)[1](links.total_tokens(db, db_got, db_last))[0]
    datt = (gate_a * dr).astype(BF)
    datt, g_down, down_far, g_sent, g_keep, hidden = sync(
        datt, g_down, down_far, g_sent, g_keep, hidden
    )

    datt_hops = links.first_hop(datt, "datt")
    down_far = links.sum_x(g_down, 1, 0, True, down_far).astype(BF)
    down_here = links.send_x(g_down, 1, 0, False, "g_downB")
    down_one = links.send_h(down_far, 0, "g_downA", 0)
    ff = call(down_kernel, "down", [hidden], wd, [], [])
    g_up = add_core(g_keep, g_sent)
    datt_near, down_far, down_here, down_one, ff, g_up = sync(
        links.near(datt_hops), down_far, down_here, down_one, ff, g_up
    )

    datt_far = links.last_hop(datt_near, "datt")
    down_here = links.sum_x(g_down, 1, 0, False, down_here)
    down_two = links.send_h(down_far, 0, "g_downB", 1)
    up_far = links.send_x(g_up, 0, 1, True, "g_upA")
    datt_far, down_two, up_far, g_up, ff = sync(datt_far, down_two, up_far, g_up, ff)

    up_far = links.sum_x(g_up, 0, 1, True, up_far).astype(BF)
    up_one = links.send_h(up_far, 1, "g_upA", 0)
    up_here = links.send_x(g_up, 0, 1, False, "g_upB")
    ff_got = links.send_late(ff, "ff")
    datt, dqkv, *da = call(
        attention_back_kernel,
        "attention_back",
        [datt_near[0], datt_far[0], datt_near[1], datt_far[1], qkv],
        wqo,
        [],
        [whole(D), whole(3 * heads)],
    )
    up_far, up_one, up_here, ff_got, datt, dqkv, da = sync(
        up_far, up_one, up_here, ff_got, datt, dqkv, da
    )

    up_two = links.send_h(up_far, 1, "g_upB", 1)
    da_got = links.send_late(da, "da")
    left, right = flat(a_rows), flat(dqkv)
    g_send = gradient("g_qkv_send", nh, nd, left, right, False, 1)
    g_sent = links.from_core(g_send, "g_qkv")
    g_keep = gradient("g_qkv_keep", nh, nd, left, right, False, 0)
    left, right = sync(flat(datt), flat(o), g_keep)[:2]
    o_send = gradient("g_out_send", nh, nd, left, right, False, 1)
    o_sent = links.from_core(o_send, "g_out")
    o_keep = gradient("g_out_keep", nh, nd, left, right, False, 0)
    up_two, da_got, g_sent, g_keep, o_sent, o_keep = sync(
        up_two, da_got, g_sent, g_keep, o_sent, o_keep
    )

    g_qkv, g_out = add_core(g_keep, g_sent), add_core(o_keep, o_sent)
    qkv_far = links.send_x(g_qkv, 0, 1, True, "g_qkvA")
    da_last = links.send_on(links.onward(da, da_got), "da")
    ff_last = links.send_on(links.onward(ff, ff_got), "ff")
    qkv_far, da_last, ff_last, g_qkv, g_out = sync(qkv_far, da_last, ff_last, g_qkv, g_out)

    qkv_far = links.sum_x(g_qkv, 0, 1, True, qkv_far).astype(BF)
    qkv_there = links.send_h(qkv_far, 1, "g_qkv")
    qkv_here = links.send_x(g_qkv, 0, 1, False, "g_qkvB")
    out_far = links.send_x(g_out, 0, 1, True, "g_outA")
    out_here = links.send_x(g_out, 0, 1, False, "g_outB")
    output = (residual + gate_f * links.total_tokens(ff, ff_got, ff_last)).astype(BF)
    da = links.total_tokens(da, da_got, da_last)
    input_grad = (dr + jax.vjp(first_norm, stream)[1](da)[0]).astype(BF)
    qkv_there, qkv_here, out_far, out_here, g_out, output, input_grad = sync(
        qkv_there, qkv_here, out_far, out_here, g_out, output, input_grad
    )

    out_far = links.sum_x(g_out, 0, 1, True, out_far).astype(BF)
    out_there = links.send_h(out_far, 1, "g_out")
    output = links.at_home(output, links.leave_group(output, "output"))
    input_grad = links.at_home(input_grad, links.leave_group(input_grad, "input_grad")).astype(F32)

    def total(here, there):
        return here + sum(v.astype(F32) for v in there)

    g_down = total(down_here, joined((down_one, down_two)))
    up_here = links.sum_x(g_up, 0, 1, False, up_here)
    g_up = total(up_here, joined((up_one, up_two)))
    g_qkv = total(links.sum_x(g_qkv, 0, 1, False, qkv_here), qkv_there)
    g_qkv = jnp.stack([g_qkv[:, i * block : (i + 1) * block] for i in range(3)])
    g_out = total(links.sum_x(g_out, 0, 1, False, out_here), out_there)
    (g_out,) = sync(g_out)
    g_out = g_out.T
    squares = (
        jnp.sum(g_qkv * g_qkv)
        + jnp.sum(g_out * g_out)
        + jnp.sum(g_up * g_up)
        + jnp.sum(g_down * g_down)
    )
    grad_norm = jnp.sqrt(links.total(squares))
    factor = jnp.minimum(1.0, clip_limit / (grad_norm + 1e-06))
    one_qkv, two_qkv, new_qkv = (
        v.transpose(1, 0, 2)
        for v in adam_update(
            g_qkv, *(v.transpose(1, 0, 2) for v in (m_qkv, v_qkv, w_qkv)), factor, learn_rate
        )
    )
    one_out, two_out, new_out = adam_update(g_out, m_out, v_out, w_out, factor, output_rate)
    one_up, two_up, new_up = adam_update(g_up, m_up, v_up, w_up, factor, learn_rate)
    one_down, two_down, new_down = adam_update(g_down, m_down, v_down, w_down, factor, learn_rate)
    return (
        output,
        input_grad,
        grad_norm,
        one_qkv,
        one_out,
        one_up,
        one_down,
        two_qkv,
        two_out,
        two_up,
        two_down,
        new_qkv,
        new_out,
        new_up,
        new_down,
    )


def solution(mesh):
    n_dp, n_mp = mesh.shape["dp"], mesh.shape["mp"]
    links = Links(n_dp, n_mp)
    fine = Mesh(mesh.devices.reshape(links.X, 2, links.H, 2, 2), ("x", "core", "h", "p", "q"))
    dp, mp = ("x", "core"), ("h", "p", "q")
    tokens, qkv = P(dp, mp, None), P(dp, None, mp)
    rows, columns = P(mp, dp), P(dp, mp)
    weights = (qkv, rows, columns, rows)
    return jax.shard_map(
        lambda *args: per_device(links, *args),
        mesh=fine,
        in_specs=(tokens, tokens, P(), P(dp), P(dp), P(dp)) + 3 * weights,
        out_specs=(tokens, tokens, P()) + 3 * weights,
        check_vma=False,
    )
```

time: 904 us -> 808 us (0.89)
  matrix products: 202 us -> 0.63 us
  Pallas kernels: 0 us -> 162 us
  waiting for transfers between devices: 459 us -> 417 us
  local copies, waits for them, and re-layouts: 67.6 us -> 46.8 us
    dot_general x18 -> x0, matrix products: 201 us -> none  [the longest x12 193 us: matmul(): lax.dot_general(a, b, (contract, ((), ())), preferred_element_type=F32)]
    pallas_call x0 -> x13, Pallas kernels: none -> 162 us  [the longest x4 107 us: group_call(): pl.pallas_call(lambda *refs: kernel(nh, nd, len(gates), *refs), name=name...]
    ppermute x89 -> x78, waiting for transfers between devices: 459 us -> 417 us  [the longest x73 410 us: shifted(): lax.ppermute(v, axis, [((dst + offset) % size, dst) for dst in range(size)])]
    slice x34 -> x20, local copies, waits for them, and re-layouts: 22.6 us -> 8.39 us  [the longest x7 2.51 us: part(): lax.slice_in_dim(g, width if far else 0, g.shape[h] if far else width, ax...]
    unnamed x216 -> x208, local copies, waits for them, and re-layouts: 20.2 us -> 31.6 us
    reshape x3 -> x0, local copies, waits for them, and re-layouts: 9.11 us -> none  [the longest x1 6.4 us: per_device(): qkv = qkv.reshape(images, length, H, 3, block)]
    ppermute x89 -> x78, starting transfers between devices: 81.2 us -> 86.8 us  [the longest x73 77.6 us: shifted(): lax.ppermute(v, axis, [((dst + offset) % size, dst) for dst in range(size)])]
    convert_element_type x27 -> x26, other arithmetic: 34.3 us -> 33.3 us  [the longest x4 15 us: add_core(): return (keep.astype(F32) + sent.astype(F32)).astype(BF)]
  transfers between devices with their start and end apart: 89 -> 78, of which waited for: 44 -> 39; matrix products, arithmetic and copies ran while one was open for 29% -> 10% of each run, Pallas kernels for 0% -> 12%
where the time goes in v2:
time: 808 us; the launch traced here: 801 us
  waiting for transfers between devices  417 us (52%)
  Pallas kernels  162 us (20%)
  starting transfers between devices  86.8 us (11%)
  other arithmetic  77.9 us (10%)
  local copies, waits for them, and re-layouts  46.8 us (6%)
  between operations  10.4 us (1%)
    ppermute x73, waiting for transfers between devices, shifted(): lax.ppermute(v, axis, [((dst + offset) % size, dst) for dst in range(size)])  410 us
    pallas_call x4, Pallas kernels, group_call(): pl.pallas_call(lambda *refs: kernel(nh, nd, len(gates), *refs), name=name...  107 us
    ppermute x73, starting transfers between devices, shifted(): lax.ppermute(v, axis, [((dst + offset) % size, dst) for dst in range(size)])  77.6 us
    pallas_call x8, Pallas kernels, gradient(): pl.pallas_call(kernel, name=name, grid=(nh, half), in_specs=in_specs, out...  54.2 us
    unnamed x208, local copies, waits for them, and re-layouts  31.6 us
  transfers between devices with their start and end apart: 78, of which 39 were waited for; matrix products, arithmetic and copies ran while one was open for 10% of the time, Pallas kernels for 12%

profile of v2, /device:TPU:0, one launch (start us, length us, event | category | flops | bytes accessed | tf_op | source)
XLA Modules:
  0.0 800.8 jit_solution(12336988279932687142)
XLA Ops:
  14.0 19.3 %collective-permute-done = bf16[4,32,2048]{2,1,0:T(8,128)(2,1)} collective-permute-done((bf16[4,32,2048]{2,1,0:T(8,128)(2,1)}, bf16[4,32,2048]{2,1,0:T(8,128)(2,1)}, u32[]{:S(2)}, u32[]{:S(2)}) %collective-permute-start) | collective-permute-done | bytes 524320 | tf_op jit(solution)/shard_map/stream_h/ppermute | solution.py:297
  57.6 23.3 %collective-permute-done.4 = bf16[256,1024]{1,0:T(8,128)(2,1)S(1)} collective-permute-done((bf16[256,1024]{1,0:T(8,128)(2,1)S(1)}, bf16[256,1024]{1,0:T(8,128)(2,1)S(1)}, u32[]{:S(2)}, u32[]{:S(2)}) %collective-permute-start.4) | collective-permute-done | bytes 524320 | tf_op jit(solution)/shard_map/wqoA_h/ppermute | solution.py:297
  87.8 30.9 %collective-permute-done.9 = bf16[256,1024]{1,0:T(8,128)(2,1)S(1)} collective-permute-done((bf16[256,1024]{1,0:T(8,128)(2,1)S(1)}, bf16[256,1024]{1,0:T(8,128)(2,1)S(1)}, u32[]{:S(2)}, u32[]{:S(2)}) %collective-permute-start.9) | collective-permute-done | bytes 524320 | tf_op jit(solution)/shard_map/wqoB_h/ppermute | solution.py:297
  125.9 24.0 %collective-permute-done.12 = bf16[4,32,2048]{2,1,0:T(8,128)(2,1)S(1)} collective-permute-done((bf16[4,32,2048]{2,1,0:T(8,128)(2,1)S(1)}, bf16[4,32,2048]{2,1,0:T(8,128)(2,1)S(1)}, u32[]{:S(2)}, u32[]{:S(2)}) %collective-permute-start.12) | collective-permute-done | bytes 524320 | tf_op jit(solution)/shard_map/cot_h/ppermute | solution.py:297
  153.3 13.2 %collective-permute-done.16 = bf16[2,64,2048]{2,1,0:T(8,128)(2,1)S(1)} collective-permute-done((bf16[2,64,2048]{2,1,0:T(8,128)(2,1)S(1)}, bf16[2,64,2048]{2,1,0:T(8,128)(2,1)S(1)}, u32[]{:S(2)}, u32[]{:S(2)}) %collective-permute-start.16) | collective-permute-done | bytes 524320 | tf_op jit(solution)/shard_map/df1_q/ppermute | solution.py:297
  173.3 23.7 %attention.1 = (bf16[2,2,256,2048]{3,2,1,0:T(8,128)(2,1)}, bf16[2,2,256,1536]{3,2,1,0:T(8,128)(2,1)}, bf16[2,2,256,512]{3,2,1,0:T(8,128)(2,1)}, bf16[2,128,2048]...) custom-call(bf16[2,128,2048]{2,1,0:T(8,128)(2,1)} %copy-done.47, ...), custom_call_target="tpu_custom_call" | custom-call | tf_op jit(solution)/shard_map/attention/pallas_call | solution.py:230
  209.9 29.3 %collective-permute-done.23 = bf16[256,1024]{1,0:T(8,128)(2,1)S(1)} collective-permute-done((bf16[256,1024]{1,0:T(8,128)(2,1)}, bf16[256,1024]{1,0:T(8,128)(2,1)S(1)}, u32[]{:S(2)}, u32[]{:S(2)}) %collective-permute-start.23) | collective-permute-done | bytes 524320 | tf_op jit(solution)/shard_map/wuB_h/ppermute | solution.py:297
  244.6 18.5 %collective-permute-done.24 = bf16[2,64,2048]{2,1,0:T(8,128)(2,1)S(1)} collective-permute-done((bf16[2,64,2048]{2,1,0:T(8,128)(2,1)S(1)}, bf16[2,64,2048]{2,1,0:T(8,128)(2,1)S(1)}, u32[]{:S(2)}, u32[]{:S(2)}) %collective-permute-start.24) | collective-permute-done | bytes 524320 | tf_op jit(solution)/shard_map/att0_p/ppermute | solution.py:297
  271.2 9.9 %collective-permute-done.30 = bf16[2,64,2048]{2,1,0:T(8,128)(2,1)S(1)} collective-permute-done((bf16[2,64,2048]{2,1,0:T(8,128)(2,1)S(1)}, bf16[2,64,2048]{2,1,0:T(8,128)(2,1)S(1)}, u32[]{:S(2)}, u32[]{:S(2)}) %collective-permute-start.30) | collective-permute-done | bytes 524320 | tf_op jit(solution)/shard_map/b1_q/ppermute | solution.py:297
  281.3 12.1 %collective-permute-done.29 = bf16[2,64,2048]{2,1,0:T(8,128)(2,1)S(1)} collective-permute-done((bf16[2,64,2048]{2,1,0:T(8,128)(2,1)S(1)}, bf16[2,64,2048]{2,1,0:T(8,128)(2,1)S(1)}, u32[]{:S(2)}, u32[]{:S(2)}) %collective-permute-start.29) | collective-permute-done | bytes 524320 | tf_op jit(solution)/shard_map/b0_p/ppermute | solution.py:297
  294.7 12.0 %collective-permute-done.32 = bf16[512,512]{1,0:T(8,128)(2,1)S(1)} collective-permute-done((bf16[512,512]{1,0:T(8,128)(2,1)S(1)}, bf16[512,512]{1,0:T(8,128)(2,1)S(1)}, u32[]{:S(2)}, u32[]{:S(2)}) %collective-permute-start.32) | collective-permute-done | bytes 524320 | tf_op jit(solution)/shard_map/wdA1_x/ppermute | solution.py:297
  308.0 11.0 %collective-permute-done.35 = bf16[512,512]{1,0:T(8,128)(2,1)S(1)} collective-permute-done((bf16[512,512]{1,0:T(8,128)(2,1)S(1)}, bf16[512,512]{1,0:T(8,128)(2,1)S(1)}, u32[]{:S(2)}, u32[]{:S(2)}) %collective-permute-start.35) | collective-permute-done | bytes 524320 | tf_op jit(solution)/shard_map/wdB1_x/ppermute | solution.py:297
  321.0 25.2 %collective-permute-done.33.refs_1_ = bf16[2,128,2048]{2,1,0:T(8,128)(2,1)S(1)} collective-permute-done((bf16[2,128,2048]{2,1,0:T(8,128)(2,1)S(1)}, bf16[2,128,2048]{2,1,0:T(8,128)(2,1)S(1)}, u32[]{:S(2)}, u32[]{:S(2)}) %collective-permute-start.33) | collective-permute-done | bytes 1048608 | tf_op jit(solution)/shard_map/b0_q/ppermute | solution.py:297
  348.2 39.9 %mlp.1 = (bf16[2,2,256,2048]{3,2,1,0:T(8,128)(2,1)}, bf16[2,2,256,2048]{3,2,1,0:T(8,128)(2,1)}, bf16[2,2,256,2048]{3,2,1,0:T(8,128)(2,1)}, bf16[2,2,256,2048]{3,...) custom-call(bf16[2,128,2048]{2,1,0:T(8,128)(2,1)} %copy-done.49, ...), custom_call_target="tpu_custom_call" | custom-call | tf_op jit(solution)/shard_map/mlp/pallas_call | solution.py:230
  405.2 16.9 %collective-permute-done.37 = bf16[2,128,2048]{2,1,0:T(8,128)(2,1)} collective-permute-done((bf16[2,128,2048]{2,1,0:T(8,128)(2,1)}, bf16[2,128,2048]{2,1,0:T(8,128)(2,1)}, u32[]{:S(2)}, u32[]{:S(2)}) %collective-permute-start.37) | collective-permute-done | bytes 1048608 | tf_op jit(solution)/shard_map/db0_q/ppermute | solution.py:297
  424.9 8.1 %g_up_send.1 = bf16[1024,2048]{1,0:T(8,128)(2,1)S(1)} custom-call(bf16[1024,2048]{1,0:T(8,128)(2,1)} %bitcast.93, bf16[1024,2048]{1,0:T(8,128)(2,1)} %bitcast.95), custom_call_target="tpu_custom_call" | custom-call | tf_op jit(solution)/shard_map/g_up_send/pallas_call | solution.py:276
  442.9 8.1 %g_up_keep.1 = bf16[1024,2048]{1,0:T(8,128)(2,1)S(1)} custom-call(bf16[1024,2048]{1,0:T(8,128)(2,1)} %bitcast.94, bf16[1024,2048]{1,0:T(8,128)(2,1)} %bitcast.96), custom_call_target="tpu_custom_call" | custom-call | tf_op jit(solution)/shard_map/g_up_keep/pallas_call | solution.py:276
  456.6 19.5 %collective-permute-done.42 = bf16[1024,512]{1,0:T(8,128)(2,1)S(1)} collective-permute-done((bf16[1024,512]{1,0:T(8,128)(2,1)S(1)}, bf16[1024,512]{1,0:T(8,128)(2,1)S(1)}, u32[]{:S(2)}, u32[]{:S(2)}) %collective-permute-start.42) | collective-permute-done | bytes 1048608 | tf_op jit(solution)/shard_map/g_downA_x/ppermute | solution.py:297
  490.1 14.7 %down.1 = (bf16[2,128,2048]{2,1,0:T(8,128)(2,1)}, bf16[2,128,2048]{2,1,0:T(8,128)(2,1)}, bf16[2,128,2048]{2,1,0:T(8,128)(2,1)}, bf16[2,128,2048]{2,1,0:T(8,128)(2,1)}) custom-call(bf16[2,2,256,2048]{3,2,1,0:T(8,128)(2,1)} %get-tuple-element.276.refs_0_, bf16[2,1024,512]{2,1,0:T(8,128)(2,1)} %copy-done.16, bf16[2,1024,512]{2,1,0:T(8,128)(2,1)} %copy-done.26, ...), custom_call_target="tpu_custom_call" | custom-call | tf_op jit(solution)/shard_map/down/pallas_call | solution.py:230
  513.3 29.9 %collective-permute-done.50 = bf16[512,512]{1,0:T(8,128)(2,1)S(1)} collective-permute-done((bf16[512,512]{1,0:T(8,128)(2,1)S(1)}, bf16[512,512]{1,0:T(8,128)(2,1)S(1)}, u32[]{:S(2)}, u32[]{:S(2)}) %collective-permute-start.50) | collective-permute-done | bytes 524320 | tf_op jit(solution)/shard_map/g_downB_h/ppermute | solution.py:297
  553.1 29.0 %attention_back.1 = (bf16[2,2,256,2048]{3,2,1,0:T(8,128)(2,1)}, bf16[2,2,256,1536]{3,2,1,0:T(8,128)(2,1)}, bf16[2,128,2048]{2,1,0:T(8,128)(2,1)}, bf16[2,128,204...) custom-call(bf16[2,128,2048]{2,1,0:T(8,128)(2,1)} %copy-done.55, ...), custom_call_target="tpu_custom_call" | custom-call | tf_op jit(solution)/shard_map/attention_back/pallas_call | solution.py:230
  621.4 24.0 %collective-permute-done.56 = bf16[256,1024]{1,0:T(8,128)(2,1)S(1)} collective-permute-done((bf16[256,1024]{1,0:T(8,128)(2,1)S(1)}, bf16[256,1024]{1,0:T(8,128)(2,1)S(1)}, u32[]{:S(2)}, u32[]{:S(2)}) %collective-permute-start.56) | collective-permute-done | bytes 524320 | tf_op jit(solution)/shard_map/g_upB_h/ppermute | solution.py:297
  686.1 21.8 %collective-permute-done.68 = bf16[512,256]{1,0:T(8,128)(2,1)S(1)} collective-permute-done((bf16[512,256]{1,0:T(8,128)(2,1)S(1)}, bf16[512,256]{1,0:T(8,128)(2,1)S(1)}, u32[]{:S(2)}, u32[]{:S(2)}) %collective-permute-start.68) | collective-permute-done | bytes 262176 | tf_op jit(solution)/shard_map/g_outA_x/ppermute | solution.py:297
  725.3 26.1 %collective-permute-done.72 = bf16[512,256]{1,0:T(8,128)(2,1)S(1)} collective-permute-done((bf16[512,256]{1,0:T(8,128)(2,1)S(1)}, bf16[512,256]{1,0:T(8,128)(2,1)S(1)}, u32[]{:S(2)}, u32[]{:S(2)}) %collective-permute-start.72) | collective-permute-done | bytes 262176 | tf_op jit(solution)/shard_map/g_out_h/ppermute | solution.py:297
  (471 shorter events, 300.1 us)
Async XLA Ops:
  82.4 39.6 %collective-permute-start.13 = (bf16[2,512,1024]{2,1,0:T(8,128)(2,1)S(1)}, bf16[2,512,1024]{2,1,0:T(8,128)(2,1)S(1)}, u32[]{:S(2)}, u32[]{:S(2)}) collective-permute-start(bf16[2,512,1024]{2,1,0:T(8,128)(2,1)S(1)} %pad_maximum_fusion.2.refs_8_), channel_id=1, source_target_pairs={{8,0},{0,8},{9,1},{1,9},{10,2},{2,10},{11,3},{3,11},{12,4},{4,12},... | collective-permute-start | bytes 6291464 | tf_op jit(solution)/shard_map/wu0_core/ppermute | solution.py:297
  82.5 36.1 %collective-permute-start.10 = (bf16[1024,512]{1,0:T(8,128)(2,1)S(1)}, bf16[1024,512]{1,0:T(8,128)(2,1)S(1)}, u32[]{:S(2)}, u32[]{:S(2)}) collective-permute-start(bf16[1024,512]{1,0:T(8,128)(2,1)S(1)} %convert_element_type.296), channel_id=1, source_target_pairs={{16,0},{0,16},{17,1},{1,17},{18,2},{2,18},{19,3},{3,19},{20,4},{4,... | collective-permute-start | bytes 3145736 | tf_op jit(solution)/shard_map/wd0_x/ppermute | solution.py:297
  83.1 35.5 %collective-permute-start.7 = (bf16[2,128,2048]{2,1,0:T(8,128)(2,1)S(1)}, bf16[2,128,2048]{2,1,0:T(8,128)(2,1)S(1)}, u32[]{:S(2)}, u32[]{:S(2)}) collective-permute-start(bf16[2,128,2048]{2,1,0:T(8,128)(2,1)S(1)} %pad_maximum_fusion.9.refs_0_), channel_id=1, source_target_pairs={{1,0},{0,1},{3,2},{2,3},{5,4},{4,5},{7,6},{6,7},{9,8},{8,9},{11,10... | collective-permute-start | bytes 3145736 | tf_op jit(solution)/shard_map/a0_q/ppermute | solution.py:297
  84.6 36.2 %collective-permute-start.8 = (bf16[2,128,2048]{2,1,0:T(8,128)(2,1)S(1)}, bf16[2,128,2048]{2,1,0:T(8,128)(2,1)S(1)}, u32[]{:S(2)}, u32[]{:S(2)}) collective-permute-start(bf16[2,128,2048]{2,1,0:T(8,128)(2,1)S(1)} %pad_maximum_fusion.10.refs_2_), channel_id=1, source_target_pairs={{2,0},{0,2},{3,1},{1,3},{6,4},{4,6},{7,5},{5,7},{10,8},{8,10},{11,... | collective-permute-start | bytes 3145736 | tf_op jit(solution)/shard_map/a1_p/ppermute | solution.py:297
  84.6 34.0 %collective-permute-start.9 = (bf16[256,1024]{1,0:T(8,128)(2,1)S(1)}, bf16[256,1024]{1,0:T(8,128)(2,1)S(1)}, u32[]{:S(2)}, u32[]{:S(2)}) collective-permute-start(bf16[256,1024]{1,0:T(8,128)(2,1)S(1)} %get-tuple-element.192), channel_id=1, source_target_pairs={{4,0},{0,4},{5,1},{1,5},{6,2},{2,6},{7,3},{3,7},{12,8},{8,12},{13,... | collective-permute-start | bytes 1572872 | tf_op jit(solution)/shard_map/wqoB_h/ppermute | solution.py:297
  168.6 33.8 %collective-permute-start.18 = (bf16[2,128,2048]{2,1,0:T(8,128)(2,1)}, bf16[2,128,2048]{2,1,0:T(8,128)(2,1)S(1)}, u32[]{:S(2)}, u32[]{:S(2)}) collective-permute-start(bf16[2,128,2048]{2,1,0:T(8,128)(2,1)} %pad_maximum_fusion.13.refs_4_), channel_id=1, source_target_pairs={{1,0},{0,1},{3,2},{2,3},{5,4},{4,5},{7,6},{6,7},{9,8},{8,9},{11,10... | collective-permute-start | bytes 3145736 | tf_op jit(solution)/shard_map/df0_q/ppermute | solution.py:297
  169.3 35.1 %collective-permute-start.19 = (bf16[2,128,2048]{2,1,0:T(8,128)(2,1)}, bf16[2,128,2048]{2,1,0:T(8,128)(2,1)S(1)}, u32[]{:S(2)}, u32[]{:S(2)}) collective-permute-start(bf16[2,128,2048]{2,1,0:T(8,128)(2,1)} %pad_maximum_fusion.14.refs_6_), channel_id=1, source_target_pairs={{2,0},{0,2},{3,1},{1,3},{6,4},{4,6},{7,5},{5,7},{10,8},{8,10},{11,... | collective-permute-start | bytes 3145736 | tf_op jit(solution)/shard_map/df1_p/ppermute | solution.py:297
  204.4 34.8 %collective-permute-start.21 = (bf16[2,128,2048]{2,1,0:T(8,128)(2,1)}, bf16[2,128,2048]{2,1,0:T(8,128)(2,1)S(1)}, u32[]{:S(2)}, u32[]{:S(2)}) collective-permute-start(bf16[2,128,2048]{2,1,0:T(8,128)(2,1)} %get-tuple-element.222), channel_id=1, source_target_pairs={{1,0},{0,1},{3,2},{2,3},{5,4},{4,5},{7,6},{6,7},{9,8},{8,9},{11,10... | collective-permute-start | bytes 3145736 | tf_op jit(solution)/shard_map/att0_q/ppermute | solution.py:297
  206.0 34.2 %collective-permute-start.22 = (bf16[2,128,2048]{2,1,0:T(8,128)(2,1)}, bf16[2,128,2048]{2,1,0:T(8,128)(2,1)S(1)}, u32[]{:S(2)}, u32[]{:S(2)}) collective-permute-start(bf16[2,128,2048]{2,1,0:T(8,128)(2,1)} %get-tuple-element.223), channel_id=1, source_target_pairs={{2,0},{0,2},{3,1},{1,3},{6,4},{4,6},{7,5},{5,7},{10,8},{8,10},{11,... | collective-permute-start | bytes 3145736 | tf_op jit(solution)/shard_map/att1_p/ppermute | solution.py:297
  433.0 43.2 %collective-permute-start.43 = (bf16[1024,2048]{1,0:T(8,128)(2,1)S(1)}, bf16[1024,2048]{1,0:T(8,128)(2,1)}, u32[]{:S(2)}, u32[]{:S(2)}) collective-permute-start(bf16[1024,2048]{1,0:T(8,128)(2,1)S(1)} %g_up_send.1), channel_id=1, source_target_pairs={{8,0},{0,8},{9,1},{1,9},{10,2},{2,10},{11,3},{3,11},{12,4},{4,12},... | collective-permute-start | bytes 12582920 | tf_op jit(solution)/shard_map/g_up_core/ppermute | solution.py:297
  508.2 35.0 %collective-permute-start.51 = (bf16[512,1024]{1,0:T(8,128)(2,1)S(1)}, bf16[512,1024]{1,0:T(8,128)(2,1)S(1)}, u32[]{:S(2)}, u32[]{:S(2)}) collective-permute-start(bf16[512,1024]{1,0:T(8,128)(2,1)S(1)} %slice.310), channel_id=1, source_target_pairs={{16,0},{0,16},{17,1},{1,17},{18,2},{2,18},{19,3},{3,19},{20,4},{4,... | collective-permute-start | bytes 3145736 | tf_op jit(solution)/shard_map/g_upA_x/ppermute | solution.py:297
  509.0 34.2 %collective-permute-start.48 = (bf16[2,128,2048]{2,1,0:T(8,128)(2,1)S(1)}, bf16[2,128,2048]{2,1,0:T(8,128)(2,1)S(1)}, u32[]{:S(2)}, u32[]{:S(2)}) collective-permute-start(bf16[2,128,2048]{2,1,0:T(8,128)(2,1)S(1)} %pad_maximum_fusion.17.refs_0_), channel_id=1, source_target_pairs={{1,0},{0,1},{3,2},{2,3},{5,4},{4,5},{7,6},{6,7},{9,8},{8,9},{11,10... | collective-permute-start | bytes 3145736 | tf_op jit(solution)/shard_map/datt0_q/ppermute | solution.py:297
  510.2 34.1 %collective-permute-start.49 = (bf16[2,128,2048]{2,1,0:T(8,128)(2,1)S(1)}, bf16[2,128,2048]{2,1,0:T(8,128)(2,1)}, u32[]{:S(2)}, u32[]{:S(2)}) collective-permute-start(bf16[2,128,2048]{2,1,0:T(8,128)(2,1)S(1)} %pad_maximum_fusion.18.refs_2_), channel_id=1, source_target_pairs={{2,0},{0,2},{3,1},{1,3},{6,4},{4,6},{7,5},{5,7},{10,8},{8,10},{11,... | collective-permute-start | bytes 3145736 | tf_op jit(solution)/shard_map/datt1_p/ppermute | solution.py:297
  545.4 36.7 %collective-permute-start.53 = (bf16[512,1024]{1,0:T(8,128)(2,1)}, bf16[512,1024]{1,0:T(8,128)(2,1)S(1)}, u32[]{:S(2)}, u32[]{:S(2)}) collective-permute-start(bf16[512,1024]{1,0:T(8,128)(2,1)} %slice.313), channel_id=1, source_target_pairs={{16,0},{0,16},{17,1},{1,17},{18,2},{2,18},{19,3},{3,19},{20,4},{4,... | collective-permute-start | bytes 3145736 | tf_op jit(solution)/shard_map/g_upB_x/ppermute | solution.py:297
  546.6 35.5 %collective-permute-start.54 = (bf16[2,128,2048]{2,1,0:T(8,128)(2,1)}, bf16[2,128,2048]{2,1,0:T(8,128)(2,1)}, u32[]{:S(2)}, u32[]{:S(2)}) collective-permute-start(bf16[2,128,2048]{2,1,0:T(8,128)(2,1)} %get-tuple-element.293), channel_id=1, source_target_pairs={{1,0},{0,1},{3,2},{2,3},{5,4},{4,5},{7,6},{6,7},{9,8},{8,9},{11,10... | collective-permute-start | bytes 3145736 | tf_op jit(solution)/shard_map/ff0_q/ppermute | solution.py:297
  547.5 34.6 %collective-permute-start.55 = (bf16[2,128,2048]{2,1,0:T(8,128)(2,1)}, bf16[2,128,2048]{2,1,0:T(8,128)(2,1)S(1)}, u32[]{:S(2)}, u32[]{:S(2)}) collective-permute-start(bf16[2,128,2048]{2,1,0:T(8,128)(2,1)} %get-tuple-element.294), channel_id=1, source_target_pairs={{2,0},{0,2},{3,1},{1,3},{6,4},{4,6},{7,5},{5,7},{10,8},{8,10},{11,... | collective-permute-start | bytes 3145736 | tf_op jit(solution)/shard_map/ff1_p/ppermute | solution.py:297
  590.5 59.2 %collective-permute-start.59 = (bf16[1024,1536]{1,0:T(8,128)(2,1)S(1)}, bf16[1024,1536]{1,0:T(8,128)(2,1)}, u32[]{:S(2)}, u32[]{:S(2)}) collective-permute-start(bf16[1024,1536]{1,0:T(8,128)(2,1)S(1)} %g_qkv_send.1), channel_id=1, source_target_pairs={{8,0},{0,8},{9,1},{1,9},{10,2},{2,10},{11,3},{3,11},{12,4},{4,12},... | collective-permute-start | bytes 9437192 | tf_op jit(solution)/shard_map/g_qkv_core/ppermute | solution.py:297
  607.9 38.4 %collective-permute-start.60 = (bf16[1024,512]{1,0:T(8,128)(2,1)S(1)}, bf16[1024,512]{1,0:T(8,128)(2,1)}, u32[]{:S(2)}, u32[]{:S(2)}) collective-permute-start(bf16[1024,512]{1,0:T(8,128)(2,1)S(1)} %g_out_send.1), channel_id=1, source_target_pairs={{8,0},{0,8},{9,1},{1,9},{10,2},{2,10},{11,3},{3,11},{12,4},{4,12},... | collective-permute-start | bytes 3145736 | tf_op jit(solution)/shard_map/g_out_core/ppermute | solution.py:297
  608.5 41.2 %collective-permute-start.57 = (bf16[2,128,2048]{2,1,0:T(8,128)(2,1)}, bf16[2,128,2048]{2,1,0:T(8,128)(2,1)S(1)}, u32[]{:S(2)}, u32[]{:S(2)}) collective-permute-start(bf16[2,128,2048]{2,1,0:T(8,128)(2,1)} %get-tuple-element.305), channel_id=1, source_target_pairs={{1,0},{0,1},{3,2},{2,3},{5,4},{4,5},{7,6},{6,7},{9,8},{8,9},{11,10... | collective-permute-start | bytes 3145736 | tf_op jit(solution)/shard_map/da0_q/ppermute | solution.py:297
  609.6 40.0 %collective-permute-start.58 = (bf16[2,128,2048]{2,1,0:T(8,128)(2,1)}, bf16[2,128,2048]{2,1,0:T(8,128)(2,1)}, u32[]{:S(2)}, u32[]{:S(2)}) collective-permute-start(bf16[2,128,2048]{2,1,0:T(8,128)(2,1)} %get-tuple-element.306), channel_id=1, source_target_pairs={{2,0},{0,2},{3,1},{1,3},{6,4},{4,6},{7,5},{5,7},{10,8},{8,10},{11,... | collective-permute-start | bytes 3145736 | tf_op jit(solution)/shard_map/da1_p/ppermute | solution.py:297
  681.7 34.4 %collective-permute-start.66 = (bf16[512,768]{1,0:T(8,128)(2,1)S(1)}, bf16[512,768]{1,0:T(8,128)(2,1)S(1)}, u32[]{:S(2)}, u32[]{:S(2)}) collective-permute-start(bf16[512,768]{1,0:T(8,128)(2,1)S(1)} %add_convert_fusion.8), channel_id=1, source_target_pairs={{4,0},{0,4},{5,1},{1,5},{6,2},{2,6},{7,3},{3,7},{12,8},{8,12},{13,... | collective-permute-start | bytes 2359304 | tf_op jit(solution)/shard_map/g_qkv_h/ppermute | solution.py:297
  716.2 35.3 %collective-permute-start.72 = (bf16[512,256]{1,0:T(8,128)(2,1)S(1)}, bf16[512,256]{1,0:T(8,128)(2,1)S(1)}, u32[]{:S(2)}, u32[]{:S(2)}) collective-permute-start(bf16[512,256]{1,0:T(8,128)(2,1)S(1)} %add_convert_fusion.17), channel_id=1, source_target_pairs={{4,0},{0,4},{5,1},{1,5},{6,2},{2,6},{7,3},{3,7},{12,8},{8,12},{13,... | collective-permute-start | bytes 786440 | tf_op jit(solution)/shard_map/g_out_h/ppermute | solution.py:297
  718.2 76.1 %collective-permute-start.71 = (bf16[4,32,2048]{2,1,0:T(8,128)(2,1)}, bf16[4,32,2048]{2,1,0:T(8,128)(2,1)}, u32[]{:S(2)}, u32[]{:S(2)}) collective-permute-start(bf16[4,32,2048]{2,1,0:T(8,128)(2,1)} %get-tuple-element.398), channel_id=1, source_target_pairs={{4,0},{0,4},{5,1},{1,5},{6,2},{2,6},{7,3},{3,7},{12,8},{8,12},{13,... | collective-permute-start | bytes 1572872 | tf_op jit(solution)/shard_map/input_grad_h/ppermute | solution.py:297
  723.1 72.4 %collective-permute-start.70 = (bf16[4,32,2048]{2,1,0:T(8,128)(2,1)}, bf16[4,32,2048]{2,1,0:T(8,128)(2,1)}, u32[]{:S(2)}, u32[]{:S(2)}) collective-permute-start(bf16[4,32,2048]{2,1,0:T(8,128)(2,1)} %get-tuple-element.404), channel_id=1, source_target_pairs={{4,0},{0,4},{5,1},{1,5},{6,2},{2,6},{7,3},{3,7},{12,8},{8,12},{13,... | collective-permute-start | bytes 1572872 | tf_op jit(solution)/shard_map/output_h/ppermute | solution.py:297
  (154 other events, 2700.8 us)

commit v3 on v2

v3 whole, which is shorter than its diff:
```python
import jax
import jax.numpy as jnp
from jax import lax
from jax.experimental import pallas as pl
from jax.experimental.pallas import tpu as pltpu
from jax.sharding import Mesh
from jax.sharding import PartitionSpec as P

HD = 128
BINS = 8
ADAM_STEP = 10

clip_limit = 1.0
beta_one = 0.9
beta_two = 0.95
learn_rate = 0.02
output_rate = 0.08
adam_epsilon = 1e-08
decay_rate = 0.01

BF = jnp.bfloat16
F32 = jnp.float32


def adam_update(gradient, moment_one, moment_two, weight, factor, step_rate):
    clipped = gradient * factor
    new_one = beta_one * moment_one + (1.0 - beta_one) * clipped
    new_two = beta_two * moment_two + (1.0 - beta_two) * clipped * clipped
    corrected = new_one / (1.0 - beta_one**ADAM_STEP)
    root_two = jnp.sqrt(new_two / (1.0 - beta_two**ADAM_STEP))
    new_weight = weight - step_rate * (corrected / (root_two + adam_epsilon) + decay_rate * weight)
    return (new_one, new_two, new_weight)


def sync(*values):
    return lax.optimization_barrier(values)


def dot(a, b, contract=(1, 0)):
    return lax.dot_general(
        a, b, (((contract[0],), (contract[1],)), ((), ())), preferred_element_type=F32
    )


def rows_of(ref, columns=slice(None)):
    value = ref[0, :, :, columns]
    return value.reshape(value.shape[0] * value.shape[1], value.shape[2])


def join_tokens(pieces, whole):
    for kind, two in enumerate(pieces):
        for r, ref in enumerate(two):
            t = ref.shape[1]
            whole[0, kind, r * t : (r + 1) * t] = ref[0]


def put_parts(value, columns, parts):
    half = value.shape[0] // (2 * len(parts))
    for kind, (keep, send) in enumerate(parts):
        keep[0, :, columns] = value[2 * kind * half : (2 * kind + 1) * half]
        send[0, :, columns] = value[(2 * kind + 1) * half : (2 * kind + 2) * half]


def softmax_rows(q, k):
    scores = dot(q, k, (1, 1)) * HD ** (-0.5)
    weights = jnp.exp(scores - jnp.max(scores, axis=-1, keepdims=True))
    return weights * (1.0 / jnp.sum(weights, axis=-1, keepdims=True))


def head_columns(jh, part, n, block):
    start = (jh * 3 + part) * block + n * HD
    return slice(start, start + HD)


class Pieces:
    def __init__(self, refs):
        self.refs, self.at = refs, 0

    def take(self, count):
        self.at += count
        return self.refs[self.at - count : self.at]

    def tokens(self):
        near_far = self.take(4)
        return near_far[:2], near_far[2:]

    def parts(self):
        a, b, c, d = self.take(4)
        return (a, b), (c, d)


class Separate:
    def __init__(self, refs, nd):
        self.refs, self.depth = refs, refs[0].shape[0]
        self.shape = refs[0].shape[1:]

    def block(self, jh, d, rows=slice(None), columns=slice(None)):
        core, x = divmod(d, self.depth)
        return self.refs[2 * jh + core][x, rows, columns]


def attention_kernel(nh, nd, *refs):
    refs = Pieces(refs)
    tokens, weights = refs.tokens(), Separate(refs.take(2 * nh), nd)
    (a, qkv, o, probs), parts = refs.take(4), refs.parts()
    join_tokens(tokens, a)
    depth, block = weights.shape[0], weights.shape[1] // 4
    width = 3 * block
    inward = (slice(None), slice(0, width))
    outward = (slice(None), slice(width, width + block))
    kinds, length = a.shape[1], a.shape[2]
    for jh in range(nh):
        total = dot(rows_of(a, slice(0, depth)), weights.block(jh, 0, *inward))
        for d in range(1, nd):
            total += dot(rows_of(a, slice(d * depth, (d + 1) * depth)), weights.block(jh, d, *inward))
        qkv[0, :, :, jh * width : (jh + 1) * width] = total.astype(BF).reshape(kinds, length, width)
    for kind in range(kinds):
        for jh in range(nh):
            for n in range(block // HD):
                q, k, v = (qkv[0, kind, :, head_columns(jh, i, n, block)] for i in range(3))
                p = softmax_rows(q, k).astype(BF)
                probs[0, kind, jh * (block // HD) + n] = p
                out = dot(p, v).astype(BF)
                o[0, kind, :, jh * block + n * HD : jh * block + (n + 1) * HD] = out
    for d in range(nd):
        total = dot(rows_of(o, slice(0, block)), weights.block(0, d, *outward), (1, 1))
        for jh in range(1, nh):
            total += dot(rows_of(o, slice(jh * block, (jh + 1) * block)), weights.block(jh, d, *outward), (1, 1))
        put_parts(total.astype(BF), slice(d * depth, (d + 1) * depth), parts)


def up_kernel(nh, nd, *refs):
    refs = Pieces(refs)
    b_tokens, wu = refs.tokens(), Separate(refs.take(2 * nh), nd)
    b, hidden, slope = refs.take(3)
    join_tokens(b_tokens, b)
    depth, width = wu.shape
    kinds, length = b.shape[1], b.shape[2]
    chunk = min(width, 512)
    curve, cubic = 0.7978845608028654, 0.044715
    for jh in range(nh):
        for c in range(0, width, chunk):
            part = slice(c, c + chunk)
            u = dot(rows_of(b, slice(0, depth)), wu.block(jh, 0, columns=part))
            for d in range(1, nd):
                cols = slice(d * depth, (d + 1) * depth)
                u += dot(rows_of(b, cols), wu.block(jh, d, columns=part))
            square = u * u
            t = jnp.tanh(curve * u * (1.0 + cubic * square))
            near = 0.5 * (1.0 + t)
            rise = near + 0.5 * u * (1.0 - t * t) * (curve * (1.0 + 3.0 * cubic * square))
            cols = slice(jh * width + c, jh * width + c + chunk)
            hidden[0, :, :, cols] = (u * near).astype(BF).reshape(kinds, length, chunk)
            slope[0, :, :, cols] = rise.astype(BF).reshape(kinds, length, chunk)


def up_back_kernel(nh, nd, *refs):
    refs = Pieces(refs)
    df_tokens, (slope,) = refs.tokens(), refs.take(1)
    wu, wd = (Separate(refs.take(2 * nh), nd) for _ in range(2))
    (df, du), parts = refs.take(2), refs.parts()
    join_tokens(df_tokens, df)
    depth, width = wu.shape
    kinds, length = df.shape[1], df.shape[2]
    chunk = min(width, 512)
    for jh in range(nh):
        for c in range(0, width, chunk):
            part = slice(c, c + chunk)
            dh = dot(rows_of(df, slice(0, depth)), wd.block(jh, 0, part), (1, 1))
            for d in range(1, nd):
                cols = slice(d * depth, (d + 1) * depth)
                dh += dot(rows_of(df, cols), wd.block(jh, d, part), (1, 1))
            cols = slice(jh * width + c, jh * width + c + chunk)
            value = dh * rows_of(slope, cols).astype(F32)
            du[0, :, :, cols] = value.astype(BF).reshape(kinds, length, chunk)
    for d in range(nd):
        total = dot(rows_of(du, slice(0, width)), wu.block(0, d), (1, 1))
        for jh in range(1, nh):
            total += dot(rows_of(du, slice(jh * width, (jh + 1) * width)), wu.block(jh, d), (1, 1))
        put_parts(total.astype(BF), slice(d * depth, (d + 1) * depth), parts)


def down_kernel(nh, nd, *refs):
    refs = Pieces(refs)
    (hidden,), wd = refs.take(1), Separate(refs.take(2 * nh), nd)
    parts = refs.parts()
    width, depth = wd.shape
    for d in range(nd):
        total = dot(rows_of(hidden, slice(0, width)), wd.block(0, d))
        for jh in range(1, nh):
            total += dot(rows_of(hidden, slice(jh * width, (jh + 1) * width)), wd.block(jh, d))
        put_parts(total.astype(BF), slice(d * depth, (d + 1) * depth), parts)


def attention_back_kernel(nh, nd, *refs):
    refs = Pieces(refs)
    (a, o), tokens, (qkv, probs) = refs.take(2), refs.tokens(), refs.take(2)
    weights = Separate(refs.take(2 * nh), nd)
    parts, (all_datt, all_dqkv, sent) = refs.parts(), refs.take(3)
    step = pl.program_id(0)
    datt, dqkv = (v.at[pl.ds(step, 1)] for v in (all_datt, all_dqkv))
    join_tokens(tokens, datt)
    depth, block = weights.shape[0], weights.shape[1] // 4
    width = 3 * block
    inward = (slice(None), slice(0, width))
    outward = (slice(None), slice(width, width + block))
    kinds, length = datt.shape[1], datt.shape[2]
    for jh in range(nh):
        do_all = dot(rows_of(datt, slice(0, depth)), weights.block(jh, 0, *outward))
        for d in range(1, nd):
            do_all += dot(rows_of(datt, slice(d * depth, (d + 1) * depth)), weights.block(jh, d, *outward))
        do_all = do_all.astype(BF)
        for kind in range(kinds):
            for n in range(block // HD):
                q, k, v = (qkv[0, kind, :, head_columns(jh, i, n, block)] for i in range(3))
                do = do_all[kind * length : (kind + 1) * length, n * HD : (n + 1) * HD]
                rounded = probs[0, kind, jh * (block // HD) + n]
                dv = dot(rounded, do, (0, 0))
                dp = dot(do, v, (1, 1))
                p = rounded.astype(F32)
                ds = (p * (dp - jnp.sum(p * dp, axis=-1, keepdims=True))).astype(BF)
                dq = dot(ds, k) * HD ** (-0.5)
                dk = dot(ds, q, (0, 0)) * HD ** (-0.5)
                for i, value in enumerate((dq, dk, dv)):
                    dqkv[0, kind, :, head_columns(jh, i, n, block)] = value.astype(BF)
    for d in range(nd):
        total = dot(rows_of(dqkv, slice(0, width)), weights.block(0, d, *inward), (1, 1))
        for jh in range(1, nh):
            total += dot(rows_of(dqkv, slice(jh * width, (jh + 1) * width)), weights.block(jh, d, *inward), (1, 1))
        put_parts(total.astype(BF), slice(d * depth, (d + 1) * depth), parts)
    across, both = nd // 2, width + block

    def every_row(ref, columns=slice(None)):
        value = ref[:, :, :, columns]
        return value.reshape(-1, value.shape[-1])

    @pl.when(step == pl.num_programs(0) - 1)
    def _():
        for jx in range(across):
            cols = slice((across + jx) * depth, (across + jx + 1) * depth)
            inward = dot(a[cols], every_row(all_dqkv)).astype(BF)
            outward = dot(every_row(all_datt, cols), every_row(o), (0, 0)).astype(BF)
            rows = slice(jx * depth, (jx + 1) * depth)
            for jh in range(nh):
                at = jh * both
                sent[rows, at : at + width] = inward[:, jh * width : (jh + 1) * width]
                sent[rows, at + width : at + both] = outward[:, jh * block : (jh + 1) * block]


def group_call(kernel, name, nh, nd, steps, blocked, whole, outs, resident=(), whole_outs=()):
    def cut(shape):
        zeros = (0,) * (len(shape) - 1)
        return pl.BlockSpec((1,) + tuple(shape[1:]), lambda i: (i,) + zeros)

    def stay(shape):
        zeros = (0,) * len(shape)
        return pl.BlockSpec(tuple(shape), lambda i: zeros)

    return pl.pallas_call(
        lambda *refs: kernel(nh, nd, *refs),
        name=name,
        grid=(steps,),
        in_specs=[stay(v.shape) for v in resident]
        + [cut(v.shape) for v in blocked]
        + [pl.BlockSpec(memory_space=pltpu.VMEM)] * len(whole),
        out_specs=[cut(s) for s in outs] + [stay(s) for s in whole_outs],
        out_shape=[jax.ShapeDtypeStruct(s, BF) for s in (*outs, *whole_outs)],
        compiler_params=pltpu.CompilerParams(vmem_limit_bytes=62 * 2**20),
        cost_estimate=pl.CostEstimate(flops=0, bytes_accessed=0, transcendentals=0),
    )(*resident, *blocked, *whole)


def image_call(kernel, name, steps, arrays, outs):
    def seen(shape):
        return (2, steps, *shape[1:]) if shape[0] == 2 * steps else tuple(shape)

    def cut(shape):
        zeros = (0,) * (len(shape) - 2)
        if shape[0] == 2 and len(shape) == 4:
            return pl.BlockSpec((2, 1, *shape[2:]), lambda i: (0, i, *zeros))
        return pl.BlockSpec((1, *shape[1:]), lambda i: (i, 0, *zeros))

    made = pl.pallas_call(
        kernel,
        name=name,
        grid=(steps,),
        in_specs=[cut(seen(v.shape)) for v in arrays],
        out_specs=[cut(seen(shape)) for shape, _ in outs],
        out_shape=[jax.ShapeDtypeStruct(seen(shape), dtype) for shape, dtype in outs],
        compiler_params=pltpu.CompilerParams(vmem_limit_bytes=32 * 2**20),
        cost_estimate=pl.CostEstimate(flops=0, bytes_accessed=0, transcendentals=0),
    )(*[v.reshape(seen(v.shape)) for v in arrays])
    return [v.reshape(shape) for v, (shape, _) in zip(made, outs)]


def row_parts(values):
    center = values - jnp.mean(values, axis=-1, keepdims=True)
    factor = lax.rsqrt(jnp.mean(center * center, axis=-1, keepdims=True) + 1e-06)
    return center * factor, factor


def norm_back(values, gradient):
    rows, factor = row_parts(values)
    return factor * (
        gradient
        - jnp.mean(gradient, axis=-1, keepdims=True)
        - rows * jnp.mean(gradient * rows, axis=-1, keepdims=True)
    )


def token_sum(sums, kind):
    keep, got, last = sums[kind], sums[2 + kind], sums[4 + kind]
    t = last.shape[1]
    return keep[0, :t].astype(F32) + got[0, :t].astype(F32) + last[0].astype(F32)


def first_norm_kernel(stream, mod, *a):
    for kind in range(2):
        rows, _ = row_parts(stream[kind, 0].astype(F32))
        a[kind][0] = (rows * mod[kind, 0, 1:2] + mod[kind, 0, 0:1]).astype(BF)


def loss_kernel(cot, weight, mod, *df):
    for kind in range(2):
        seed = cot[kind, 0].astype(F32) * weight[kind, 0]
        df[kind][0] = (mod[kind, 0, 5:6] * seed).astype(BF)


def second_norm_kernel(stream, mod, *refs):
    sums, residual, b = refs[:6], refs[6], refs[7:]
    for kind in range(2):
        r = stream[kind, 0].astype(F32) + mod[kind, 0, 2:3] * token_sum(sums, kind)
        residual[kind, 0] = r
        rows, _ = row_parts(r)
        b[kind][0] = (rows * mod[kind, 0, 4:5] + mod[kind, 0, 3:4]).astype(BF)


def second_norm_back_kernel(cot, weight, residual, mod, *refs):
    sums, dr, datt = refs[:6], refs[6], refs[7:]
    for kind in range(2):
        seed = cot[kind, 0].astype(F32) * weight[kind, 0]
        g = seed + norm_back(residual[kind, 0], token_sum(sums, kind) * mod[kind, 0, 4:5])
        dr[kind, 0] = g
        datt[kind][0] = (mod[kind, 0, 2:3] * g).astype(BF)


def first_norm_back_kernel(stream, dr, mod, *refs):
    sums, out = refs[:6], refs[6]
    for kind in range(2):
        g = norm_back(stream[kind, 0].astype(F32), token_sum(sums, kind) * mod[kind, 0, 1:2])
        out[kind, 0] = (dr[kind, 0] + g).astype(BF)


def output_kernel(residual, mod, *refs):
    sums, out = refs[:6], refs[6]
    for kind in range(2):
        out[kind, 0] = (residual[kind, 0] + mod[kind, 0, 5:6] * token_sum(sums, kind)).astype(BF)


def pack_attention_weights(w_qkv, w_out):
    depth, _, block = w_qkv.shape

    def kernel(inward, outward, packed):
        for i in range(3):
            packed[:, i * block : (i + 1) * block] = inward[i].astype(BF)
        packed[:, 3 * block :] = outward[...].T.astype(BF)

    return pl.pallas_call(
        kernel,
        name="pack",
        out_shape=jax.ShapeDtypeStruct((depth, 4 * block), BF),
        compiler_params=pltpu.CompilerParams(vmem_limit_bytes=32 * 2**20),
    )(w_qkv.transpose(1, 0, 2), w_out)


def gradient(name, nh, nd, left, right, left_is_hidden, core):
    rows = left.shape[0]
    hidden, features = (left, right) if left_is_hidden else (right, left)
    h_width, d_width, half = hidden.shape[1] // nh, features.shape[1] // nd, nd // 2

    def kernel(left, right, out):
        out[...] = dot(left[...], right[...], (0, 0)).astype(BF)

    h_spec = pl.BlockSpec((rows, h_width), lambda jh, d: (0, jh))
    d_spec = pl.BlockSpec((rows, d_width), lambda jh, d: (0, core * half + d))
    if left_is_hidden:
        in_specs, out_spec = [h_spec, d_spec], pl.BlockSpec((h_width, d_width), lambda jh, d: (jh, d))
        shape = (nh * h_width, half * d_width)
    else:
        in_specs, out_spec = [d_spec, h_spec], pl.BlockSpec((d_width, h_width), lambda jh, d: (d, jh))
        shape = (half * d_width, nh * h_width)
    return pl.pallas_call(
        kernel,
        name=name,
        grid=(nh, half),
        in_specs=in_specs,
        out_specs=out_spec,
        out_shape=jax.ShapeDtypeStruct(shape, BF),
        compiler_params=pltpu.CompilerParams(vmem_limit_bytes=48 * 2**20),
        cost_estimate=pl.CostEstimate(flops=0, bytes_accessed=0, transcendentals=0),
    )(left, right)


def one_step(kernel, name, arrays, columns, outs, dtype=BF):
    return pl.pallas_call(
        kernel,
        name=name,
        grid=(1,),
        in_specs=[
            pl.BlockSpec((v.shape[0], c or v.shape[1]), lambda i: (0, 0))
            for v, c in zip(arrays, columns)
        ],
        out_specs=[pl.BlockSpec(shape, lambda i: (0, 0)) for shape in outs],
        out_shape=[jax.ShapeDtypeStruct(shape, dtype) for shape in outs],
        compiler_params=pltpu.CompilerParams(vmem_limit_bytes=60 * 2**20),
        cost_estimate=pl.CostEstimate(flops=0, bytes_accessed=0, transcendentals=0),
    )(*arrays)


def down_kept(nh, nd, hidden, df, sent):
    half = nd // 2
    height, width = hidden.shape[1] // nh, df.shape[1] // nd
    cut = height // 2

    def kernel(hidden, df, sent, *outs):
        for jx in range(half):
            one, two, three = outs[3 * jx : 3 * jx + 3]
            cols = slice(jx * width, (jx + 1) * width)
            for jh in range(nh):
                rows = slice(jh * height, (jh + 1) * height)
                g = dot(hidden[:, rows], df[:, cols], (0, 0)) + sent[rows, cols].astype(F32)
                g = g.astype(BF)
                if jh:
                    one[(jh - 1) * cut : jh * cut] = g[:cut]
                    two[(jh - 1) * cut : jh * cut] = g[cut:]
                else:
                    two[(nh - 1) * cut :] = g[:cut]
                    three[...] = g[cut:]

    shapes = [((nh - 1) * cut, width), (nh * cut, width), (cut, width)] * half
    return one_step(kernel, "g_down_keep", (hidden, df, sent), (None, half * width, None), shapes)


def up_kept(nh, nd, b, du, sent):
    half = nd // 2
    height, width = b.shape[1] // nd, du.shape[1] // nh

    def kernel(b, du, sent, *outs):
        for jx in range(half):
            far, here = outs[2 * jx : 2 * jx + 2]
            rows = slice(jx * height, (jx + 1) * height)
            for jh in range(nh):
                cols = slice(jh * width, (jh + 1) * width)
                g = dot(b[:, rows], du[:, cols], (0, 0)) + sent[rows, cols].astype(F32)
                if jh:
                    far[:, (jh - 1) * width : jh * width] = g.astype(BF)
                else:
                    here[...] = g.astype(BF)

    shapes = [(height, (nh - 1) * width), (height, width)] * half
    return one_step(kernel, "g_up_keep", (b, du, sent), (half * height, None, None), shapes)


def attention_kept(nh, nd, a, dqkv, datt, o, sent):
    half = nd // 2
    height = a.shape[0] // nd
    width, block = dqkv.shape[1] // nh, o.shape[1] // nh
    both = width + block

    def kernel(a, dqkv, datt, o, sent, *outs):
        for jx in range(half):
            far, here = outs[2 * jx : 2 * jx + 2]
            rows = slice(jx * height, (jx + 1) * height)
            inward = dot(a[rows], dqkv[...])
            outward = dot(datt[:, rows], o[...], (0, 0))
            for jh in range(nh):
                out, at = (far, (jh - 1) * both) if jh else (here, 0)
                terms = sent[rows, jh * both : (jh + 1) * both].astype(F32)
                g = inward[:, jh * width : (jh + 1) * width] + terms[:, :width]
                out[:, at : at + width] = g.astype(BF)
                g = outward[:, jh * block : (jh + 1) * block] + terms[:, width:]
                out[:, at + width : at + both] = g.astype(BF)

    shapes = [(height, (nh - 1) * both), (height, both)] * half
    cols = half * height
    return one_step(
        kernel, "g_att_keep", (a, dqkv, datt, o, sent), (None, None, cols, None, None), shapes
    )


def add_terms(name, terms, cuts=1, rows=None):
    rows, width = rows or terms[0].shape[0], terms[0].shape[1]
    size = rows // cuts

    def kernel(*refs):
        terms, outs = refs[: len(refs) - cuts], refs[len(refs) - cuts :]
        for c, out in enumerate(outs):
            out[...] = sum(
                v[c * size : (c + 1) * size].astype(F32) for v in terms
            ).astype(BF)

    return one_step(kernel, name, terms, [None] * len(terms), [(size, width)] * cuts)


def onward_kernel(*refs):
    for kind in range(2):
        keep, got, out = refs[kind], refs[2 + kind], refs[4 + kind]
        t = out.shape[1]
        out[0] = (keep[0, t:].astype(F32) + got[0, t:].astype(F32)).astype(BF)


def unpack_attention_gradient(terms):
    depth, width = terms[0].shape
    block = width // 4

    def kernel(*refs):
        *terms, inward, outward, squares = refs
        total = sum(v[...].astype(F32) for v in terms)
        square = total * total
        squares[...] = sum(
            jnp.sum(square[:, c : c + 128].reshape(depth // 8, 8, 128), axis=0)
            for c in range(0, width, 128)
        )
        for i in range(3):
            inward[i] = total[:, i * block : (i + 1) * block]
        outward[...] = total[:, 3 * block :].T

    return pl.pallas_call(
        kernel,
        name="unpack",
        out_shape=[
            jax.ShapeDtypeStruct((3, depth, block), F32),
            jax.ShapeDtypeStruct((block, depth), F32),
            jax.ShapeDtypeStruct((8, 128), F32),
        ],
        compiler_params=pltpu.CompilerParams(vmem_limit_bytes=32 * 2**20),
        cost_estimate=pl.CostEstimate(flops=0, bytes_accessed=0, transcendentals=0),
    )(*terms)


class Links:
    axes = ("x", "core", "h", "p", "q")

    def __init__(self, n_dp, n_mp):
        self.X, self.H = n_dp // 2, n_mp // 4
        self.n_dp, self.n_mp = n_dp, n_mp

    def shifted(self, v, axis, size, offset, name):
        with jax.named_scope(f"{name}_{axis}"):
            return lax.ppermute(v, axis, [((dst + offset) % size, dst) for dst in range(size)])

    def from_core(self, v, name):
        return self.shifted(v, "core", 2, 1, name)

    def from_x(self, v, jx, name):
        return self.shifted(v, "x", self.X, jx, name)

    def from_h(self, v, jh, name):
        return self.shifted(v, "h", self.H, jh, name)

    def over_h(self, w, name):
        return [self.from_h(w, jh, name) for jh in range(1, self.H)]

    def over_x(self, w, name):
        return [self.from_x(w, jx, name) for jx in range(1, self.X)]

    def send_x(self, parts, name):
        return [self.from_x(parts[jx], -jx, name) for jx in range(1, self.X)]

    def send_h(self, g, h, name):
        width = g.shape[h] // (self.H - 1)
        return [
            self.from_h(lax.slice_in_dim(g, (jh - 1) * width, jh * width, axis=h), -jh, name)
            for jh in range(1, self.H)
        ]

    def for_groups(self, v):
        here = lax.axis_index("h")
        images = v.shape[0] // self.H
        return [
            lax.dynamic_slice_in_dim(v, ((here - jh) % self.H) * images, images, axis=0)
            for jh in range(self.H)
        ]

    def to_group(self, parts, name):
        return [self.from_h(parts[jh], jh, name) for jh in range(1, self.H)]

    def leave_group(self, v, name):
        tokens = v.shape[1] // self.H
        return [
            self.from_h(v[:, jh * tokens : (jh + 1) * tokens], -jh, name) for jh in range(1, self.H)
        ]

    def at_home(self, v, received):
        here = lax.axis_index("h")
        images = v.shape[0]
        tokens = v.shape[1] // self.H
        out = jnp.zeros((images * self.H, tokens, v.shape[2]), v.dtype)
        for jh, part in enumerate([v[:, :tokens], *received]):
            out = lax.dynamic_update_slice_in_dim(
                out, part, ((here - jh) % self.H) * images, axis=0
            )
        return self.features_home(out)

    def over(self, v, kind, late, name):
        return self.shifted(v, "p" if (kind == 0) != late else "q", 2, 1, f"{name}{kind}")

    def first_hop(self, own, name):
        return [(own[k], self.over(own[k], k, False, name)) for k in range(2)]

    def near(self, hops):
        return [jnp.concatenate(pair, axis=1) for pair in hops]

    def last_hop(self, near, name):
        return [self.over(near[k], k, True, name) for k in range(2)]

    def send_late(self, parts, name):
        return [self.over(parts[2 * k + 1], k, True, name) for k in range(2)]

    def send_on(self, onward, name):
        return [self.over(onward[k], k, False, name) for k in range(2)]

    def features_here(self, v):
        x, c = lax.axis_index("x"), lax.axis_index("core")
        width = v.shape[-1] // self.n_dp
        return jnp.concatenate(
            [
                lax.dynamic_slice_in_dim(
                    v, (((x + jx) % self.X) * 2 + (c ^ jc)) * width, width, axis=v.ndim - 1
                )
                for jc in range(2)
                for jx in range(self.X)
            ],
            axis=-1,
        )

    def features_home(self, v):
        x, c = lax.axis_index("x"), lax.axis_index("core")
        width = v.shape[-1] // self.n_dp
        return jnp.concatenate(
            [
                lax.dynamic_slice_in_dim(
                    v,
                    (((e % 2) ^ c) * self.X + (e // 2 - x) % self.X) * width,
                    width,
                    axis=v.ndim - 1,
                )
                for e in range(self.n_dp)
            ],
            axis=-1,
        )

    def total(self, v):
        for axis, size in (("core", 2), ("q", 2), ("x", self.X), ("p", 2), ("h", self.H)):
            step = 1
            while step < size:
                with jax.named_scope("norm"):
                    v = v + lax.ppermute(v, axis, [(i ^ step, i) for i in range(size)])
                step *= 2
        return v


def per_device(
    links,
    stream_in,
    cotangent,
    noise_table,
    timesteps,
    bins,
    counts,
    w_qkv,
    w_out,
    w_up,
    w_down,
    m_qkv,
    m_out,
    m_up,
    m_down,
    v_qkv,
    v_out,
    v_up,
    v_down,
):
    H = links.H
    slots, _, D = stream_in.shape
    images = slots // H
    here = lax.axis_index("h")

    steps_here = lax.dynamic_slice_in_dim(timesteps, here * images, images)
    table_rows = noise_table.shape[0]
    picks = (steps_here[:, None] == jnp.arange(table_rows)[None, :]).astype(F32)
    modulation = jnp.dot(
        picks, noise_table.reshape(table_rows, -1), precision=lax.Precision.HIGHEST
    ).reshape(images, 6, D)
    modulation = links.features_here(modulation)
    live = jnp.arange(slots) < counts[0]
    loss_scale = live.astype(F32) * (bins.astype(F32) + 1.0) / BINS
    loss_scale = lax.dynamic_slice_in_dim(loss_scale, here * images, images)
    loss_scale = jnp.broadcast_to(loss_scale[:, None, None], (images, 1, D))

    block = w_qkv.shape[2]
    length = stream_in.shape[1] * H * 4
    steps = images // 2
    rows = images * length
    nh, nd = H, 2 * links.X
    heads = H * block
    hidden_width = H * w_up.shape[1]
    whole = lambda width: (steps, 2, length, width)
    parts = [(steps, length // 2, D)] * 4

    tokens = length // 4
    every, kinds = (images, tokens, D), [((steps, tokens, D), BF)] * 2

    def over_images(kernel, name, arrays, outs):
        return image_call(kernel, name, steps, arrays, outs)

    def onward(parts, got, name):
        arrays = [parts[0], parts[2], *got]
        return over_images(onward_kernel, name, arrays, kinds)

    def sums(parts, got, last):
        return [parts[0], parts[2], *got, *last]

    def flat(v):
        return v.reshape(rows, v.shape[-1])

    def call(kernel, name, blocked, weights, outs, resident=(), whole_outs=()):
        return list(
            group_call(kernel, name, nh, nd, steps, blocked, weights, outs, resident, whole_outs)
        )

    def halves(w):
        size = w.shape[0] // 2
        return w[:size], w[size:]

    def joined(pair):
        return [jnp.concatenate(two, axis=0) for two in zip(*pair)]

    def total(here, there):
        return here + sum(v.astype(F32) for v in there)

    stream_parts = links.for_groups(links.features_here(stream_in))
    packed = pack_attention_weights(w_qkv, w_out)
    stream_got = links.to_group(stream_parts, "stream")
    x_packed = links.over_x(packed, "wqo0")
    up, down = w_up.astype(BF), w_down.astype(BF)
    stream_parts, stream_got, x_packed, packed, up = sync(
        stream_parts, stream_got, x_packed, packed, up
    )

    stream = jnp.concatenate([stream_parts[0], *stream_got], axis=1)
    a_own = over_images(first_norm_kernel, "first_norm", [stream, modulation], kinds)
    a_hops = links.first_hop(a_own, "a")
    packed_one, packed_two = halves(packed)
    far_one = links.over_h(packed_one, "wqoA")
    x_up = links.over_x(up, "wu0")
    wqo = [jnp.stack([packed, *x_packed])]
    a_near, far_one, x_up, wqo, packed_two = sync(
        links.near(a_hops), far_one, x_up, wqo, packed_two
    )

    a_far = links.last_hop(a_near, "a")
    far_two = links.over_h(packed_two, "wqoB")
    x_one = [links.over_x(w, "wqoA1") for w in far_one]
    cot_parts = links.for_groups(links.features_here(cotangent.astype(BF)))
    cot_one = [v[:steps] for v in cot_parts]
    cot_two = [v[steps:] for v in cot_parts]
    wu = [jnp.stack([up, *x_up])]
    a_far, far_two, x_one, cot_one, cot_two, wqo, wu = sync(
        a_far, far_two, x_one, cot_one, cot_two, wqo, wu
    )

    x_two = [links.over_x(w, "wqoB1") for w in far_two]
    cot_one = [cot_one[0], *links.to_group(cot_one, "cotA")]
    wqo.append(links.from_core(wqo[0], "wqo0"))
    wu.append(links.from_core(wu[0], "wu0"))
    packed_far = joined((far_one, far_two))
    packed_far, x_two, cot_one, cot_two, wqo, wu = sync(
        packed_far, x_two, cot_one, cot_two, wqo, wu
    )

    cot_two = [cot_two[0], *links.to_group(cot_two, "cotB")]
    for w, one, two in zip(packed_far, x_one, x_two):
        wqo.append(jnp.stack([w, *joined((one, two))]))
        wqo.append(links.from_core(wqo[-1], "wqo1"))
    up_one, up_two = halves(up)
    cot_one, cot_two, wqo, up_one, up_two, down = sync(cot_one, cot_two, wqo, up_one, up_two, down)

    cot = jnp.concatenate([jnp.concatenate(v, axis=1) for v in (cot_one, cot_two)], axis=0)
    df_own = over_images(loss_kernel, "loss", [cot, loss_scale, modulation], kinds)
    df_near = links.near(links.first_hop(df_own, "df"))
    up_one = links.over_h(up_one, "wuA")
    x_down = links.over_x(down, "wd0")
    a_rows, qkv, o, probs, *att = call(
        attention_kernel,
        "attention",
        [a_near[0], a_far[0], a_near[1], a_far[1]],
        wqo,
        [whole(D), whole(3 * heads), whole(heads), (steps, 2, heads // HD, length, length), *parts],
    )
    df_near, att, up_one, up_two, x_down = sync(df_near, att, up_one, up_two, x_down)

    att_got = links.send_late(att, "att")
    up_two = links.over_h(up_two, "wuB")
    wd = [jnp.stack([down, *x_down])]
    wd.append(links.from_core(wd[0], "wd0"))
    att_got, up_two, wd, down = sync(att_got, up_two, wd, down)

    att_last = links.send_on(onward(att, att_got, "att_onward"), "att")
    down_one, down_two = halves(down)
    down_one = links.over_h(down_one, "wdA")
    up_far = joined((up_one, up_two))
    x_up = [links.over_x(w, "wu1") for w in up_far]
    residual, *b = over_images(
        second_norm_kernel,
        "second_norm",
        [stream, modulation, *sums(att, att_got, att_last)],
        [(every, F32), *kinds],
    )
    b, down_one, up_far, x_up, down_two = sync(b, down_one, up_far, x_up, down_two)

    b_hops = links.first_hop(b, "b")
    down_two = links.over_h(down_two, "wdB")
    x_one = [links.over_x(w, "wdA1") for w in down_one]
    wu_far = [jnp.stack([w, *others]) for w, others in zip(up_far, x_up)]
    b_near, down_two, x_one, wu_far = sync(links.near(b_hops), down_two, x_one, wu_far)

    b_far = links.last_hop(b_near, "b")
    x_two = [links.over_x(w, "wdB1") for w in down_two]
    for w in wu_far:
        wu += [w, links.from_core(w, "wu1")]
    b_far, x_two, wu, df_near = sync(b_far, x_two, wu, df_near)

    df_far = links.last_hop(df_near, "df")
    for w, one, two in zip(joined((down_one, down_two)), x_one, x_two):
        wd.append(jnp.stack([w, *joined((one, two))]))
        wd.append(links.from_core(wd[-1], "wd1"))
    b_rows, hidden, slope = call(
        up_kernel,
        "up",
        [b_near[0], b_far[0], b_near[1], b_far[1]],
        wu,
        [whole(D), whole(hidden_width), whole(hidden_width)],
    )
    df_far, wd, b_rows, hidden, slope = sync(df_far, wd, b_rows, hidden, slope)

    df_rows, du, *db = call(
        up_back_kernel,
        "up_back",
        [df_near[0], df_far[0], df_near[1], df_far[1], slope],
        wu + wd,
        [whole(D), whole(hidden_width), *parts],
    )
    b_rows, df_rows, hidden, du, db, a_rows = sync(b_rows, df_rows, hidden, du, db, a_rows)

    db_got = links.send_late(db, "db")
    down_send = gradient("g_down_send", nh, nd, flat(hidden), flat(df_rows), True, 1)
    up_send = gradient("g_up_send", nh, nd, flat(b_rows), flat(du), False, 1)
    a_columns = flat(a_rows).T
    db_got, down_send, up_send, b_rows, du, hidden, df_rows, a_columns = sync(
        db_got, down_send, up_send, b_rows, du, hidden, df_rows, a_columns
    )

    db_last = links.send_on(onward(db, db_got, "db_onward"), "db")
    down_sent = links.from_core(down_send, "g_down")
    g_down = down_kept(nh, nd, flat(hidden), flat(df_rows), down_sent)
    db_last, g_down, up_send, b_rows, du, hidden = sync(
        db_last, g_down, up_send, b_rows, du, hidden
    )

    dr, *datt_own = over_images(
        second_norm_back_kernel,
        "second_norm_back",
        [cot, loss_scale, residual, modulation, *sums(db, db_got, db_last)],
        [(every, F32), *kinds],
    )
    datt_hops = links.first_hop(datt_own, "datt")
    down_one = links.send_x(g_down[0::3], "g_downA")
    up_sent = links.from_core(up_send, "g_up")
    (down_one,) = add_terms("g_downA_sum", [g_down[0], *down_one])
    datt_near, g_down, down_one, up_sent, b_rows, du, hidden = sync(
        links.near(datt_hops), g_down, down_one, up_sent, b_rows, du, hidden
    )

    datt_far = links.last_hop(datt_near, "datt")
    down_one = links.send_h(down_one, 0, "g_downA")
    down_mid = links.send_x(g_down[1::3], "g_downB")
    ff = call(down_kernel, "down", [hidden], wd, parts)
    g_up = up_kept(nh, nd, flat(b_rows), flat(du), up_sent)
    far = (nh - 1) * (g_down[1].shape[0] // nh)
    (down_two,) = add_terms("g_downB_sum", [g_down[1], *down_mid], 1, far)
    datt_far, down_one, down_mid, down_two, g_down, g_up, ff = sync(
        datt_far, down_one, down_mid, down_two, g_down, g_up, ff
    )

    down_two = links.send_h(down_two, 0, "g_downB")
    up_far = links.send_x(g_up[0::2], "g_upA")
    ff_got = links.send_late(ff, "ff")
    *da, datt, dqkv, att_send = call(
        attention_back_kernel,
        "attention_back",
        [datt_near[0], datt_far[0], datt_near[1], datt_far[1], qkv, probs],
        wqo,
        parts,
        (a_columns, o),
        (whole(D), whole(3 * heads), (D // 2, 4 * heads)),
    )
    up_one, up_two = add_terms("g_upA_sum", [g_up[0], *up_far], 2)
    down_two, up_one, up_two, ff_got, datt, dqkv, da, att_send, g_up, g_down = sync(
        down_two, up_one, up_two, ff_got, datt, dqkv, da, att_send, g_up, g_down
    )

    da_got = links.send_late(da, "da")
    att_sent = links.from_core(att_send, "g_att")
    up_one = links.send_h(up_one, 1, "g_upA")
    down_last = links.send_x(g_down[2::3], "g_downC")
    g_att = attention_kept(nh, nd, a_columns, flat(dqkv), flat(datt), flat(o), att_sent)
    da_got, g_att, g_up, up_one, up_two, da, ff_got, down_last = sync(
        da_got, g_att, g_up, up_one, up_two, da, ff_got, down_last
    )

    att_far = links.send_x(g_att[0::2], "g_attA")
    up_two = links.send_h(up_two, 1, "g_upB")
    da_last = links.send_on(onward(da, da_got, "da_onward"), "da")
    att_one, att_two = add_terms("g_attA_sum", [g_att[0], *att_far], 2)
    att_one, att_two, up_two, da_last, g_att, g_up, ff_got = sync(
        att_one, att_two, up_two, da_last, g_att, g_up, ff_got
    )

    att_one = links.send_h(att_one, 1, "g_attA")
    up_here = links.send_x(g_up[1::2], "g_upC")
    ff_last = links.send_on(onward(ff, ff_got, "ff_onward"), "ff")
    (input_grad,) = over_images(
        first_norm_back_kernel,
        "first_norm_back",
        [stream, dr, modulation, *sums(da, da_got, da_last)],
        [(every, BF)],
    )
    g_down = jnp.concatenate(
        [
            sum(v[far:].astype(F32) for v in (g_down[1], *down_mid)),
            sum(v.astype(F32) for v in (g_down[2], *down_last)),
        ],
        axis=0,
    )
    g_down = total(g_down, joined((down_one, down_two)))
    att_one, att_two, up_here, ff_last, g_att, g_up, input_grad = sync(
        att_one, att_two, up_here, ff_last, g_att, g_up, input_grad
    )

    att_two = links.send_h(att_two, 1, "g_attB")
    att_here = links.send_x(g_att[1::2], "g_attC")
    (output,) = over_images(
        output_kernel,
        "output",
        [residual, modulation, *sums(ff, ff_got, ff_last)],
        [(every, BF)],
    )
    g_up = total(
        g_up[1].astype(F32) + sum(v.astype(F32) for v in up_here), joined((up_one, up_two))
    )
    att_two, att_here, g_att, output, input_grad = sync(
        att_two, att_here, g_att, output, input_grad
    )

    input_grad_got = links.leave_group(input_grad, "input_grad")
    att_there = joined((att_one, att_two))
    g_qkv, g_out, squares = unpack_attention_gradient(
        [g_att[1], *att_here, *att_there]
    )
    squares = jnp.sum(squares) + jnp.sum(g_up * g_up) + jnp.sum(g_down * g_down)
    grad_norm = jnp.sqrt(links.total(squares))
    grad_norm, output = sync(grad_norm, output)
    output_got = links.leave_group(output, "output")
    input_grad = links.at_home(input_grad, input_grad_got).astype(F32)
    output = links.at_home(output, output_got)
    factor = jnp.minimum(1.0, clip_limit / (grad_norm + 1e-06))
    one_qkv, two_qkv, new_qkv = (
        v.transpose(1, 0, 2)
        for v in adam_update(
            g_qkv, *(v.transpose(1, 0, 2) for v in (m_qkv, v_qkv, w_qkv)), factor, learn_rate
        )
    )
    one_out, two_out, new_out = adam_update(g_out, m_out, v_out, w_out, factor, output_rate)
    one_up, two_up, new_up = adam_update(g_up, m_up, v_up, w_up, factor, learn_rate)
    one_down, two_down, new_down = adam_update(g_down, m_down, v_down, w_down, factor, learn_rate)
    return (
        output,
        input_grad,
        grad_norm,
        one_qkv,
        one_out,
        one_up,
        one_down,
        two_qkv,
        two_out,
        two_up,
        two_down,
        new_qkv,
        new_out,
        new_up,
        new_down,
    )


def solution(mesh):
    n_dp, n_mp = mesh.shape["dp"], mesh.shape["mp"]
    links = Links(n_dp, n_mp)
    fine = Mesh(mesh.devices.reshape(links.X, 2, links.H, 2, 2), links.axes)
    dp, mp = ("x", "core"), ("h", "p", "q")
    tokens, qkv = P(dp, mp, None), P(dp, None, mp)
    rows, columns = P(mp, dp), P(dp, mp)
    weights = (qkv, rows, columns, rows)
    return jax.shard_map(
        lambda *args: per_device(links, *args),
        mesh=fine,
        in_specs=(tokens, tokens, P(), P(dp), P(dp), P(dp)) + 3 * weights,
        out_specs=(tokens, tokens, P()) + 3 * weights,
        check_vma=False,
    )
```

time: 808 us -> 703 us (0.87)
  waiting for transfers between devices: 417 us -> 299 us
  Pallas kernels: 162 us -> 198 us
  other arithmetic: 77.9 us -> 59.8 us
    ppermute x73, waiting for transfers between devices: 410 us -> 288 us  [shifted(): lax.ppermute(v, axis, [((dst + offset) % size, dst) for dst in range(size)])]
    pallas_call x4 -> x23, Pallas kernels: 107 us -> 182 us  [the longest x5 119 us: group_call(): pl.pallas_call(lambda *refs: kernel(nh, nd, *refs), name=name, grid=(step...]
    pallas_call x8 -> x2, Pallas kernels: 54.2 us -> 15.9 us  [gradient(): pl.pallas_call(kernel, name=name, grid=(nh, half), in_specs=in_specs, out...]
    convert_element_type x23 -> x1, other arithmetic: 31.2 us -> 1.57 us  [per_device(): input_grad = links.at_home(input_grad, input_grad_got).astype(F32)]
    reduce_sum x12 -> x3, other arithmetic: 15.7 us -> 6.18 us  [per_device(): squares = jnp.sum(squares) + jnp.sum(g_up * g_up) + jnp.sum(g_down * g_down)]
    unnamed x208 -> x161, local copies, waits for them, and re-layouts: 31.6 us -> 23.1 us
  transfers between devices with their start and end apart: 78 -> 78, of which waited for: 39 -> 38; matrix products, arithmetic and copies ran while one was open for 10% -> 10% of each run, Pallas kernels for 12% -> 24%
where the time goes in v3:
time: 703 us; the launch traced here: 692 us
  waiting for transfers between devices  299 us (43%)
  Pallas kernels  198 us (28%)
  starting transfers between devices  83.2 us (12%)
  other arithmetic  59.8 us (9%)
  local copies, waits for them, and re-layouts  41.6 us (6%)
  between operations  9.18 us (1%)
    ppermute x73, waiting for transfers between devices, shifted(): lax.ppermute(v, axis, [((dst + offset) % size, dst) for dst in range(size)])  288 us
    pallas_call x5, Pallas kernels, group_call(): pl.pallas_call(lambda *refs: kernel(nh, nd, *refs), name=name, grid=(step...  119 us
    ppermute x73, starting transfers between devices, shifted(): lax.ppermute(v, axis, [((dst + offset) % size, dst) for dst in range(size)])  69.5 us
    pallas_call x7, Pallas kernels, one_step(): pl.pallas_call(kernel, name=name, grid=(1,), in_specs=[pl.BlockSpec((v.sh...  40.3 us
    unnamed x161, local copies, waits for them, and re-layouts  23.1 us
    pallas_call x10, Pallas kernels, image_call(): pl.pallas_call(kernel, name=name, grid=(steps,), in_specs=[cut(seen(v.sha...  20.9 us
    pallas_call x2, Pallas kernels, gradient(): pl.pallas_call(kernel, name=name, grid=(nh, half), in_specs=in_specs, out...  15.9 us
  transfers between devices with their start and end apart: 78, of which 38 were waited for; matrix products, arithmetic and copies ran while one was open for 10% of the time, Pallas kernels for 24%

profile of v3, /device:TPU:0, one launch (start us, length us, event | category | flops | bytes accessed | tf_op | source)
XLA Modules:
  0.0 691.9 jit_solution(2818682690802611964)
XLA Ops:
  18.9 19.6 %collective-permute-done = bf16[4,32,2048]{2,1,0:T(8,128)(2,1)} collective-permute-done((bf16[4,32,2048]{2,1,0:T(8,128)(2,1)}, bf16[4,32,2048]{2,1,0:T(8,128)(2,1)}, u32[]{:S(2)}, u32[]{:S(2)}) %collective-permute-start) | collective-permute-done | bytes 524320 | tf_op jit(solution)/shard_map/stream_h/ppermute | solution.py:550
  50.3 12.2 %collective-permute-done.2 = bf16[2,64,2048]{2,1,0:T(8,128)(2,1)S(1)} collective-permute-done((bf16[2,64,2048]{2,1,0:T(8,128)(2,1)S(1)}, bf16[2,64,2048]{2,1,0:T(8,128)(2,1)S(1)}, u32[]{:S(2)}, u32[]{:S(2)}) %collective-permute-start.2) | collective-permute-done | bytes 524320 | tf_op jit(solution)/shard_map/a0_p/ppermute | solution.py:550
  78.2 25.1 %collective-permute-done.8 = bf16[256,1024]{1,0:T(8,128)(2,1)} collective-permute-done((bf16[256,1024]{1,0:T(8,128)(2,1)}, bf16[256,1024]{1,0:T(8,128)(2,1)}, u32[]{:S(2)}, u32[]{:S(2)}) %collective-permute-start.8) | collective-permute-done | bytes 524320 | tf_op jit(solution)/shard_map/wqoB_h/ppermute | solution.py:550
  110.1 11.9 %collective-permute-done.11 = bf16[2,32,2048]{2,1,0:T(8,128)(2,1)S(1)} collective-permute-done((bf16[2,32,2048]{2,1,0:T(8,128)(2,1)S(1)}, bf16[2,32,2048]{2,1,0:T(8,128)(2,1)S(1)}, u32[]{:S(2)}, u32[]{:S(2)}) %collective-permute-start.11) | collective-permute-done | bytes 262176 | tf_op jit(solution)/shard_map/cotA_h/ppermute | solution.py:550
  129.4 13.3 %collective-permute-done.14 = bf16[2,32,2048]{2,1,0:T(8,128)(2,1)S(1)} collective-permute-done((bf16[2,32,2048]{2,1,0:T(8,128)(2,1)S(1)}, bf16[2,32,2048]{2,1,0:T(8,128)(2,1)S(1)}, u32[]{:S(2)}, u32[]{:S(2)}) %collective-permute-start.14) | collective-permute-done | bytes 262176 | tf_op jit(solution)/shard_map/cotB_h/ppermute | solution.py:550
  149.1 23.2 %attention.1 = (bf16[2,2,256,2048]{3,2,1,0:T(8,128)(2,1)}, bf16[2,2,256,1536]{3,2,1,0:T(8,128)(2,1)}, bf16[2,2,256,512]{3,2,1,0:T(8,128)(2,1)}, bf16[2,2,4,256,2...) custom-call(bf16[2,128,2048]{2,1,0:T(8,128)(2,1)} %pad_maximum_fusio, ...), custom_call_target="tpu_custom_call" | custom-call | tf_op jit(solution)/shard_map/attention/pallas_call | solution.py:259
  183.6 30.1 %collective-permute-done.22 = bf16[256,1024]{1,0:T(8,128)(2,1)S(1)} collective-permute-done((bf16[256,1024]{1,0:T(8,128)(2,1)S(1)}, bf16[256,1024]{1,0:T(8,128)(2,1)S(1)}, u32[]{:S(2)}, u32[]{:S(2)}) %collective-permute-start.22) | collective-permute-done | bytes 524320 | tf_op jit(solution)/shard_map/wuB_h/ppermute | solution.py:550
  225.0 13.8 %collective-permute-done.24.refs_4_ = bf16[2,64,2048]{2,1,0:T(8,128)(2,1)S(1)} collective-permute-done((bf16[2,64,2048]{2,1,0:T(8,128)(2,1)S(1)}, bf16[2,64,2048]{2,1,0:T(8,128)(2,1)S(1)}, u32[]{:S(2)}, u32[]{:S(2)}) %collective-permute-start.24) | collective-permute-done | bytes 524320 | tf_op jit(solution)/shard_map/att0_p/ppermute | solution.py:550
  251.2 18.4 %collective-permute-done.28 = bf16[2,64,2048]{2,1,0:T(8,128)(2,1)S(1)} collective-permute-done((bf16[2,64,2048]{2,1,0:T(8,128)(2,1)S(1)}, bf16[2,64,2048]{2,1,0:T(8,128)(2,1)S(1)}, u32[]{:S(2)}, u32[]{:S(2)}) %collective-permute-start.28) | collective-permute-done | bytes 524320 | tf_op jit(solution)/shard_map/b0_p/ppermute | solution.py:550
  274.5 13.4 %collective-permute-done.34 = bf16[512,512]{1,0:T(8,128)(2,1)S(1)} collective-permute-done((bf16[512,512]{1,0:T(8,128)(2,1)S(1)}, bf16[512,512]{1,0:T(8,128)(2,1)S(1)}, u32[]{:S(2)}, u32[]{:S(2)}) %collective-permute-start.34) | collective-permute-done | bytes 524320 | tf_op jit(solution)/shard_map/wdB1_x/ppermute | solution.py:550
  287.8 9.9 %collective-permute-done.32.refs_1_ = bf16[2,128,2048]{2,1,0:T(8,128)(2,1)S(1)} collective-permute-done((bf16[2,128,2048]{2,1,0:T(8,128)(2,1)S(1)}, bf16[2,128,2048]{2,1,0:T(8,128)(2,1)S(1)}, u32[]{:S(2)}, u32[]{:S(2)}) %collective-permute-start.32) | collective-permute-done | bytes 1048608 | tf_op jit(solution)/shard_map/b0_q/ppermute | solution.py:550
  302.7 19.5 %up.1 = (bf16[2,2,256,2048]{3,2,1,0:T(8,128)(2,1)}, bf16[2,2,256,2048]{3,2,1,0:T(8,128)(2,1)}, bf16[2,2,256,2048]{3,2,1,0:T(8,128)(2,1)}) custom-call(bf16[2,128,2048]{2,1,0:T(8,128)(2,1)} %copy-done.53, bf16[2,128,2048]{2,1,0:T(8,128)(2,1)} %copy-done.64, bf16[2,128,2048]{2,1,0:T(8,128)(2,1)} %copy-done.54, bf16[2,128,2048]{2,1,0:T(8,128)(2,1)} %copy-done.65, ...), custom_call_target="tpu_custom_call" | custom-call | tf_op jit(solution)/shard_map/up/pallas_call | solution.py:259
  328.1 26.6 %up_back.1 = (bf16[2,2,256,2048]{3,2,1,0:T(8,128)(2,1)}, bf16[2,2,256,2048]{3,2,1,0:T(8,128)(2,1)}, bf16[2,128,2048]{2,1,0:T(8,128)(2,1)}, bf16[2,128,2048]{2,1,...) custom-call(bf16[2,128,2048]{2,1,0:T(8,128)(2,1)} %pad_maximum_fusion.12.refs_0_, ...), custom_call_target="tpu_custom_call" | custom-call | tf_op jit(solution)/shard_map/up_back/pallas_call | solution.py:259
  370.9 8.1 %g_up_send.1 = bf16[1024,2048]{1,0:T(8,128)(2,1)S(1)} custom-call(bf16[1024,2048]{1,0:T(8,128)(2,1)} %bitcast.92, bf16[1024,2048]{1,0:T(8,128)(2,1)} %bitcast.94), custom_call_target="tpu_custom_call" | custom-call | tf_op jit(solution)/shard_map/g_up_send/pallas_call | solution.py:392
  390.0 9.7 %g_down_keep.1 = (bf16[512,512]{1,0:T(8,128)(2,1)}, bf16[1024,512]{1,0:T(8,128)(2,1)}, bf16[512,512]{1,0:T(8,128)(2,1)}, bf16[512,512]{1,0:T(8,128)(2,1)}, bf16[...) custom-call(bf16[1024,2048]{1,0:T(8,128)(2,1)} %bitcast.89, bf16[1024,2048]{1,0:T(8,128)(2,1)} %bitcast.97, ...), custom_call_target="tpu_custom_call" | custom-call | tf_op jit(solution)/shard_map/g_down_keep/pallas_call | solution.py:405
  431.3 14.3 %down.1 = (bf16[2,128,2048]{2,1,0:T(8,128)(2,1)}, bf16[2,128,2048]{2,1,0:T(8,128)(2,1)}, bf16[2,128,2048]{2,1,0:T(8,128)(2,1)}, bf16[2,128,2048]{2,1,0:T(8,128)(2,1)}) custom-call(bf16[2,2,256,2048]{3,2,1,0:T(8,128)(2,1)} %get-tuple-element.446.refs_0_, bf16[2,1024,512]{2,1,0:T(8,128)(2,1)} %copy-done.35, bf16[2,1024,512]{2,1,0:T(8,128)(2,1)} %copy-done.46, ...), custom_call_target="tpu_custom_call" | custom-call | tf_op jit(solution)/shard_map/down/pallas_call | solution.py:259
  445.6 9.6 %g_up_keep.1 = (bf16[512,1024]{1,0:T(8,128)(2,1)}, bf16[512,1024]{1,0:T(8,128)(2,1)}, bf16[512,1024]{1,0:T(8,128)(2,1)}, bf16[512,1024]{1,0:T(8,128)(2,1)}) custom-call(bf16[1024,2048]{1,0:T(8,128)(2,1)} %bitcast.93, bf16[1024,2048]{1,0:T(8,128)(2,1)} %bitcast.95, bf16[1024,2048]{1,0:T(8,128)(2,1)} %collective-permute-done.47.sent), custom_call_target="tpu_custom_call" | custom-call | tf_op jit(solution)/shard_map/g_up_keep/pallas_call | solution.py:405
  468.6 35.0 %attention_back.1 = (bf16[2,128,2048]{2,1,0:T(8,128)(2,1)}, bf16[2,128,2048]{2,1,0:T(8,128)(2,1)}, bf16[2,128,2048]{2,1,0:T(8,128)(2,1)}, bf16[2,128,2048]{2,1,0...) custom-call(bf16[2048,1024]{1,0:T(8,128)(2,1)} %bitcast.90, ...), custom_call_target="tpu_custom_call" | custom-call | tf_op jit(solution)/shard_map/attention_back/pallas_call | solution.py:259
  515.7 11.2 %g_att_keep.1 = (bf16[512,1024]{1,0:T(8,128)(2,1)}, bf16[512,1024]{1,0:T(8,128)(2,1)}, bf16[512,1024]{1,0:T(8,128)(2,1)}, bf16[512,1024]{1,0:T(8,128)(2,1)}) custom-call(bf16[2048,1024]{1,0:T(8,128)(2,1)} %bitcast.91, bf16[1024,1536]{1,0:T(8,128)(2,1)} %bitcast.103, bf16[1024,2048]{1,0:T(8,128)(2,1)} %bitcast.102, bf16[1024,512]{1,0:T(8,128)(2,1)} %bitcast.99, ...), custom_call_target="tpu_custom_call" | custom-call | tf_op jit(solution)/shard_map/g_att_keep/pallas_call | solution.py:405
  526.9 15.6 %collective-permute-done.59 = bf16[256,1024]{1,0:T(8,128)(2,1)} collective-permute-done((bf16[256,1024]{1,0:T(8,128)(2,1)}, bf16[256,1024]{1,0:T(8,128)(2,1)}, u32[]{:S(2)}, u32[]{:S(2)}) %collective-permute-start.59) | collective-permute-done | bytes 524320 | tf_op jit(solution)/shard_map/g_upA_h/ppermute | solution.py:550
  552.1 16.4 %collective-permute-done.61.refs_1_ = bf16[512,1024]{1,0:T(8,128)(2,1)} collective-permute-done((bf16[512,1024]{1,0:T(8,128)(2,1)}, bf16[512,1024]{1,0:T(8,128)(2,1)}, u32[]{:S(2)}, u32[]{:S(2)}) %collective-permute-start.61) | collective-permute-done | bytes 1048608 | tf_op jit(solution)/shard_map/g_attA_x/ppermute | solution.py:550
  582.3 15.4 %collective-permute-done.65 = bf16[256,1024]{1,0:T(8,128)(2,1)S(1)} collective-permute-done((bf16[256,1024]{1,0:T(8,128)(2,1)}, bf16[256,1024]{1,0:T(8,128)(2,1)S(1)}, u32[]{:S(2)}, u32[]{:S(2)}) %collective-permute-start.65) | collective-permute-done | bytes 524320 | tf_op jit(solution)/shard_map/g_attA_h/ppermute | solution.py:550
  612.9 13.0 %collective-permute-done.69 = bf16[256,1024]{1,0:T(8,128)(2,1)S(1)} collective-permute-done((bf16[256,1024]{1,0:T(8,128)(2,1)}, bf16[256,1024]{1,0:T(8,128)(2,1)S(1)}, u32[]{:S(2)}, u32[]{:S(2)}) %collective-permute-start.69) | collective-permute-done | bytes 524320 | tf_op jit(solution)/shard_map/g_attB_h/ppermute | solution.py:550
  651.5 8.8 %collective-permute-done.75 = f32[]{:T(128)} collective-permute-done((f32[]{:T(128)}, f32[]{:T(128)}, u32[]{:S(2)}, u32[]{:S(2)}) %collective-permute-start.75) | collective-permute-done | bytes 36 | tf_op jit(solution)/shard_map/norm/ppermute | solution.py:658
  (381 shorter events, 288.8 us)
Async XLA Ops:
  3.4 35.0 %collective-permute-start.1 = (bf16[512,1024]{1,0:T(8,128)(2,1)S(1)}, bf16[512,1024]{1,0:T(8,128)(2,1)}, u32[]{:S(2)}, u32[]{:S(2)}) collective-permute-start(bf16[512,1024]{1,0:T(8,128)(2,1)S(1)} %pack.1), channel_id=1, source_target_pairs={{16,0},{0,16},{17,1},{1,17},{18,2},{2,18},{19,3},{3,19},{20,4},{4,... | collective-permute-start | bytes 3145736 | tf_op jit(solution)/shard_map/wqo0_x/ppermute | solution.py:550
  38.5 31.8 %collective-permute-start.5 = (bf16[512,1024]{1,0:T(8,128)(2,1)S(1)}, bf16[512,1024]{1,0:T(8,128)(2,1)S(1)}, u32[]{:S(2)}, u32[]{:S(2)}) collective-permute-start(bf16[512,1024]{1,0:T(8,128)(2,1)S(1)} %copy-done.42), channel_id=1, source_target_pairs={{16,0},{0,16},{17,1},{1,17},{18,2},{2,18},{19,3},{3,19},{20,4},{4,... | collective-permute-start | bytes 3145736 | tf_op jit(solution)/shard_map/wu0_x/ppermute | solution.py:550
  70.3 33.1 %collective-permute-start.6 = (bf16[2,128,2048]{2,1,0:T(8,128)(2,1)}, bf16[2,128,2048]{2,1,0:T(8,128)(2,1)}, u32[]{:S(2)}, u32[]{:S(2)}) collective-permute-start(bf16[2,128,2048]{2,1,0:T(8,128)(2,1)} %pad_maximum_fusion.8.refs_0_), channel_id=1, source_target_pairs={{1,0},{0,1},{3,2},{2,3},{5,4},{4,5},{7,6},{6,7},{9,8},{8,9},{11,10... | collective-permute-start | bytes 3145736 | tf_op jit(solution)/shard_map/a0_q/ppermute | solution.py:550
  70.8 34.8 %collective-permute-start.7 = (bf16[2,128,2048]{2,1,0:T(8,128)(2,1)}, bf16[2,128,2048]{2,1,0:T(8,128)(2,1)}, u32[]{:S(2)}, u32[]{:S(2)}) collective-permute-start(bf16[2,128,2048]{2,1,0:T(8,128)(2,1)} %pad_maximum_fusion.9.refs_2_), channel_id=1, source_target_pairs={{2,0},{0,2},{3,1},{1,3},{6,4},{4,6},{7,5},{5,7},{10,8},{8,10},{11,... | collective-permute-start | bytes 3145736 | tf_op jit(solution)/shard_map/a1_p/ppermute | solution.py:550
  70.8 32.6 %collective-permute-start.8 = (bf16[256,1024]{1,0:T(8,128)(2,1)}, bf16[256,1024]{1,0:T(8,128)(2,1)}, u32[]{:S(2)}, u32[]{:S(2)}) collective-permute-start(bf16[256,1024]{1,0:T(8,128)(2,1)} %get-tuple-element.294), channel_id=1, source_target_pairs={{4,0},{0,4},{5,1},{1,5},{6,2},{2,6},{7,3},{3,7},{12,8},{8,12},{13,... | collective-permute-start | bytes 1572872 | tf_op jit(solution)/shard_map/wqoB_h/ppermute | solution.py:550
  142.7 34.2 %collective-permute-start.19 = (bf16[1024,512]{1,0:T(8,128)(2,1)}, bf16[1024,512]{1,0:T(8,128)(2,1)}, u32[]{:S(2)}, u32[]{:S(2)}) collective-permute-start(bf16[1024,512]{1,0:T(8,128)(2,1)} %convert_element_type.43), channel_id=1, source_target_pairs={{16,0},{0,16},{17,1},{1,17},{18,2},{2,18},{19,3},{3,19},{20,4},{4,... | collective-permute-start | bytes 3145736 | tf_op jit(solution)/shard_map/wd0_x/ppermute | solution.py:550
  147.2 29.7 %collective-permute-start.18 = (bf16[256,1024]{1,0:T(8,128)(2,1)}, bf16[256,1024]{1,0:T(8,128)(2,1)}, u32[]{:S(2)}, u32[]{:S(2)}) collective-permute-start(bf16[256,1024]{1,0:T(8,128)(2,1)} %get-tuple-element.329), channel_id=1, source_target_pairs={{4,0},{0,4},{5,1},{1,5},{6,2},{2,6},{7,3},{3,7},{12,8},{8,12},{13,... | collective-permute-start | bytes 1572872 | tf_op jit(solution)/shard_map/wuA_h/ppermute | solution.py:550
  178.9 37.0 %collective-permute-start.23 = (bf16[2,1024,512]{2,1,0:T(8,128)(2,1)S(1)}, bf16[2,1024,512]{2,1,0:T(8,128)(2,1)S(1)}, u32[]{:S(2)}, u32[]{:S(2)}) collective-permute-start(bf16[2,1024,512]{2,1,0:T(8,128)(2,1)S(1)} %pad_maximum_fusion.3.refs_9_.refs_1_), channel_id=1, source_target_pairs={{8,0},{0,8},{9,1},{1,9},{10,2},{2,10},{11,3},{3,11},{12,4},{4,12},... | collective-permute-start | bytes 6291464 | tf_op jit(solution)/shard_map/wd0_core/ppermute | solution.py:550
  178.9 34.7 %collective-permute-start.20 = (bf16[2,128,2048]{2,1,0:T(8,128)(2,1)S(1)}, bf16[2,128,2048]{2,1,0:T(8,128)(2,1)S(1)}, u32[]{:S(2)}, u32[]{:S(2)}) collective-permute-start(bf16[2,128,2048]{2,1,0:T(8,128)(2,1)S(1)} %copy-done.77), channel_id=1, source_target_pairs={{1,0},{0,1},{3,2},{2,3},{5,4},{4,5},{7,6},{6,7},{9,8},{8,9},{11,10... | collective-permute-start | bytes 3145736 | tf_op jit(solution)/shard_map/att0_q/ppermute | solution.py:550
  179.4 36.5 %collective-permute-start.21 = (bf16[2,128,2048]{2,1,0:T(8,128)(2,1)S(1)}, bf16[2,128,2048]{2,1,0:T(8,128)(2,1)S(1)}, u32[]{:S(2)}, u32[]{:S(2)}) collective-permute-start(bf16[2,128,2048]{2,1,0:T(8,128)(2,1)S(1)} %copy-done.76), channel_id=1, source_target_pairs={{2,0},{0,2},{3,1},{1,3},{6,4},{4,6},{7,5},{5,7},{10,8},{8,10},{11,... | collective-permute-start | bytes 3145736 | tf_op jit(solution)/shard_map/att1_p/ppermute | solution.py:550
  179.6 34.1 %collective-permute-start.22 = (bf16[256,1024]{1,0:T(8,128)(2,1)S(1)}, bf16[256,1024]{1,0:T(8,128)(2,1)S(1)}, u32[]{:S(2)}, u32[]{:S(2)}) collective-permute-start(bf16[256,1024]{1,0:T(8,128)(2,1)S(1)} %copy-done.75), channel_id=1, source_target_pairs={{4,0},{0,4},{5,1},{1,5},{6,2},{2,6},{7,3},{3,7},{12,8},{8,12},{13,... | collective-permute-start | bytes 1572872 | tf_op jit(solution)/shard_map/wuB_h/ppermute | solution.py:550
  217.1 31.0 %collective-permute-start.27 = (bf16[512,1024]{1,0:T(8,128)(2,1)S(1)}, bf16[512,1024]{1,0:T(8,128)(2,1)S(1)}, u32[]{:S(2)}, u32[]{:S(2)}) collective-permute-start(bf16[512,1024]{1,0:T(8,128)(2,1)S(1)} %constant_dynamic-update-slice_fusion.2), channel_id=1, source_target_pairs={{16,0},{0,16},{17,1},{1,17},{18,2},{2,18},{19,3},{3,19},{20,4},{4,... | collective-permute-start | bytes 3145736 | tf_op jit(solution)/shard_map/wu1_x/ppermute | solution.py:550
  428.7 33.8 %collective-permute-start.48 = (bf16[2,128,2048]{2,1,0:T(8,128)(2,1)}, bf16[2,128,2048]{2,1,0:T(8,128)(2,1)}, u32[]{:S(2)}, u32[]{:S(2)}) collective-permute-start(bf16[2,128,2048]{2,1,0:T(8,128)(2,1)} %pad_maximum_fusion.16.refs_2_), channel_id=1, source_target_pairs={{1,0},{0,1},{3,2},{2,3},{5,4},{4,5},{7,6},{6,7},{9,8},{8,9},{11,10... | collective-permute-start | bytes 3145736 | tf_op jit(solution)/shard_map/datt0_q/ppermute | solution.py:550
  429.3 35.3 %collective-permute-start.49 = (bf16[2,128,2048]{2,1,0:T(8,128)(2,1)}, bf16[2,128,2048]{2,1,0:T(8,128)(2,1)}, u32[]{:S(2)}, u32[]{:S(2)}) collective-permute-start(bf16[2,128,2048]{2,1,0:T(8,128)(2,1)} %pad_maximum_fusion.17.refs_4_), channel_id=1, source_target_pairs={{2,0},{0,2},{3,1},{1,3},{6,4},{4,6},{7,5},{5,7},{10,8},{8,10},{11,... | collective-permute-start | bytes 3145736 | tf_op jit(solution)/shard_map/datt1_p/ppermute | solution.py:550
  429.6 32.9 %collective-permute-start.50 = (bf16[512,512]{1,0:T(8,128)(2,1)}, bf16[512,512]{1,0:T(8,128)(2,1)}, u32[]{:S(2)}, u32[]{:S(2)}) collective-permute-start(bf16[512,512]{1,0:T(8,128)(2,1)} %g_downA_sum.1), channel_id=1, source_target_pairs={{4,0},{0,4},{5,1},{1,5},{6,2},{2,6},{7,3},{3,7},{12,8},{8,12},{13,... | collective-permute-start | bytes 1572872 | tf_op jit(solution)/shard_map/g_downA_h/ppermute | solution.py:550
  464.6 39.0 %collective-permute-start.53 = (bf16[512,1024]{1,0:T(8,128)(2,1)}, bf16[512,1024]{1,0:T(8,128)(2,1)}, u32[]{:S(2)}, u32[]{:S(2)}) collective-permute-start(bf16[512,1024]{1,0:T(8,128)(2,1)} %get-tuple-element.453), channel_id=1, source_target_pairs={{16,0},{0,16},{17,1},{1,17},{18,2},{2,18},{19,3},{3,19},{20,4},{4,... | collective-permute-start | bytes 3145736 | tf_op jit(solution)/shard_map/g_upA_x/ppermute | solution.py:550
  465.1 41.1 %collective-permute-start.54 = (bf16[2,128,2048]{2,1,0:T(8,128)(2,1)}, bf16[2,128,2048]{2,1,0:T(8,128)(2,1)}, u32[]{:S(2)}, u32[]{:S(2)}) collective-permute-start(bf16[2,128,2048]{2,1,0:T(8,128)(2,1)} %get-tuple-element.456), channel_id=1, source_target_pairs={{1,0},{0,1},{3,2},{2,3},{5,4},{4,5},{7,6},{6,7},{9,8},{8,9},{11,10... | collective-permute-start | bytes 3145736 | tf_op jit(solution)/shard_map/ff0_q/ppermute | solution.py:550
  466.5 39.7 %collective-permute-start.55 = (bf16[2,128,2048]{2,1,0:T(8,128)(2,1)}, bf16[2,128,2048]{2,1,0:T(8,128)(2,1)}, u32[]{:S(2)}, u32[]{:S(2)}) collective-permute-start(bf16[2,128,2048]{2,1,0:T(8,128)(2,1)} %get-tuple-element.457), channel_id=1, source_target_pairs={{2,0},{0,2},{3,1},{1,3},{6,4},{4,6},{7,5},{5,7},{10,8},{8,10},{11,... | collective-permute-start | bytes 3145736 | tf_op jit(solution)/shard_map/ff1_p/ppermute | solution.py:550
  467.0 39.3 %collective-permute-start.52 = (bf16[512,512]{1,0:T(8,128)(2,1)}, bf16[512,512]{1,0:T(8,128)(2,1)}, u32[]{:S(2)}, u32[]{:S(2)}) collective-permute-start(bf16[512,512]{1,0:T(8,128)(2,1)} %g_downB_sum.1), channel_id=1, source_target_pairs={{4,0},{0,4},{5,1},{1,5},{6,2},{2,6},{7,3},{3,7},{12,8},{8,12},{13,... | collective-permute-start | bytes 1572872 | tf_op jit(solution)/shard_map/g_downB_h/ppermute | solution.py:550
  506.3 36.2 %collective-permute-start.56 = (bf16[2,128,2048]{2,1,0:T(8,128)(2,1)}, bf16[2,128,2048]{2,1,0:T(8,128)(2,1)}, u32[]{:S(2)}, u32[]{:S(2)}) collective-permute-start(bf16[2,128,2048]{2,1,0:T(8,128)(2,1)} %get-tuple-element.476), channel_id=1, source_target_pairs={{1,0},{0,1},{3,2},{2,3},{5,4},{4,5},{7,6},{6,7},{9,8},{8,9},{11,10... | collective-permute-start | bytes 3145736 | tf_op jit(solution)/shard_map/da0_q/ppermute | solution.py:550
  507.0 36.8 %collective-permute-start.57 = (bf16[2,128,2048]{2,1,0:T(8,128)(2,1)}, bf16[2,128,2048]{2,1,0:T(8,128)(2,1)}, u32[]{:S(2)}, u32[]{:S(2)}) collective-permute-start(bf16[2,128,2048]{2,1,0:T(8,128)(2,1)} %get-tuple-element.477), channel_id=1, source_target_pairs={{2,0},{0,2},{3,1},{1,3},{6,4},{4,6},{7,5},{5,7},{10,8},{8,10},{11,... | collective-permute-start | bytes 3145736 | tf_op jit(solution)/shard_map/da1_p/ppermute | solution.py:550
  508.2 34.3 %collective-permute-start.59 = (bf16[256,1024]{1,0:T(8,128)(2,1)}, bf16[256,1024]{1,0:T(8,128)(2,1)}, u32[]{:S(2)}, u32[]{:S(2)}) collective-permute-start(bf16[256,1024]{1,0:T(8,128)(2,1)} %get-tuple-element.487), channel_id=1, source_target_pairs={{4,0},{0,4},{5,1},{1,5},{6,2},{2,6},{7,3},{3,7},{12,8},{8,12},{13,... | collective-permute-start | bytes 1572872 | tf_op jit(solution)/shard_map/g_upA_h/ppermute | solution.py:550
  509.9 32.6 %collective-permute-start.60 = (bf16[512,512]{1,0:T(8,128)(2,1)}, bf16[512,512]{1,0:T(8,128)(2,1)}, u32[]{:S(2)}, u32[]{:S(2)}) collective-permute-start(bf16[512,512]{1,0:T(8,128)(2,1)} %get-tuple-element.493), channel_id=1, source_target_pairs={{16,0},{0,16},{17,1},{1,17},{18,2},{2,18},{19,3},{3,19},{20,4},{4,... | collective-permute-start | bytes 1572872 | tf_op jit(solution)/shard_map/g_downC_x/ppermute | solution.py:550
  633.7 47.3 %collective-permute-start.77 = (bf16[4,32,2048]{2,1,0:T(8,128)(2,1)S(1)}, bf16[4,32,2048]{2,1,0:T(8,128)(2,1)}, u32[]{:S(2)}, u32[]{:S(2)}) collective-permute-start(bf16[4,32,2048]{2,1,0:T(8,128)(2,1)S(1)} %get-tuple-element.569), channel_id=1, source_target_pairs={{4,0},{0,4},{5,1},{1,5},{6,2},{2,6},{7,3},{3,7},{12,8},{8,12},{13,... | collective-permute-start | bytes 1572872 | tf_op jit(solution)/shard_map/input_grad_h/ppermute | solution.py:550
  (134 other events, 1885.3 us)

commit v4 on v3

--- a/solution.py
+++ b/solution.py
@@ -99,11 +99,23 @@
         return self.refs[2 * jh + core][x, rows, columns]
 
 
+class Merged:
+    def __init__(self, refs):
+        self.refs = refs
+        x, rows, columns = refs[0].shape
+        self.shape = (x * rows, columns)
+
+    def block(self, jh, core, rows=slice(None), columns=slice(None)):
+        value = self.refs[2 * jh + core][:, :, columns]
+        return value.reshape(self.shape[0], value.shape[2])
+
+
 def attention_kernel(nh, nd, *refs):
     refs = Pieces(refs)
-    tokens, weights = refs.tokens(), Separate(refs.take(2 * nh), nd)
+    tokens, weights = refs.tokens(), Merged(refs.take(2 * nh))
     (a, qkv, o, probs), parts = refs.take(4), refs.parts()
     join_tokens(tokens, a)
+    nd = 2
     depth, block = weights.shape[0], weights.shape[1] // 4
     width = 3 * block
     inward = (slice(None), slice(0, width))
@@ -131,9 +143,10 @@
 
 def up_kernel(nh, nd, *refs):
     refs = Pieces(refs)
-    b_tokens, wu = refs.tokens(), Separate(refs.take(2 * nh), nd)
+    b_tokens, wu = refs.tokens(), Merged(refs.take(2 * nh))
     b, hidden, slope = refs.take(3)
     join_tokens(b_tokens, b)
+    nd = 2
     depth, width = wu.shape
     kinds, length = b.shape[1], b.shape[2]
     chunk = min(width, 512)
@@ -157,10 +170,10 @@
 def up_back_kernel(nh, nd, *refs):
     refs = Pieces(refs)
     df_tokens, (slope,) = refs.tokens(), refs.take(1)
-    wu, wd = (Separate(refs.take(2 * nh), nd) for _ in range(2))
+    wu, wd = Merged(refs.take(2 * nh)), Separate(refs.take(2 * nh), nd)
     (df, du), parts = refs.take(2), refs.parts()
     join_tokens(df_tokens, df)
-    depth, width = wu.shape
+    width, depth = wd.shape
     kinds, length = df.shape[1], df.shape[2]
     chunk = min(width, 512)
     for jh in range(nh):
@@ -173,7 +186,8 @@
             cols = slice(jh * width + c, jh * width + c + chunk)
             value = dh * rows_of(slope, cols).astype(F32)
             du[0, :, :, cols] = value.astype(BF).reshape(kinds, length, chunk)
-    for d in range(nd):
+    depth = wu.shape[0]
+    for d in range(2):
         total = dot(rows_of(du, slice(0, width)), wu.block(0, d), (1, 1))
         for jh in range(1, nh):
             total += dot(rows_of(du, slice(jh * width, (jh + 1) * width)), wu.block(jh, d), (1, 1))
@@ -195,11 +209,12 @@
 def attention_back_kernel(nh, nd, *refs):
     refs = Pieces(refs)
     (a, o), tokens, (qkv, probs) = refs.take(2), refs.tokens(), refs.take(2)
-    weights = Separate(refs.take(2 * nh), nd)
+    weights = Merged(refs.take(2 * nh))
     parts, (all_datt, all_dqkv, sent) = refs.parts(), refs.take(3)
     step = pl.program_id(0)
     datt, dqkv = (v.at[pl.ds(step, 1)] for v in (all_datt, all_dqkv))
     join_tokens(tokens, datt)
+    nd = 2
     depth, block = weights.shape[0], weights.shape[1] // 4
     width = 3 * block
     inward = (slice(None), slice(0, width))
@@ -293,6 +308,59 @@
     return [v.reshape(shape) for v, (shape, _) in zip(made, outs)]
 
 
+def move_call(kernel, name, table, arrays, outs):
+    def whole(shape):
+        zeros = (0,) * len(shape)
+        return pl.BlockSpec(tuple(shape), lambda i, table: zeros)
+
+    return pl.pallas_call(
+        kernel,
+        name=name,
+        grid_spec=pltpu.PrefetchScalarGridSpec(
+            num_scalar_prefetch=1,
+            grid=(1,),
+            in_specs=[whole(v.shape) for v in arrays],
+            out_specs=[whole(shape) for shape, _ in outs],
+        ),
+        out_shape=[jax.ShapeDtypeStruct(shape, dtype) for shape, dtype in outs],
+        compiler_params=pltpu.CompilerParams(vmem_limit_bytes=32 * 2**20),
+        cost_estimate=pl.CostEstimate(flops=0, bytes_accessed=0, transcendentals=0),
+    )(table, *arrays)
+
+
+def leave_home(name, table, groups, v):
+    slots, t, D = v.shape
+    blocks, images = table.shape[0] - groups, slots // groups
+    width = D // blocks
+
+    def kernel(table, v, *outs):
+        for jh in range(groups):
+            picked = pl.ds(table[jh] * images, images)
+            for e in range(blocks):
+                columns = pl.ds(pl.multiple_of(table[groups + e] * width, width), width)
+                outs[jh][:, :, e * width : (e + 1) * width] = v[picked, :, columns].astype(BF)
+
+    return move_call(kernel, name, table, [v], [((images, t, D), BF)] * groups)
+
+
+def come_home(name, table, groups, own, received, dtype):
+    images, length, D = own.shape
+    blocks, t = table.shape[0] - groups, length // groups
+    width = D // blocks
+
+    def kernel(table, own, *refs):
+        *received, out = refs
+        for jh in range(groups):
+            picked = pl.ds(table[jh] * images, images)
+            for e in range(blocks):
+                columns = pl.ds(pl.multiple_of(table[groups + e] * width, width), width)
+                part = received[jh - 1][:, :, columns] if jh else own[:, :t, columns]
+                out[picked, :, e * width : (e + 1) * width] = part.astype(dtype)
+
+    shape = (images * groups, t, D)
+    return move_call(kernel, name, table, [own, *received], [(shape, dtype)])[0]
+
+
 def row_parts(values):
     center = values - jnp.mean(values, axis=-1, keepdims=True)
     factor = lax.rsqrt(jnp.mean(center * center, axis=-1, keepdims=True) + 1e-06)
@@ -357,6 +425,24 @@
         out[kind, 0] = (residual[kind, 0] + mod[kind, 0, 5:6] * token_sum(sums, kind)).astype(BF)
 
 
+def rounded(weights):
+    def kernel(*refs):
+        for source, copy in zip(refs[: len(weights)], refs[len(weights) :]):
+            copy[...] = source[...].astype(BF)
+
+    halves = [pl.BlockSpec((v.shape[0] // 2, v.shape[1]), lambda i: (i, 0)) for v in weights]
+    return pl.pallas_call(
+        kernel,
+        name="rounded",
+        grid=(2,),
+        in_specs=halves,
+        out_specs=halves,
+        out_shape=[jax.ShapeDtypeStruct(v.shape, BF) for v in weights],
+        compiler_params=pltpu.CompilerParams(vmem_limit_bytes=32 * 2**20),
+        cost_estimate=pl.CostEstimate(flops=0, bytes_accessed=0, transcendentals=0),
+    )(*weights)
+
+
 def pack_attention_weights(w_qkv, w_out):
     depth, _, block = w_qkv.shape
 
@@ -370,6 +456,7 @@
         name="pack",
         out_shape=jax.ShapeDtypeStruct((depth, 4 * block), BF),
         compiler_params=pltpu.CompilerParams(vmem_limit_bytes=32 * 2**20),
+        cost_estimate=pl.CostEstimate(flops=0, bytes_accessed=0, transcendentals=0),
     )(w_qkv.transpose(1, 0, 2), w_out)
 
 
@@ -574,13 +661,14 @@
             for jh in range(1, self.H)
         ]
 
-    def for_groups(self, v):
-        here = lax.axis_index("h")
-        images = v.shape[0] // self.H
-        return [
-            lax.dynamic_slice_in_dim(v, ((here - jh) % self.H) * images, images, axis=0)
-            for jh in range(self.H)
+    def tables(self):
+        x, core, h = (lax.axis_index(axis) for axis in self.axes[:3])
+        groups = [(h - jh) % self.H for jh in range(self.H)]
+        here = [
+            ((x + jx) % self.X) * 2 + (core ^ jc) for jc in range(2) for jx in range(self.X)
         ]
+        home = [((e % 2) ^ core) * self.X + (e // 2 - x) % self.X for e in range(self.n_dp)]
+        return [jnp.stack(groups + rest).astype(jnp.int32) for rest in (here, home)]
 
     def to_group(self, parts, name):
         return [self.from_h(parts[jh], jh, name) for jh in range(1, self.H)]
@@ -590,17 +678,6 @@
         return [
             self.from_h(v[:, jh * tokens : (jh + 1) * tokens], -jh, name) for jh in range(1, self.H)
         ]
-
-    def at_home(self, v, received):
-        here = lax.axis_index("h")
-        images = v.shape[0]
-        tokens = v.shape[1] // self.H
-        out = jnp.zeros((images * self.H, tokens, v.shape[2]), v.dtype)
-        for jh, part in enumerate([v[:, :tokens], *received]):
-            out = lax.dynamic_update_slice_in_dim(
-                out, part, ((here - jh) % self.H) * images, axis=0
-            )
-        return self.features_home(out)
 
     def over(self, v, kind, late, name):
         return self.shifted(v, "p" if (kind == 0) != late else "q", 2, 1, f"{name}{kind}")
@@ -630,22 +707,6 @@
                 )
                 for jc in range(2)
                 for jx in range(self.X)
-            ],
-            axis=-1,
-        )
-
-    def features_home(self, v):
-        x, c = lax.axis_index("x"), lax.axis_index("core")
-        width = v.shape[-1] // self.n_dp
-        return jnp.concatenate(
-            [
-                lax.dynamic_slice_in_dim(
-                    v,
-                    (((e % 2) ^ c) * self.X + (e // 2 - x) % self.X) * width,
-                    width,
-                    axis=v.ndim - 1,
-                )
-                for e in range(self.n_dp)
             ],
             axis=-1,
         )
@@ -739,13 +800,14 @@
     def total(here, there):
         return here + sum(v.astype(F32) for v in there)
 
-    stream_parts = links.for_groups(links.features_here(stream_in))
+    leave, come = links.tables()
+    stream_parts = leave_home("stream_leaves", leave, H, stream_in)
     packed = pack_attention_weights(w_qkv, w_out)
     stream_got = links.to_group(stream_parts, "stream")
     x_packed = links.over_x(packed, "wqo0")
-    up, down = w_up.astype(BF), w_down.astype(BF)
-    stream_parts, stream_got, x_packed, packed, up = sync(
-        stream_parts, stream_got, x_packed, packed, up
+    up, down = rounded([w_up, w_down])
+    stream_parts, stream_got, x_packed, packed, up, down = sync(
+        stream_parts, stream_got, x_packed, packed, up, down
     )
 
     stream = jnp.concatenate([stream_parts[0], *stream_got], axis=1)
@@ -762,7 +824,7 @@
     a_far = links.last_hop(a_near, "a")
     far_two = links.over_h(packed_two, "wqoB")
     x_one = [links.over_x(w, "wqoA1") for w in far_one]
-    cot_parts = links.for_groups(links.features_here(cotangent.astype(BF)))
+    cot_parts = leave_home("cot_leaves", leave, H, cotangent)
     cot_one = [v[:steps] for v in cot_parts]
     cot_two = [v[steps:] for v in cot_parts]
     wu = [jnp.stack([up, *x_up])]
@@ -972,8 +1034,8 @@
     grad_norm = jnp.sqrt(links.total(squares))
     grad_norm, output = sync(grad_norm, output)
     output_got = links.leave_group(output, "output")
-    input_grad = links.at_home(input_grad, input_grad_got).astype(F32)
-    output = links.at_home(output, output_got)
+    input_grad = come_home("input_grad_home", come, H, input_grad, input_grad_got, F32)
+    output = come_home("output_home", come, H, output, output_got, BF)
     factor = jnp.minimum(1.0, clip_limit / (grad_norm + 1e-06))
     one_qkv, two_qkv, new_qkv = (
         v.transpose(1, 0, 2)

time: 703 us -> 694 us (0.987)
  other arithmetic: 59.8 us -> 43.8 us
    unnamed x161 -> x191, local copies, waits for them, and re-layouts: 23.1 us -> 32.2 us
    convert_element_type x4 -> x0, other arithmetic: 8.13 us -> none  [the longest x2 3.85 us: per_device(): up, down = (w_up.astype(BF), w_down.astype(BF))]
  transfers between devices with their start and end apart: 78 -> 78, of which waited for: 38 -> 37; matrix products, arithmetic and copies ran while one was open for 10% -> 7% of each run, Pallas kernels for 24% -> 25%
where the time goes in v4:
time: 694 us; the launch traced here: 684 us
  waiting for transfers between devices  301 us (43%)
  Pallas kernels  200 us (29%)
  starting transfers between devices  86.5 us (12%)
  other arithmetic  43.8 us (6%)
  local copies, waits for them, and re-layouts  43.6 us (6%)
  between operations  9.3 us (1%)
    ppermute x73, waiting for transfers between devices, shifted(): lax.ppermute(v, axis, [((dst + offset) % size, dst) for dst in range(size)])  289 us
    pallas_call x5, Pallas kernels, group_call(): pl.pallas_call(lambda *refs: kernel(nh, nd, *refs), name=name, grid=(step...  114 us
    ppermute x73, starting transfers between devices, shifted(): lax.ppermute(v, axis, [((dst + offset) % size, dst) for dst in range(size)])  73.9 us
    pallas_call x7, Pallas kernels, one_step(): pl.pallas_call(kernel, name=name, grid=(1,), in_specs=[pl.BlockSpec((v.sh...  40.3 us
    unnamed x191, local copies, waits for them, and re-layouts  32.2 us
    pallas_call x10, Pallas kernels, image_call(): pl.pallas_call(kernel, name=name, grid=(steps,), in_specs=[cut(seen(v.sha...  20.8 us
    pallas_call x2, Pallas kernels, gradient(): pl.pallas_call(kernel, name=name, grid=(nh, half), in_specs=in_specs, out...  15.9 us
  transfers between devices with their start and end apart: 78, of which 37 were waited for; matrix products, arithmetic and copies ran while one was open for 7% of the time, Pallas kernels for 25%

profile of v4, /device:TPU:0, one launch (start us, length us, event | category | flops | bytes accessed | tf_op | source)
XLA Modules:
  0.0 684.1 jit_solution(12750043833409738744)
XLA Ops:
  16.8 18.9 %collective-permute-done = bf16[4,32,2048]{2,1,0:T(8,128)(2,1)} collective-permute-done((bf16[4,32,2048]{2,1,0:T(8,128)(2,1)}, bf16[4,32,2048]{2,1,0:T(8,128)(2,1)}, u32[]{:S(2)}, u32[]{:S(2)}) %collective-permute-start) | collective-permute-done | bytes 524320 | tf_op jit(solution)/shard_map/stream_h/ppermute | solution.py:637
  45.7 15.0 %collective-permute-done.2 = bf16[2,64,2048]{2,1,0:T(8,128)(2,1)S(1)} collective-permute-done((bf16[2,64,2048]{2,1,0:T(8,128)(2,1)S(1)}, bf16[2,64,2048]{2,1,0:T(8,128)(2,1)S(1)}, u32[]{:S(2)}, u32[]{:S(2)}) %collective-permute-start.2) | collective-permute-done | bytes 524320 | tf_op jit(solution)/shard_map/a0_p/ppermute | solution.py:637
  72.8 27.1 %collective-permute-done.8 = bf16[256,1024]{1,0:T(8,128)(2,1)S(1)} collective-permute-done((bf16[256,1024]{1,0:T(8,128)(2,1)S(1)}, bf16[256,1024]{1,0:T(8,128)(2,1)S(1)}, u32[]{:S(2)}, u32[]{:S(2)}) %collective-permute-start.8) | collective-permute-done | bytes 524320 | tf_op jit(solution)/shard_map/wqoB_h/ppermute | solution.py:637
  105.5 12.7 %collective-permute-done.11 = bf16[2,32,2048]{2,1,0:T(8,128)(2,1)S(1)} collective-permute-done((bf16[2,32,2048]{2,1,0:T(8,128)(2,1)S(1)}, bf16[2,32,2048]{2,1,0:T(8,128)(2,1)S(1)}, u32[]{:S(2)}, u32[]{:S(2)}) %collective-permute-start.11) | collective-permute-done | bytes 262176 | tf_op jit(solution)/shard_map/cotA_h/ppermute | solution.py:637
  124.3 14.2 %collective-permute-done.14 = bf16[2,32,2048]{2,1,0:T(8,128)(2,1)S(1)} collective-permute-done((bf16[2,32,2048]{2,1,0:T(8,128)(2,1)S(1)}, bf16[2,32,2048]{2,1,0:T(8,128)(2,1)S(1)}, u32[]{:S(2)}, u32[]{:S(2)}) %collective-permute-start.14) | collective-permute-done | bytes 262176 | tf_op jit(solution)/shard_map/cotB_h/ppermute | solution.py:637
  145.7 18.0 %attention.1 = (bf16[2,2,256,2048]{3,2,1,0:T(8,128)(2,1)}, bf16[2,2,256,1536]{3,2,1,0:T(8,128)(2,1)}, bf16[2,2,256,512]{3,2,1,0:T(8,128)(2,1)}, bf16[2,2,4,256,2...) custom-call(bf16[2,128,2048]{2,1,0:T(8,128)(2,1)} %copy-done.66, ...), custom_call_target="tpu_custom_call" | custom-call | tf_op jit(solution)/shard_map/attention/pallas_call | solution.py:274
  177.8 30.2 %collective-permute-done.22 = bf16[256,1024]{1,0:T(8,128)(2,1)S(1)} collective-permute-done((bf16[256,1024]{1,0:T(8,128)(2,1)S(1)}, bf16[256,1024]{1,0:T(8,128)(2,1)S(1)}, u32[]{:S(2)}, u32[]{:S(2)}) %collective-permute-start.22) | collective-permute-done | bytes 524320 | tf_op jit(solution)/shard_map/wuB_h/ppermute | solution.py:637
  216.8 16.8 %collective-permute-done.24.refs_4_ = bf16[2,64,2048]{2,1,0:T(8,128)(2,1)S(1)} collective-permute-done((bf16[2,64,2048]{2,1,0:T(8,128)(2,1)S(1)}, bf16[2,64,2048]{2,1,0:T(8,128)(2,1)S(1)}, u32[]{:S(2)}, u32[]{:S(2)}) %collective-permute-start.24) | collective-permute-done | bytes 524320 | tf_op jit(solution)/shard_map/att0_p/ppermute | solution.py:637
  245.0 15.3 %collective-permute-done.28 = bf16[2,64,2048]{2,1,0:T(8,128)(2,1)S(1)} collective-permute-done((bf16[2,64,2048]{2,1,0:T(8,128)(2,1)S(1)}, bf16[2,64,2048]{2,1,0:T(8,128)(2,1)S(1)}, u32[]{:S(2)}, u32[]{:S(2)}) %collective-permute-start.28) | collective-permute-done | bytes 524320 | tf_op jit(solution)/shard_map/b0_p/ppermute | solution.py:637
  267.5 12.5 %collective-permute-done.34 = bf16[512,512]{1,0:T(8,128)(2,1)S(1)} collective-permute-done((bf16[512,512]{1,0:T(8,128)(2,1)S(1)}, bf16[512,512]{1,0:T(8,128)(2,1)S(1)}, u32[]{:S(2)}, u32[]{:S(2)}) %collective-permute-start.34) | collective-permute-done | bytes 524320 | tf_op jit(solution)/shard_map/wdB1_x/ppermute | solution.py:637
  280.0 10.8 %collective-permute-done.32.refs_1_ = bf16[2,128,2048]{2,1,0:T(8,128)(2,1)S(1)} collective-permute-done((bf16[2,128,2048]{2,1,0:T(8,128)(2,1)S(1)}, bf16[2,128,2048]{2,1,0:T(8,128)(2,1)S(1)}, u32[]{:S(2)}, u32[]{:S(2)}) %collective-permute-start.32) | collective-permute-done | bytes 1048608 | tf_op jit(solution)/shard_map/b0_q/ppermute | solution.py:637
  295.9 19.5 %up.1 = (bf16[2,2,256,2048]{3,2,1,0:T(8,128)(2,1)}, bf16[2,2,256,2048]{3,2,1,0:T(8,128)(2,1)}, bf16[2,2,256,2048]{3,2,1,0:T(8,128)(2,1)}) custom-call(bf16[2,128,2048]{2,1,0:T(8,128)(2,1)} %copy-done.68, bf16[2,128,2048]{2,1,0:T(8,128)(2,1)} %copy-done.82, bf16[2,128,2048]{2,1,0:T(8,128)(2,1)} %copy-done.69, bf16[2,128,2048]{2,1,0:T(8,128)(2,1)} %copy-done.83, ...), custom_call_target="tpu_custom_call" | custom-call | tf_op jit(solution)/shard_map/up/pallas_call | solution.py:274
  321.2 26.6 %up_back.1 = (bf16[2,2,256,2048]{3,2,1,0:T(8,128)(2,1)}, bf16[2,2,256,2048]{3,2,1,0:T(8,128)(2,1)}, bf16[2,128,2048]{2,1,0:T(8,128)(2,1)}, bf16[2,128,2048]{2,1,...) custom-call(bf16[2,128,2048]{2,1,0:T(8,128)(2,1)} %pad_maximum_fusion.10.refs_0_, ...), custom_call_target="tpu_custom_call" | custom-call | tf_op jit(solution)/shard_map/up_back/pallas_call | solution.py:274
  365.2 8.0 %g_down_send.1 = bf16[2048,1024]{1,0:T(8,128)(2,1)S(1)} custom-call(bf16[1024,2048]{1,0:T(8,128)(2,1)} %bitcast.101, bf16[1024,2048]{1,0:T(8,128)(2,1)} %bitcast.109), custom_call_target="tpu_custom_call" | custom-call | tf_op jit(solution)/shard_map/g_down_send/pallas_call | solution.py:479
  382.4 9.7 %g_down_keep.1 = (bf16[512,512]{1,0:T(8,128)(2,1)}, bf16[1024,512]{1,0:T(8,128)(2,1)}, bf16[512,512]{1,0:T(8,128)(2,1)}, bf16[512,512]{1,0:T(8,128)(2,1)}, bf16[...) custom-call(bf16[1024,2048]{1,0:T(8,128)(2,1)} %bitcast.102, bf16[1024,2048]{1,0:T(8,128)(2,1)} %bitcast.110, ...), custom_call_target="tpu_custom_call" | custom-call | tf_op jit(solution)/shard_map/g_down_keep/pallas_call | solution.py:492
  424.4 14.3 %down.1 = (bf16[2,128,2048]{2,1,0:T(8,128)(2,1)}, bf16[2,128,2048]{2,1,0:T(8,128)(2,1)}, bf16[2,128,2048]{2,1,0:T(8,128)(2,1)}, bf16[2,128,2048]{2,1,0:T(8,128)(2,1)}) custom-call(bf16[2,2,256,2048]{3,2,1,0:T(8,128)(2,1)} %get-tuple-element.460.refs_0_, bf16[2,1024,512]{2,1,0:T(8,128)(2,1)} %copy-done.53, bf16[2,1024,512]{2,1,0:T(8,128)(2,1)} %copy-done.60, ...), custom_call_target="tpu_custom_call" | custom-call | tf_op jit(solution)/shard_map/down/pallas_call | solution.py:274
  438.7 9.6 %g_up_keep.1 = (bf16[512,1024]{1,0:T(8,128)(2,1)}, bf16[512,1024]{1,0:T(8,128)(2,1)}, bf16[512,1024]{1,0:T(8,128)(2,1)}, bf16[512,1024]{1,0:T(8,128)(2,1)}) custom-call(bf16[1024,2048]{1,0:T(8,128)(2,1)} %bitcast.106, bf16[1024,2048]{1,0:T(8,128)(2,1)} %bitcast.108, bf16[1024,2048]{1,0:T(8,128)(2,1)} %collective-permute-done.47.sent), custom_call_target="tpu_custom_call" | custom-call | tf_op jit(solution)/shard_map/g_up_keep/pallas_call | solution.py:492
  462.4 35.2 %attention_back.1 = (bf16[2,128,2048]{2,1,0:T(8,128)(2,1)}, bf16[2,128,2048]{2,1,0:T(8,128)(2,1)}, bf16[2,128,2048]{2,1,0:T(8,128)(2,1)}, bf16[2,128,2048]{2,1,0...) custom-call(bf16[2048,1024]{1,0:T(8,128)(2,1)} %bitcast.103, ...), custom_call_target="tpu_custom_call" | custom-call | tf_op jit(solution)/shard_map/attention_back/pallas_call | solution.py:274
  509.7 11.2 %g_att_keep.1 = (bf16[512,1024]{1,0:T(8,128)(2,1)}, bf16[512,1024]{1,0:T(8,128)(2,1)}, bf16[512,1024]{1,0:T(8,128)(2,1)}, bf16[512,1024]{1,0:T(8,128)(2,1)}) custom-call(bf16[2048,1024]{1,0:T(8,128)(2,1)} %bitcast.104, bf16[1024,1536]{1,0:T(8,128)(2,1)} %bitcast.115, bf16[1024,2048]{1,0:T(8,128)(2,1)} %bitcast.114, bf16[1024,512]{1,0:T(8,128)(2,1)} %bitcast.111, ...), custom_call_target="tpu_custom_call" | custom-call | tf_op jit(solution)/shard_map/g_att_keep/pallas_call | solution.py:492
  520.9 17.1 %collective-permute-done.59 = bf16[256,1024]{1,0:T(8,128)(2,1)S(1)} collective-permute-done((bf16[256,1024]{1,0:T(8,128)(2,1)}, bf16[256,1024]{1,0:T(8,128)(2,1)S(1)}, u32[]{:S(2)}, u32[]{:S(2)}) %collective-permute-start.59) | collective-permute-done | bytes 524320 | tf_op jit(solution)/shard_map/g_upA_h/ppermute | solution.py:637
  545.2 18.5 %collective-permute-done.61.refs_1_ = bf16[512,1024]{1,0:T(8,128)(2,1)} collective-permute-done((bf16[512,1024]{1,0:T(8,128)(2,1)}, bf16[512,1024]{1,0:T(8,128)(2,1)}, u32[]{:S(2)}, u32[]{:S(2)}) %collective-permute-start.61) | collective-permute-done | bytes 1048608 | tf_op jit(solution)/shard_map/g_attA_x/ppermute | solution.py:637
  578.8 13.6 %collective-permute-done.65 = bf16[256,1024]{1,0:T(8,128)(2,1)S(1)} collective-permute-done((bf16[256,1024]{1,0:T(8,128)(2,1)}, bf16[256,1024]{1,0:T(8,128)(2,1)S(1)}, u32[]{:S(2)}, u32[]{:S(2)}) %collective-permute-start.65) | collective-permute-done | bytes 524320 | tf_op jit(solution)/shard_map/g_attA_h/ppermute | solution.py:637
  608.3 11.1 %collective-permute-done.69 = bf16[256,1024]{1,0:T(8,128)(2,1)S(1)} collective-permute-done((bf16[256,1024]{1,0:T(8,128)(2,1)}, bf16[256,1024]{1,0:T(8,128)(2,1)S(1)}, u32[]{:S(2)}, u32[]{:S(2)}) %collective-permute-start.69) | collective-permute-done | bytes 524320 | tf_op jit(solution)/shard_map/g_attB_h/ppermute | solution.py:637
  645.6 8.0 %collective-permute-done.75 = f32[]{:T(128)} collective-permute-done((f32[]{:T(128)}, f32[]{:T(128)}, u32[]{:S(2)}, u32[]{:S(2)}) %collective-permute-start.75) | collective-permute-done | bytes 36 | tf_op jit(solution)/shard_map/norm/ppermute | solution.py:719
  (403 shorter events, 280.9 us)
Async XLA Ops:
  3.4 32.4 %collective-permute-start.1 = (bf16[512,1024]{1,0:T(8,128)(2,1)S(1)}, bf16[512,1024]{1,0:T(8,128)(2,1)}, u32[]{:S(2)}, u32[]{:S(2)}) collective-permute-start(bf16[512,1024]{1,0:T(8,128)(2,1)S(1)} %pack.1), channel_id=1, source_target_pairs={{16,0},{0,16},{17,1},{1,17},{18,2},{2,18},{19,3},{3,19},{20,4},{4,... | collective-permute-start | bytes 3145736 | tf_op jit(solution)/shard_map/wqo0_x/ppermute | solution.py:637
  35.8 31.0 %collective-permute-start.5 = (bf16[512,1024]{1,0:T(8,128)(2,1)S(1)}, bf16[512,1024]{1,0:T(8,128)(2,1)S(1)}, u32[]{:S(2)}, u32[]{:S(2)}) collective-permute-start(bf16[512,1024]{1,0:T(8,128)(2,1)S(1)} %get-tuple-element.300), channel_id=1, source_target_pairs={{16,0},{0,16},{17,1},{1,17},{18,2},{2,18},{19,3},{3,19},{20,4},{4,... | collective-permute-start | bytes 3145736 | tf_op jit(solution)/shard_map/wu0_x/ppermute | solution.py:637
  66.8 33.1 %collective-permute-start.6 = (bf16[2,128,2048]{2,1,0:T(8,128)(2,1)S(1)}, bf16[2,128,2048]{2,1,0:T(8,128)(2,1)S(1)}, u32[]{:S(2)}, u32[]{:S(2)}) collective-permute-start(bf16[2,128,2048]{2,1,0:T(8,128)(2,1)S(1)} %pad_maximum_fusion.7.refs_0_), channel_id=1, source_target_pairs={{1,0},{0,1},{3,2},{2,3},{5,4},{4,5},{7,6},{6,7},{9,8},{8,9},{11,10... | collective-permute-start | bytes 3145736 | tf_op jit(solution)/shard_map/a0_q/ppermute | solution.py:637
  67.3 34.4 %collective-permute-start.7 = (bf16[2,128,2048]{2,1,0:T(8,128)(2,1)S(1)}, bf16[2,128,2048]{2,1,0:T(8,128)(2,1)S(1)}, u32[]{:S(2)}, u32[]{:S(2)}) collective-permute-start(bf16[2,128,2048]{2,1,0:T(8,128)(2,1)S(1)} %pad_maximum_fusion.8.refs_2_), channel_id=1, source_target_pairs={{2,0},{0,2},{3,1},{1,3},{6,4},{4,6},{7,5},{5,7},{10,8},{8,10},{11,... | collective-permute-start | bytes 3145736 | tf_op jit(solution)/shard_map/a1_p/ppermute | solution.py:637
  67.9 32.0 %collective-permute-start.8 = (bf16[256,1024]{1,0:T(8,128)(2,1)S(1)}, bf16[256,1024]{1,0:T(8,128)(2,1)S(1)}, u32[]{:S(2)}, u32[]{:S(2)}) collective-permute-start(bf16[256,1024]{1,0:T(8,128)(2,1)S(1)} %get-tuple-element.305), channel_id=1, source_target_pairs={{4,0},{0,4},{5,1},{1,5},{6,2},{2,6},{7,3},{3,7},{12,8},{8,12},{13,... | collective-permute-start | bytes 1572872 | tf_op jit(solution)/shard_map/wqoB_h/ppermute | solution.py:637
  71.0 28.9 %collective-permute-start.9 = (bf16[256,1024]{1,0:T(8,128)(2,1)S(1)}, bf16[256,1024]{1,0:T(8,128)(2,1)S(1)}, u32[]{:S(2)}, u32[]{:S(2)}) collective-permute-start(bf16[256,1024]{1,0:T(8,128)(2,1)S(1)} %collective-permute-done.4), channel_id=1, source_target_pairs={{16,0},{0,16},{17,1},{1,17},{18,2},{2,18},{19,3},{3,19},{20,4},{4,... | collective-permute-start | bytes 1572872 | tf_op jit(solution)/shard_map/wqoA1_x/ppermute | solution.py:637
  138.5 30.9 %collective-permute-start.19 = (bf16[1024,512]{1,0:T(8,128)(2,1)}, bf16[1024,512]{1,0:T(8,128)(2,1)}, u32[]{:S(2)}, u32[]{:S(2)}) collective-permute-start(bf16[1024,512]{1,0:T(8,128)(2,1)} %get-tuple-element.359), channel_id=1, source_target_pairs={{16,0},{0,16},{17,1},{1,17},{18,2},{2,18},{19,3},{3,19},{20,4},{4,... | collective-permute-start | bytes 3145736 | tf_op jit(solution)/shard_map/wd0_x/ppermute | solution.py:637
  171.3 38.9 %collective-permute-start.23 = (bf16[2,1024,512]{2,1,0:T(8,128)(2,1)S(1)}, bf16[2,1024,512]{2,1,0:T(8,128)(2,1)S(1)}, u32[]{:S(2)}, u32[]{:S(2)}) collective-permute-start(bf16[2,1024,512]{2,1,0:T(8,128)(2,1)S(1)} %pad_maximum_fusion.3.refs_9_.refs_1_), channel_id=1, source_target_pairs={{8,0},{0,8},{9,1},{1,9},{10,2},{2,10},{11,3},{3,11},{12,4},{4,12},... | collective-permute-start | bytes 6291464 | tf_op jit(solution)/shard_map/wd0_core/ppermute | solution.py:637
  171.4 36.6 %collective-permute-start.20 = (bf16[2,128,2048]{2,1,0:T(8,128)(2,1)S(1)}, bf16[2,128,2048]{2,1,0:T(8,128)(2,1)S(1)}, u32[]{:S(2)}, u32[]{:S(2)}) collective-permute-start(bf16[2,128,2048]{2,1,0:T(8,128)(2,1)S(1)} %copy-done.92), channel_id=1, source_target_pairs={{1,0},{0,1},{3,2},{2,3},{5,4},{4,5},{7,6},{6,7},{9,8},{8,9},{11,10... | collective-permute-start | bytes 3145736 | tf_op jit(solution)/shard_map/att0_q/ppermute | solution.py:637
  173.8 36.5 %collective-permute-start.21 = (bf16[2,128,2048]{2,1,0:T(8,128)(2,1)S(1)}, bf16[2,128,2048]{2,1,0:T(8,128)(2,1)S(1)}, u32[]{:S(2)}, u32[]{:S(2)}) collective-permute-start(bf16[2,128,2048]{2,1,0:T(8,128)(2,1)S(1)} %copy-done.91), channel_id=1, source_target_pairs={{2,0},{0,2},{3,1},{1,3},{6,4},{4,6},{7,5},{5,7},{10,8},{8,10},{11,... | collective-permute-start | bytes 3145736 | tf_op jit(solution)/shard_map/att1_p/ppermute | solution.py:637
  173.8 34.3 %collective-permute-start.22 = (bf16[256,1024]{1,0:T(8,128)(2,1)S(1)}, bf16[256,1024]{1,0:T(8,128)(2,1)S(1)}, u32[]{:S(2)}, u32[]{:S(2)}) collective-permute-start(bf16[256,1024]{1,0:T(8,128)(2,1)S(1)} %copy-done.89), channel_id=1, source_target_pairs={{4,0},{0,4},{5,1},{1,5},{6,2},{2,6},{7,3},{3,7},{12,8},{8,12},{13,... | collective-permute-start | bytes 1572872 | tf_op jit(solution)/shard_map/wuB_h/ppermute | solution.py:637
  210.3 29.8 %collective-permute-start.27 = (bf16[512,1024]{1,0:T(8,128)(2,1)S(1)}, bf16[512,1024]{1,0:T(8,128)(2,1)S(1)}, u32[]{:S(2)}, u32[]{:S(2)}) collective-permute-start(bf16[512,1024]{1,0:T(8,128)(2,1)S(1)} %constant_dynamic-update-slice_fusion), channel_id=1, source_target_pairs={{16,0},{0,16},{17,1},{1,17},{18,2},{2,18},{19,3},{3,19},{20,4},{4,... | collective-permute-start | bytes 3145736 | tf_op jit(solution)/shard_map/wu1_x/ppermute | solution.py:637
  421.0 35.9 %collective-permute-start.48 = (bf16[2,128,2048]{2,1,0:T(8,128)(2,1)}, bf16[2,128,2048]{2,1,0:T(8,128)(2,1)}, u32[]{:S(2)}, u32[]{:S(2)}) collective-permute-start(bf16[2,128,2048]{2,1,0:T(8,128)(2,1)} %pad_maximum_fusion.14.refs_2_), channel_id=1, source_target_pairs={{1,0},{0,1},{3,2},{2,3},{5,4},{4,5},{7,6},{6,7},{9,8},{8,9},{11,10... | collective-permute-start | bytes 3145736 | tf_op jit(solution)/shard_map/datt0_q/ppermute | solution.py:637
  422.4 35.3 %collective-permute-start.49 = (bf16[2,128,2048]{2,1,0:T(8,128)(2,1)}, bf16[2,128,2048]{2,1,0:T(8,128)(2,1)}, u32[]{:S(2)}, u32[]{:S(2)}) collective-permute-start(bf16[2,128,2048]{2,1,0:T(8,128)(2,1)} %pad_maximum_fusion.15.refs_4_), channel_id=1, source_target_pairs={{2,0},{0,2},{3,1},{1,3},{6,4},{4,6},{7,5},{5,7},{10,8},{8,10},{11,... | collective-permute-start | bytes 3145736 | tf_op jit(solution)/shard_map/datt1_p/ppermute | solution.py:637
  424.1 32.8 %collective-permute-start.50 = (bf16[512,512]{1,0:T(8,128)(2,1)}, bf16[512,512]{1,0:T(8,128)(2,1)S(1)}, u32[]{:S(2)}, u32[]{:S(2)}) collective-permute-start(bf16[512,512]{1,0:T(8,128)(2,1)} %g_downA_sum.1), channel_id=1, source_target_pairs={{4,0},{0,4},{5,1},{1,5},{6,2},{2,6},{7,3},{3,7},{12,8},{8,12},{13,... | collective-permute-start | bytes 1572872 | tf_op jit(solution)/shard_map/g_downA_h/ppermute | solution.py:637
  457.6 39.9 %collective-permute-start.53 = (bf16[512,1024]{1,0:T(8,128)(2,1)}, bf16[512,1024]{1,0:T(8,128)(2,1)}, u32[]{:S(2)}, u32[]{:S(2)}) collective-permute-start(bf16[512,1024]{1,0:T(8,128)(2,1)} %get-tuple-element.467), channel_id=1, source_target_pairs={{16,0},{0,16},{17,1},{1,17},{18,2},{2,18},{19,3},{3,19},{20,4},{4,... | collective-permute-start | bytes 3145736 | tf_op jit(solution)/shard_map/g_upA_x/ppermute | solution.py:637
  459.0 41.2 %collective-permute-start.54 = (bf16[2,128,2048]{2,1,0:T(8,128)(2,1)}, bf16[2,128,2048]{2,1,0:T(8,128)(2,1)}, u32[]{:S(2)}, u32[]{:S(2)}) collective-permute-start(bf16[2,128,2048]{2,1,0:T(8,128)(2,1)} %get-tuple-element.470), channel_id=1, source_target_pairs={{1,0},{0,1},{3,2},{2,3},{5,4},{4,5},{7,6},{6,7},{9,8},{8,9},{11,10... | collective-permute-start | bytes 3145736 | tf_op jit(solution)/shard_map/ff0_q/ppermute | solution.py:637
  459.8 40.5 %collective-permute-start.55 = (bf16[2,128,2048]{2,1,0:T(8,128)(2,1)}, bf16[2,128,2048]{2,1,0:T(8,128)(2,1)}, u32[]{:S(2)}, u32[]{:S(2)}) collective-permute-start(bf16[2,128,2048]{2,1,0:T(8,128)(2,1)} %get-tuple-element.471), channel_id=1, source_target_pairs={{2,0},{0,2},{3,1},{1,3},{6,4},{4,6},{7,5},{5,7},{10,8},{8,10},{11,... | collective-permute-start | bytes 3145736 | tf_op jit(solution)/shard_map/ff1_p/ppermute | solution.py:637
  461.4 38.8 %collective-permute-start.52 = (bf16[512,512]{1,0:T(8,128)(2,1)}, bf16[512,512]{1,0:T(8,128)(2,1)}, u32[]{:S(2)}, u32[]{:S(2)}) collective-permute-start(bf16[512,512]{1,0:T(8,128)(2,1)} %g_downB_sum.1), channel_id=1, source_target_pairs={{4,0},{0,4},{5,1},{1,5},{6,2},{2,6},{7,3},{3,7},{12,8},{8,12},{13,... | collective-permute-start | bytes 1572872 | tf_op jit(solution)/shard_map/g_downB_h/ppermute | solution.py:637
  500.3 37.7 %collective-permute-start.56 = (bf16[2,128,2048]{2,1,0:T(8,128)(2,1)}, bf16[2,128,2048]{2,1,0:T(8,128)(2,1)}, u32[]{:S(2)}, u32[]{:S(2)}) collective-permute-start(bf16[2,128,2048]{2,1,0:T(8,128)(2,1)} %get-tuple-element.490), channel_id=1, source_target_pairs={{1,0},{0,1},{3,2},{2,3},{5,4},{4,5},{7,6},{6,7},{9,8},{8,9},{11,10... | collective-permute-start | bytes 3145736 | tf_op jit(solution)/shard_map/da0_q/ppermute | solution.py:637
  501.7 37.1 %collective-permute-start.57 = (bf16[2,128,2048]{2,1,0:T(8,128)(2,1)}, bf16[2,128,2048]{2,1,0:T(8,128)(2,1)}, u32[]{:S(2)}, u32[]{:S(2)}) collective-permute-start(bf16[2,128,2048]{2,1,0:T(8,128)(2,1)} %get-tuple-element.491), channel_id=1, source_target_pairs={{2,0},{0,2},{3,1},{1,3},{6,4},{4,6},{7,5},{5,7},{10,8},{8,10},{11,... | collective-permute-start | bytes 3145736 | tf_op jit(solution)/shard_map/da1_p/ppermute | solution.py:637
  503.7 34.3 %collective-permute-start.59 = (bf16[256,1024]{1,0:T(8,128)(2,1)}, bf16[256,1024]{1,0:T(8,128)(2,1)S(1)}, u32[]{:S(2)}, u32[]{:S(2)}) collective-permute-start(bf16[256,1024]{1,0:T(8,128)(2,1)} %get-tuple-element.501), channel_id=1, source_target_pairs={{4,0},{0,4},{5,1},{1,5},{6,2},{2,6},{7,3},{3,7},{12,8},{8,12},{13,... | collective-permute-start | bytes 1572872 | tf_op jit(solution)/shard_map/g_upA_h/ppermute | solution.py:637
  504.0 34.0 %collective-permute-start.60 = (bf16[512,512]{1,0:T(8,128)(2,1)}, bf16[512,512]{1,0:T(8,128)(2,1)}, u32[]{:S(2)}, u32[]{:S(2)}) collective-permute-start(bf16[512,512]{1,0:T(8,128)(2,1)} %get-tuple-element.507), channel_id=1, source_target_pairs={{16,0},{0,16},{17,1},{1,17},{18,2},{2,18},{19,3},{3,19},{20,4},{4,... | collective-permute-start | bytes 1572872 | tf_op jit(solution)/shard_map/g_downC_x/ppermute | solution.py:637
  627.8 45.4 %collective-permute-start.77 = (bf16[4,32,2048]{2,1,0:T(8,128)(2,1)}, bf16[4,32,2048]{2,1,0:T(8,128)(2,1)S(1)}, u32[]{:S(2)}, u32[]{:S(2)}) collective-permute-start(bf16[4,32,2048]{2,1,0:T(8,128)(2,1)} %slice.55), channel_id=1, source_target_pairs={{4,0},{0,4},{5,1},{1,5},{6,2},{2,6},{7,3},{3,7},{12,8},{8,12},{13,... | collective-permute-start | bytes 1572872 | tf_op jit(solution)/shard_map/input_grad_h/ppermute | solution.py:637
  (149 other events, 2009.3 us)

commit v5 on v4

--- a/solution.py
+++ b/solution.py
@@ -61,10 +61,10 @@
         send[0, :, columns] = value[(2 * kind + 1) * half : (2 * kind + 2) * half]
 
 
-def softmax_rows(q, k):
-    scores = dot(q, k, (1, 1)) * HD ** (-0.5)
-    weights = jnp.exp(scores - jnp.max(scores, axis=-1, keepdims=True))
-    return weights * (1.0 / jnp.sum(weights, axis=-1, keepdims=True))
+def softmax_columns(q, k):
+    scores = dot(k, q, (1, 1)) * HD ** (-0.5)
+    weights = jnp.exp(scores - jnp.max(scores, axis=0, keepdims=True))
+    return weights * (1.0 / jnp.sum(weights, axis=0, keepdims=True))
 
 
 def head_columns(jh, part, n, block):
@@ -130,9 +130,9 @@
         for jh in range(nh):
             for n in range(block // HD):
                 q, k, v = (qkv[0, kind, :, head_columns(jh, i, n, block)] for i in range(3))
-                p = softmax_rows(q, k).astype(BF)
+                p = softmax_columns(q, k).astype(BF)
                 probs[0, kind, jh * (block // HD) + n] = p
-                out = dot(p, v).astype(BF)
+                out = dot(p, v, (0, 0)).astype(BF)
                 o[0, kind, :, jh * block + n * HD : jh * block + (n + 1) * HD] = out
     for d in range(nd):
         total = dot(rows_of(o, slice(0, block)), weights.block(0, d, *outward), (1, 1))
@@ -230,12 +230,12 @@
                 q, k, v = (qkv[0, kind, :, head_columns(jh, i, n, block)] for i in range(3))
                 do = do_all[kind * length : (kind + 1) * length, n * HD : (n + 1) * HD]
                 rounded = probs[0, kind, jh * (block // HD) + n]
-                dv = dot(rounded, do, (0, 0))
-                dp = dot(do, v, (1, 1))
+                dv = dot(rounded, do)
+                dp = dot(v, do, (1, 1))
                 p = rounded.astype(F32)
-                ds = (p * (dp - jnp.sum(p * dp, axis=-1, keepdims=True))).astype(BF)
-                dq = dot(ds, k) * HD ** (-0.5)
-                dk = dot(ds, q, (0, 0)) * HD ** (-0.5)
+                ds = (p * (dp - jnp.sum(p * dp, axis=0, keepdims=True))).astype(BF)
+                dq = dot(ds, k, (0, 0)) * HD ** (-0.5)
+                dk = dot(ds, q) * HD ** (-0.5)
                 for i, value in enumerate((dq, dk, dv)):
                     dqkv[0, kind, :, head_columns(jh, i, n, block)] = value.astype(BF)
     for d in range(nd):
@@ -689,10 +689,10 @@
         return [jnp.concatenate(pair, axis=1) for pair in hops]
 
     def last_hop(self, near, name):
-        return [self.over(near[k], k, True, name) for k in range(2)]
+        return [self.over(near[k], k, True, name) for k in (1, 0)][::-1]
 
     def send_late(self, parts, name):
-        return [self.over(parts[2 * k + 1], k, True, name) for k in range(2)]
+        return [self.over(parts[2 * k + 1], k, True, name) for k in (1, 0)][::-1]
 
     def send_on(self, onward, name):
         return [self.over(onward[k], k, False, name) for k in range(2)]
@@ -817,12 +817,11 @@
     far_one = links.over_h(packed_one, "wqoA")
     x_up = links.over_x(up, "wu0")
     wqo = [jnp.stack([packed, *x_packed])]
-    a_near, far_one, x_up, wqo, packed_two = sync(
-        links.near(a_hops), far_one, x_up, wqo, packed_two
-    )
-
+    a_hops, far_one, x_up, wqo, packed_two = sync(a_hops, far_one, x_up, wqo, packed_two)
+    a_near = links.near(a_hops)
+
+    far_two = links.over_h(packed_two, "wqoB")
     a_far = links.last_hop(a_near, "a")
-    far_two = links.over_h(packed_two, "wqoB")
     x_one = [links.over_x(w, "wqoA1") for w in far_one]
     cot_parts = leave_home("cot_leaves", leave, H, cotangent)
     cot_one = [v[:steps] for v in cot_parts]
@@ -850,8 +849,8 @@
 
     cot = jnp.concatenate([jnp.concatenate(v, axis=1) for v in (cot_one, cot_two)], axis=0)
     df_own = over_images(loss_kernel, "loss", [cot, loss_scale, modulation], kinds)
-    df_near = links.near(links.first_hop(df_own, "df"))
     up_one = links.over_h(up_one, "wuA")
+    df_hops = links.first_hop(df_own, "df")
     x_down = links.over_x(down, "wd0")
     a_rows, qkv, o, probs, *att = call(
         attention_kernel,
@@ -860,17 +859,17 @@
         wqo,
         [whole(D), whole(3 * heads), whole(heads), (steps, 2, heads // HD, length, length), *parts],
     )
-    df_near, att, up_one, up_two, x_down = sync(df_near, att, up_one, up_two, x_down)
-
+    df_hops, att, up_one, up_two, x_down = sync(df_hops, att, up_one, up_two, x_down)
+
+    up_two = links.over_h(up_two, "wuB")
     att_got = links.send_late(att, "att")
-    up_two = links.over_h(up_two, "wuB")
     wd = [jnp.stack([down, *x_down])]
     wd.append(links.from_core(wd[0], "wd0"))
     att_got, up_two, wd, down = sync(att_got, up_two, wd, down)
 
-    att_last = links.send_on(onward(att, att_got, "att_onward"), "att")
     down_one, down_two = halves(down)
     down_one = links.over_h(down_one, "wdA")
+    att_last = links.send_on(onward(att, att_got, "att_onward"), "att")
     up_far = joined((up_one, up_two))
     x_up = [links.over_x(w, "wu1") for w in up_far]
     residual, *b = over_images(
@@ -881,13 +880,16 @@
     )
     b, down_one, up_far, x_up, down_two = sync(b, down_one, up_far, x_up, down_two)
 
+    down_two = links.over_h(down_two, "wdB")
     b_hops = links.first_hop(b, "b")
-    down_two = links.over_h(down_two, "wdB")
     x_one = [links.over_x(w, "wdA1") for w in down_one]
     wu_far = [jnp.stack([w, *others]) for w, others in zip(up_far, x_up)]
-    b_near, down_two, x_one, wu_far = sync(links.near(b_hops), down_two, x_one, wu_far)
+    b_near, down_two, x_one, wu_far, df_hops = sync(
+        links.near(b_hops), down_two, x_one, wu_far, df_hops
+    )
 
     b_far = links.last_hop(b_near, "b")
+    df_near = links.near(df_hops)
     x_two = [links.over_x(w, "wdB1") for w in down_two]
     for w in wu_far:
         wu += [w, links.from_core(w, "wu1")]
@@ -940,12 +942,13 @@
     down_one = links.send_x(g_down[0::3], "g_downA")
     up_sent = links.from_core(up_send, "g_up")
     (down_one,) = add_terms("g_downA_sum", [g_down[0], *down_one])
-    datt_near, g_down, down_one, up_sent, b_rows, du, hidden = sync(
-        links.near(datt_hops), g_down, down_one, up_sent, b_rows, du, hidden
-    )
-
+    datt_hops, g_down, down_one, up_sent, b_rows, du, hidden = sync(
+        datt_hops, g_down, down_one, up_sent, b_rows, du, hidden
+    )
+    datt_near = links.near(datt_hops)
+
+    down_one = links.send_h(down_one, 0, "g_downA")
     datt_far = links.last_hop(datt_near, "datt")
-    down_one = links.send_h(down_one, 0, "g_downA")
     down_mid = links.send_x(g_down[1::3], "g_downB")
     ff = call(down_kernel, "down", [hidden], wd, parts)
     g_up = up_kept(nh, nd, flat(b_rows), flat(du), up_sent)
@@ -972,17 +975,17 @@
         down_two, up_one, up_two, ff_got, datt, dqkv, da, att_send, g_up, g_down
     )
 
+    up_one = links.send_h(up_one, 1, "g_upA")
     da_got = links.send_late(da, "da")
     att_sent = links.from_core(att_send, "g_att")
-    up_one = links.send_h(up_one, 1, "g_upA")
     down_last = links.send_x(g_down[2::3], "g_downC")
     g_att = attention_kept(nh, nd, a_columns, flat(dqkv), flat(datt), flat(o), att_sent)
     da_got, g_att, g_up, up_one, up_two, da, ff_got, down_last = sync(
         da_got, g_att, g_up, up_one, up_two, da, ff_got, down_last
     )
 
+    up_two = links.send_h(up_two, 1, "g_upB")
     att_far = links.send_x(g_att[0::2], "g_attA")
-    up_two = links.send_h(up_two, 1, "g_upB")
     da_last = links.send_on(onward(da, da_got, "da_onward"), "da")
     att_one, att_two = add_terms("g_attA_sum", [g_att[0], *att_far], 2)
     att_one, att_two, up_two, da_last, g_att, g_up, ff_got = sync(

time: 694 us -> 690 us (level)
  local copies, waits for them, and re-layouts: 43.6 us -> 52.8 us
    unnamed x191 -> x193, local copies, waits for them, and re-layouts: 32.2 us -> 39.4 us
  transfers between devices with their start and end apart: 78 -> 78, of which waited for: 37 -> 39; matrix products, arithmetic and copies ran while one was open for 7% -> 7% of each run, Pallas kernels for 25% -> 25%
where the time goes in v5:
time: 690 us; the launch traced here: 679 us
  waiting for transfers between devices  296 us (43%)
  Pallas kernels  200 us (29%)
  starting transfers between devices  83.7 us (12%)
  local copies, waits for them, and re-layouts  52.8 us (8%)
  other arithmetic  37.1 us (5%)
  between operations  9.07 us (1%)
    ppermute x73, waiting for transfers between devices, shifted(): lax.ppermute(v, axis, [((dst + offset) % size, dst) for dst in range(size)])  285 us
    pallas_call x5, Pallas kernels, group_call(): pl.pallas_call(lambda *refs: kernel(nh, nd, *refs), name=name, grid=(step...  114 us
    ppermute x73, starting transfers between devices, shifted(): lax.ppermute(v, axis, [((dst + offset) % size, dst) for dst in range(size)])  70 us
    pallas_call x7, Pallas kernels, one_step(): pl.pallas_call(kernel, name=name, grid=(1,), in_specs=[pl.BlockSpec((v.sh...  40.3 us
    unnamed x193, local copies, waits for them, and re-layouts  39.4 us
    pallas_call x10, Pallas kernels, image_call(): pl.pallas_call(kernel, name=name, grid=(steps,), in_specs=[cut(seen(v.sha...  20.8 us
    pallas_call x2, Pallas kernels, gradient(): pl.pallas_call(kernel, name=name, grid=(nh, half), in_specs=in_specs, out...  15.9 us
  transfers between devices with their start and end apart: 78, of which 39 were waited for; matrix products, arithmetic and copies ran while one was open for 7% of the time, Pallas kernels for 25%

profile of v5, /device:TPU:0, one launch (start us, length us, event | category | flops | bytes accessed | tf_op | source)
XLA Modules:
  0.0 679.5 jit_solution(5913140996190235393)
XLA Ops:
  17.5 18.2 %collective-permute-done = bf16[4,32,2048]{2,1,0:T(8,128)(2,1)} collective-permute-done((bf16[4,32,2048]{2,1,0:T(8,128)(2,1)}, bf16[4,32,2048]{2,1,0:T(8,128)(2,1)}, u32[]{:S(2)}, u32[]{:S(2)}) %collective-permute-start) | collective-permute-done | bytes 524320 | tf_op jit(solution)/shard_map/stream_h/ppermute | solution.py:637
  45.8 15.0 %collective-permute-done.2 = bf16[2,64,2048]{2,1,0:T(8,128)(2,1)S(1)} collective-permute-done((bf16[2,64,2048]{2,1,0:T(8,128)(2,1)S(1)}, bf16[2,64,2048]{2,1,0:T(8,128)(2,1)S(1)}, u32[]{:S(2)}, u32[]{:S(2)}) %collective-permute-start.2) | collective-permute-done | bytes 524320 | tf_op jit(solution)/shard_map/a0_p/ppermute | solution.py:637
  73.3 26.5 %collective-permute-done.8 = bf16[256,1024]{1,0:T(8,128)(2,1)S(1)} collective-permute-done((bf16[256,1024]{1,0:T(8,128)(2,1)S(1)}, bf16[256,1024]{1,0:T(8,128)(2,1)S(1)}, u32[]{:S(2)}, u32[]{:S(2)}) %collective-permute-start.8) | collective-permute-done | bytes 524320 | tf_op jit(solution)/shard_map/wqoB_h/ppermute | solution.py:637
  105.4 13.2 %collective-permute-done.11 = bf16[2,32,2048]{2,1,0:T(8,128)(2,1)S(1)} collective-permute-done((bf16[2,32,2048]{2,1,0:T(8,128)(2,1)S(1)}, bf16[2,32,2048]{2,1,0:T(8,128)(2,1)S(1)}, u32[]{:S(2)}, u32[]{:S(2)}) %collective-permute-start.11) | collective-permute-done | bytes 262176 | tf_op jit(solution)/shard_map/cotA_h/ppermute | solution.py:637
  122.6 13.1 %collective-permute-done.14 = bf16[2,32,2048]{2,1,0:T(8,128)(2,1)S(1)} collective-permute-done((bf16[2,32,2048]{2,1,0:T(8,128)(2,1)S(1)}, bf16[2,32,2048]{2,1,0:T(8,128)(2,1)S(1)}, u32[]{:S(2)}, u32[]{:S(2)}) %collective-permute-start.14) | collective-permute-done | bytes 262176 | tf_op jit(solution)/shard_map/cotB_h/ppermute | solution.py:637
  143.5 17.7 %attention.1 = (bf16[2,2,256,2048]{3,2,1,0:T(8,128)(2,1)}, bf16[2,2,256,1536]{3,2,1,0:T(8,128)(2,1)}, bf16[2,2,256,512]{3,2,1,0:T(8,128)(2,1)}, bf16[2,2,4,256,2...) custom-call(bf16[2,128,2048]{2,1,0:T(8,128)(2,1)} %copy-done.69, ...), custom_call_target="tpu_custom_call" | custom-call | tf_op jit(solution)/shard_map/attention/pallas_call | solution.py:274
  172.1 30.7 %collective-permute-done.22 = bf16[256,1024]{1,0:T(8,128)(2,1)S(1)} collective-permute-done((bf16[256,1024]{1,0:T(8,128)(2,1)S(1)}, bf16[256,1024]{1,0:T(8,128)(2,1)S(1)}, u32[]{:S(2)}, u32[]{:S(2)}) %collective-permute-start.22) | collective-permute-done | bytes 524320 | tf_op jit(solution)/shard_map/wuB_h/ppermute | solution.py:637
  212.6 15.3 %collective-permute-done.24.refs_4_ = bf16[2,64,2048]{2,1,0:T(8,128)(2,1)S(1)} collective-permute-done((bf16[2,64,2048]{2,1,0:T(8,128)(2,1)S(1)}, bf16[2,64,2048]{2,1,0:T(8,128)(2,1)S(1)}, u32[]{:S(2)}, u32[]{:S(2)}) %collective-permute-start.24) | collective-permute-done | bytes 524320 | tf_op jit(solution)/shard_map/att0_p/ppermute | solution.py:637
  239.8 17.6 %collective-permute-done.28 = bf16[2,64,2048]{2,1,0:T(8,128)(2,1)S(1)} collective-permute-done((bf16[2,64,2048]{2,1,0:T(8,128)(2,1)S(1)}, bf16[2,64,2048]{2,1,0:T(8,128)(2,1)S(1)}, u32[]{:S(2)}, u32[]{:S(2)}) %collective-permute-start.28) | collective-permute-done | bytes 524320 | tf_op jit(solution)/shard_map/b0_p/ppermute | solution.py:637
  267.4 8.0 %collective-permute-done.34 = bf16[512,512]{1,0:T(8,128)(2,1)S(1)} collective-permute-done((bf16[512,512]{1,0:T(8,128)(2,1)S(1)}, bf16[512,512]{1,0:T(8,128)(2,1)S(1)}, u32[]{:S(2)}, u32[]{:S(2)}) %collective-permute-start.34) | collective-permute-done | bytes 524320 | tf_op jit(solution)/shard_map/wdB1_x/ppermute | solution.py:637
  275.4 10.2 %collective-permute-done.32.refs_1_ = bf16[2,128,2048]{2,1,0:T(8,128)(2,1)S(1)} collective-permute-done((bf16[2,128,2048]{2,1,0:T(8,128)(2,1)S(1)}, bf16[2,128,2048]{2,1,0:T(8,128)(2,1)S(1)}, u32[]{:S(2)}, u32[]{:S(2)}) %collective-permute-start.32) | collective-permute-done | bytes 1048608 | tf_op jit(solution)/shard_map/b0_q/ppermute | solution.py:637
  290.6 19.5 %up.1 = (bf16[2,2,256,2048]{3,2,1,0:T(8,128)(2,1)}, bf16[2,2,256,2048]{3,2,1,0:T(8,128)(2,1)}, bf16[2,2,256,2048]{3,2,1,0:T(8,128)(2,1)}) custom-call(bf16[2,128,2048]{2,1,0:T(8,128)(2,1)} %copy-done.66, bf16[2,128,2048]{2,1,0:T(8,128)(2,1)} %copy-done.82, bf16[2,128,2048]{2,1,0:T(8,128)(2,1)} %copy-done.67, bf16[2,128,2048]{2,1,0:T(8,128)(2,1)} %copy-done.83, ...), custom_call_target="tpu_custom_call" | custom-call | tf_op jit(solution)/shard_map/up/pallas_call | solution.py:274
  315.9 26.6 %up_back.1 = (bf16[2,2,256,2048]{3,2,1,0:T(8,128)(2,1)}, bf16[2,2,256,2048]{3,2,1,0:T(8,128)(2,1)}, bf16[2,128,2048]{2,1,0:T(8,128)(2,1)}, bf16[2,128,2048]{2,1,...) custom-call(bf16[2,128,2048]{2,1,0:T(8,128)(2,1)} %pad_maximum_fusion.10.refs_0_, ...), custom_call_target="tpu_custom_call" | custom-call | tf_op jit(solution)/shard_map/up_back/pallas_call | solution.py:274
  360.5 8.0 %g_down_send.1 = bf16[2048,1024]{1,0:T(8,128)(2,1)S(1)} custom-call(bf16[1024,2048]{1,0:T(8,128)(2,1)} %bitcast.101, bf16[1024,2048]{1,0:T(8,128)(2,1)} %bitcast.109), custom_call_target="tpu_custom_call" | custom-call | tf_op jit(solution)/shard_map/g_down_send/pallas_call | solution.py:479
  377.8 9.7 %g_down_keep.1 = (bf16[512,512]{1,0:T(8,128)(2,1)}, bf16[1024,512]{1,0:T(8,128)(2,1)}, bf16[512,512]{1,0:T(8,128)(2,1)}, bf16[512,512]{1,0:T(8,128)(2,1)}, bf16[...) custom-call(bf16[1024,2048]{1,0:T(8,128)(2,1)} %bitcast.102, bf16[1024,2048]{1,0:T(8,128)(2,1)} %bitcast.110, ...), custom_call_target="tpu_custom_call" | custom-call | tf_op jit(solution)/shard_map/g_down_keep/pallas_call | solution.py:492
  422.2 14.3 %down.1 = (bf16[2,128,2048]{2,1,0:T(8,128)(2,1)}, bf16[2,128,2048]{2,1,0:T(8,128)(2,1)}, bf16[2,128,2048]{2,1,0:T(8,128)(2,1)}, bf16[2,128,2048]{2,1,0:T(8,128)(2,1)}) custom-call(bf16[2,2,256,2048]{3,2,1,0:T(8,128)(2,1)} %get-tuple-element.480.refs_0_, bf16[2,1024,512]{2,1,0:T(8,128)(2,1)} %copy-done.50, bf16[2,1024,512]{2,1,0:T(8,128)(2,1)} %copy-done.59, ...), custom_call_target="tpu_custom_call" | custom-call | tf_op jit(solution)/shard_map/down/pallas_call | solution.py:274
  436.4 9.6 %g_up_keep.1 = (bf16[512,1024]{1,0:T(8,128)(2,1)}, bf16[512,1024]{1,0:T(8,128)(2,1)}, bf16[512,1024]{1,0:T(8,128)(2,1)}, bf16[512,1024]{1,0:T(8,128)(2,1)}) custom-call(bf16[1024,2048]{1,0:T(8,128)(2,1)} %bitcast.106, bf16[1024,2048]{1,0:T(8,128)(2,1)} %bitcast.108, bf16[1024,2048]{1,0:T(8,128)(2,1)} %collective-permute-done.47.sent), custom_call_target="tpu_custom_call" | custom-call | tf_op jit(solution)/shard_map/g_up_keep/pallas_call | solution.py:492
  456.8 35.5 %attention_back.1 = (bf16[2,128,2048]{2,1,0:T(8,128)(2,1)}, bf16[2,128,2048]{2,1,0:T(8,128)(2,1)}, bf16[2,128,2048]{2,1,0:T(8,128)(2,1)}, bf16[2,128,2048]{2,1,0...) custom-call(bf16[2048,1024]{1,0:T(8,128)(2,1)} %bitcast.103, ...), custom_call_target="tpu_custom_call" | custom-call | tf_op jit(solution)/shard_map/attention_back/pallas_call | solution.py:274
  504.5 11.2 %g_att_keep.1 = (bf16[512,1024]{1,0:T(8,128)(2,1)}, bf16[512,1024]{1,0:T(8,128)(2,1)}, bf16[512,1024]{1,0:T(8,128)(2,1)}, bf16[512,1024]{1,0:T(8,128)(2,1)}) custom-call(bf16[2048,1024]{1,0:T(8,128)(2,1)} %bitcast.104, bf16[1024,1536]{1,0:T(8,128)(2,1)} %bitcast.115, bf16[1024,2048]{1,0:T(8,128)(2,1)} %bitcast.114, bf16[1024,512]{1,0:T(8,128)(2,1)} %bitcast.111, ...), custom_call_target="tpu_custom_call" | custom-call | tf_op jit(solution)/shard_map/g_att_keep/pallas_call | solution.py:492
  515.7 16.3 %collective-permute-done.59 = bf16[256,1024]{1,0:T(8,128)(2,1)S(1)} collective-permute-done((bf16[256,1024]{1,0:T(8,128)(2,1)}, bf16[256,1024]{1,0:T(8,128)(2,1)S(1)}, u32[]{:S(2)}, u32[]{:S(2)}) %collective-permute-start.59) | collective-permute-done | bytes 524320 | tf_op jit(solution)/shard_map/g_upA_h/ppermute | solution.py:637
  540.5 17.5 %collective-permute-done.61.refs_1_ = bf16[512,1024]{1,0:T(8,128)(2,1)} collective-permute-done((bf16[512,1024]{1,0:T(8,128)(2,1)}, bf16[512,1024]{1,0:T(8,128)(2,1)}, u32[]{:S(2)}, u32[]{:S(2)}) %collective-permute-start.61) | collective-permute-done | bytes 1048608 | tf_op jit(solution)/shard_map/g_attA_x/ppermute | solution.py:637
  574.2 12.6 %collective-permute-done.65 = bf16[256,1024]{1,0:T(8,128)(2,1)S(1)} collective-permute-done((bf16[256,1024]{1,0:T(8,128)(2,1)}, bf16[256,1024]{1,0:T(8,128)(2,1)S(1)}, u32[]{:S(2)}, u32[]{:S(2)}) %collective-permute-start.65) | collective-permute-done | bytes 524320 | tf_op jit(solution)/shard_map/g_attA_h/ppermute | solution.py:637
  602.7 12.2 %collective-permute-done.69 = bf16[256,1024]{1,0:T(8,128)(2,1)S(1)} collective-permute-done((bf16[256,1024]{1,0:T(8,128)(2,1)}, bf16[256,1024]{1,0:T(8,128)(2,1)S(1)}, u32[]{:S(2)}, u32[]{:S(2)}) %collective-permute-start.69) | collective-permute-done | bytes 524320 | tf_op jit(solution)/shard_map/g_attB_h/ppermute | solution.py:637
  641.3 8.7 %collective-permute-done.75 = f32[]{:T(128)} collective-permute-done((f32[]{:T(128)}, f32[]{:T(128)}, u32[]{:S(2)}, u32[]{:S(2)}) %collective-permute-start.75) | collective-permute-done | bytes 36 | tf_op jit(solution)/shard_map/norm/ppermute | solution.py:719
  (405 shorter events, 283.1 us)
Async XLA Ops:
  3.4 32.4 %collective-permute-start.1 = (bf16[512,1024]{1,0:T(8,128)(2,1)S(1)}, bf16[512,1024]{1,0:T(8,128)(2,1)}, u32[]{:S(2)}, u32[]{:S(2)}) collective-permute-start(bf16[512,1024]{1,0:T(8,128)(2,1)S(1)} %pack.1), channel_id=1, source_target_pairs={{16,0},{0,16},{17,1},{1,17},{18,2},{2,18},{19,3},{3,19},{20,4},{4,... | collective-permute-start | bytes 3145736 | tf_op jit(solution)/shard_map/wqo0_x/ppermute | solution.py:637
  35.8 31.2 %collective-permute-start.5 = (bf16[512,1024]{1,0:T(8,128)(2,1)S(1)}, bf16[512,1024]{1,0:T(8,128)(2,1)S(1)}, u32[]{:S(2)}, u32[]{:S(2)}) collective-permute-start(bf16[512,1024]{1,0:T(8,128)(2,1)S(1)} %get-tuple-element.310), channel_id=1, source_target_pairs={{16,0},{0,16},{17,1},{1,17},{18,2},{2,18},{19,3},{3,19},{20,4},{4,... | collective-permute-start | bytes 3145736 | tf_op jit(solution)/shard_map/wu0_x/ppermute | solution.py:637
  67.1 34.9 %collective-permute-start.7 = (bf16[2,128,2048]{2,1,0:T(8,128)(2,1)S(1)}, bf16[2,128,2048]{2,1,0:T(8,128)(2,1)S(1)}, u32[]{:S(2)}, u32[]{:S(2)}) collective-permute-start(bf16[2,128,2048]{2,1,0:T(8,128)(2,1)S(1)} %constant_dynamic-update-slice_fusion.2.refs_2_), channel_id=1, source_target_pairs={{2,0},{0,2},{3,1},{1,3},{6,4},{4,6},{7,5},{5,7},{10,8},{8,10},{11,... | collective-permute-start | bytes 3145736 | tf_op jit(solution)/shard_map/a1_p/ppermute | solution.py:637
  67.3 34.8 %collective-permute-start.6 = (bf16[2,128,2048]{2,1,0:T(8,128)(2,1)S(1)}, bf16[2,128,2048]{2,1,0:T(8,128)(2,1)S(1)}, u32[]{:S(2)}, u32[]{:S(2)}) collective-permute-start(bf16[2,128,2048]{2,1,0:T(8,128)(2,1)S(1)} %constant_dynamic-update-slice_fusion.refs_0_), channel_id=1, source_target_pairs={{1,0},{0,1},{3,2},{2,3},{5,4},{4,5},{7,6},{6,7},{9,8},{8,9},{11,10... | collective-permute-start | bytes 3145736 | tf_op jit(solution)/shard_map/a0_q/ppermute | solution.py:637
  70.0 29.9 %collective-permute-start.8 = (bf16[256,1024]{1,0:T(8,128)(2,1)S(1)}, bf16[256,1024]{1,0:T(8,128)(2,1)S(1)}, u32[]{:S(2)}, u32[]{:S(2)}) collective-permute-start(bf16[256,1024]{1,0:T(8,128)(2,1)S(1)} %get-tuple-element.317), channel_id=1, source_target_pairs={{4,0},{0,4},{5,1},{1,5},{6,2},{2,6},{7,3},{3,7},{12,8},{8,12},{13,... | collective-permute-start | bytes 1572872 | tf_op jit(solution)/shard_map/wqoB_h/ppermute | solution.py:637
  71.5 28.3 %collective-permute-start.9 = (bf16[256,1024]{1,0:T(8,128)(2,1)S(1)}, bf16[256,1024]{1,0:T(8,128)(2,1)S(1)}, u32[]{:S(2)}, u32[]{:S(2)}) collective-permute-start(bf16[256,1024]{1,0:T(8,128)(2,1)S(1)} %collective-permute-done.4), channel_id=1, source_target_pairs={{16,0},{0,16},{17,1},{1,17},{18,2},{2,18},{19,3},{3,19},{20,4},{4,... | collective-permute-start | bytes 1572872 | tf_op jit(solution)/shard_map/wqoA1_x/ppermute | solution.py:637
  137.1 28.9 %collective-permute-start.19 = (bf16[1024,512]{1,0:T(8,128)(2,1)}, bf16[1024,512]{1,0:T(8,128)(2,1)}, u32[]{:S(2)}, u32[]{:S(2)}) collective-permute-start(bf16[1024,512]{1,0:T(8,128)(2,1)} %get-tuple-element.371), channel_id=1, source_target_pairs={{16,0},{0,16},{17,1},{1,17},{18,2},{2,18},{19,3},{3,19},{20,4},{4,... | collective-permute-start | bytes 3145736 | tf_op jit(solution)/shard_map/wd0_x/ppermute | solution.py:637
  168.0 37.0 %collective-permute-start.23 = (bf16[2,1024,512]{2,1,0:T(8,128)(2,1)S(1)}, bf16[2,1024,512]{2,1,0:T(8,128)(2,1)S(1)}, u32[]{:S(2)}, u32[]{:S(2)}) collective-permute-start(bf16[2,1024,512]{2,1,0:T(8,128)(2,1)S(1)} %pad_maximum_fusion.3.refs_9_.refs_1_), channel_id=1, source_target_pairs={{8,0},{0,8},{9,1},{1,9},{10,2},{2,10},{11,3},{3,11},{12,4},{4,12},... | collective-permute-start | bytes 6291464 | tf_op jit(solution)/shard_map/wd0_core/ppermute | solution.py:637
  168.1 34.7 %collective-permute-start.20 = (bf16[2,128,2048]{2,1,0:T(8,128)(2,1)S(1)}, bf16[2,128,2048]{2,1,0:T(8,128)(2,1)S(1)}, u32[]{:S(2)}, u32[]{:S(2)}) collective-permute-start(bf16[2,128,2048]{2,1,0:T(8,128)(2,1)S(1)} %copy-done.91), channel_id=1, source_target_pairs={{1,0},{0,1},{3,2},{2,3},{5,4},{4,5},{7,6},{6,7},{9,8},{8,9},{11,10... | collective-permute-start | bytes 3145736 | tf_op jit(solution)/shard_map/att0_q/ppermute | solution.py:637
  168.5 36.5 %collective-permute-start.21 = (bf16[2,128,2048]{2,1,0:T(8,128)(2,1)S(1)}, bf16[2,128,2048]{2,1,0:T(8,128)(2,1)S(1)}, u32[]{:S(2)}, u32[]{:S(2)}) collective-permute-start(bf16[2,128,2048]{2,1,0:T(8,128)(2,1)S(1)} %copy-done.90), channel_id=1, source_target_pairs={{2,0},{0,2},{3,1},{1,3},{6,4},{4,6},{7,5},{5,7},{10,8},{8,10},{11,... | collective-permute-start | bytes 3145736 | tf_op jit(solution)/shard_map/att1_p/ppermute | solution.py:637
  168.5 34.3 %collective-permute-start.22 = (bf16[256,1024]{1,0:T(8,128)(2,1)S(1)}, bf16[256,1024]{1,0:T(8,128)(2,1)S(1)}, u32[]{:S(2)}, u32[]{:S(2)}) collective-permute-start(bf16[256,1024]{1,0:T(8,128)(2,1)S(1)} %copy-done.89), channel_id=1, source_target_pairs={{4,0},{0,4},{5,1},{1,5},{6,2},{2,6},{7,3},{3,7},{12,8},{8,12},{13,... | collective-permute-start | bytes 1572872 | tf_op jit(solution)/shard_map/wuB_h/ppermute | solution.py:637
  205.0 30.7 %collective-permute-start.27 = (bf16[512,1024]{1,0:T(8,128)(2,1)S(1)}, bf16[512,1024]{1,0:T(8,128)(2,1)S(1)}, u32[]{:S(2)}, u32[]{:S(2)}) collective-permute-start(bf16[512,1024]{1,0:T(8,128)(2,1)S(1)} %constant_dynamic-update-slice_fusion.4), channel_id=1, source_target_pairs={{16,0},{0,16},{17,1},{1,17},{18,2},{2,18},{19,3},{3,19},{20,4},{4,... | collective-permute-start | bytes 3145736 | tf_op jit(solution)/shard_map/wu1_x/ppermute | solution.py:637
  417.7 35.5 %collective-permute-start.49 = (bf16[2,128,2048]{2,1,0:T(8,128)(2,1)}, bf16[2,128,2048]{2,1,0:T(8,128)(2,1)}, u32[]{:S(2)}, u32[]{:S(2)}) collective-permute-start(bf16[2,128,2048]{2,1,0:T(8,128)(2,1)} %constant_dynamic-update-slice_fusion.8.refs_4_), channel_id=1, source_target_pairs={{2,0},{0,2},{3,1},{1,3},{6,4},{4,6},{7,5},{5,7},{10,8},{8,10},{11,... | collective-permute-start | bytes 3145736 | tf_op jit(solution)/shard_map/datt1_p/ppermute | solution.py:637
  419.5 33.7 %collective-permute-start.48 = (bf16[2,128,2048]{2,1,0:T(8,128)(2,1)}, bf16[2,128,2048]{2,1,0:T(8,128)(2,1)}, u32[]{:S(2)}, u32[]{:S(2)}) collective-permute-start(bf16[2,128,2048]{2,1,0:T(8,128)(2,1)} %constant_dynamic-update-slice_fusion.6.refs_2_), channel_id=1, source_target_pairs={{1,0},{0,1},{3,2},{2,3},{5,4},{4,5},{7,6},{6,7},{9,8},{8,9},{11,10... | collective-permute-start | bytes 3145736 | tf_op jit(solution)/shard_map/datt0_q/ppermute | solution.py:637
  420.2 31.2 %collective-permute-start.50 = (bf16[512,512]{1,0:T(8,128)(2,1)}, bf16[512,512]{1,0:T(8,128)(2,1)S(1)}, u32[]{:S(2)}, u32[]{:S(2)}) collective-permute-start(bf16[512,512]{1,0:T(8,128)(2,1)} %g_downA_sum.1), channel_id=1, source_target_pairs={{4,0},{0,4},{5,1},{1,5},{6,2},{2,6},{7,3},{3,7},{12,8},{8,12},{13,... | collective-permute-start | bytes 1572872 | tf_op jit(solution)/shard_map/g_downA_h/ppermute | solution.py:637
  453.2 39.2 %collective-permute-start.53 = (bf16[512,1024]{1,0:T(8,128)(2,1)}, bf16[512,1024]{1,0:T(8,128)(2,1)}, u32[]{:S(2)}, u32[]{:S(2)}) collective-permute-start(bf16[512,1024]{1,0:T(8,128)(2,1)} %get-tuple-element.487), channel_id=1, source_target_pairs={{16,0},{0,16},{17,1},{1,17},{18,2},{2,18},{19,3},{3,19},{20,4},{4,... | collective-permute-start | bytes 3145736 | tf_op jit(solution)/shard_map/g_upA_x/ppermute | solution.py:637
  453.9 41.2 %collective-permute-start.54 = (bf16[2,128,2048]{2,1,0:T(8,128)(2,1)}, bf16[2,128,2048]{2,1,0:T(8,128)(2,1)}, u32[]{:S(2)}, u32[]{:S(2)}) collective-permute-start(bf16[2,128,2048]{2,1,0:T(8,128)(2,1)} %get-tuple-element.490), channel_id=1, source_target_pairs={{1,0},{0,1},{3,2},{2,3},{5,4},{4,5},{7,6},{6,7},{9,8},{8,9},{11,10... | collective-permute-start | bytes 3145736 | tf_op jit(solution)/shard_map/ff0_q/ppermute | solution.py:637
  454.5 40.5 %collective-permute-start.55 = (bf16[2,128,2048]{2,1,0:T(8,128)(2,1)}, bf16[2,128,2048]{2,1,0:T(8,128)(2,1)}, u32[]{:S(2)}, u32[]{:S(2)}) collective-permute-start(bf16[2,128,2048]{2,1,0:T(8,128)(2,1)} %get-tuple-element.491), channel_id=1, source_target_pairs={{2,0},{0,2},{3,1},{1,3},{6,4},{4,6},{7,5},{5,7},{10,8},{8,10},{11,... | collective-permute-start | bytes 3145736 | tf_op jit(solution)/shard_map/ff1_p/ppermute | solution.py:637
  455.4 39.7 %collective-permute-start.52 = (bf16[512,512]{1,0:T(8,128)(2,1)}, bf16[512,512]{1,0:T(8,128)(2,1)}, u32[]{:S(2)}, u32[]{:S(2)}) collective-permute-start(bf16[512,512]{1,0:T(8,128)(2,1)} %g_downB_sum.1), channel_id=1, source_target_pairs={{4,0},{0,4},{5,1},{1,5},{6,2},{2,6},{7,3},{3,7},{12,8},{8,12},{13,... | collective-permute-start | bytes 1572872 | tf_op jit(solution)/shard_map/g_downB_h/ppermute | solution.py:637
  495.1 36.9 %collective-permute-start.56 = (bf16[2,128,2048]{2,1,0:T(8,128)(2,1)}, bf16[2,128,2048]{2,1,0:T(8,128)(2,1)}, u32[]{:S(2)}, u32[]{:S(2)}) collective-permute-start(bf16[2,128,2048]{2,1,0:T(8,128)(2,1)} %get-tuple-element.510), channel_id=1, source_target_pairs={{1,0},{0,1},{3,2},{2,3},{5,4},{4,5},{7,6},{6,7},{9,8},{8,9},{11,10... | collective-permute-start | bytes 3145736 | tf_op jit(solution)/shard_map/da0_q/ppermute | solution.py:637
  496.5 36.8 %collective-permute-start.57 = (bf16[2,128,2048]{2,1,0:T(8,128)(2,1)}, bf16[2,128,2048]{2,1,0:T(8,128)(2,1)}, u32[]{:S(2)}, u32[]{:S(2)}) collective-permute-start(bf16[2,128,2048]{2,1,0:T(8,128)(2,1)} %get-tuple-element.511), channel_id=1, source_target_pairs={{2,0},{0,2},{3,1},{1,3},{6,4},{4,6},{7,5},{5,7},{10,8},{8,10},{11,... | collective-permute-start | bytes 3145736 | tf_op jit(solution)/shard_map/da1_p/ppermute | solution.py:637
  497.7 34.3 %collective-permute-start.59 = (bf16[256,1024]{1,0:T(8,128)(2,1)}, bf16[256,1024]{1,0:T(8,128)(2,1)S(1)}, u32[]{:S(2)}, u32[]{:S(2)}) collective-permute-start(bf16[256,1024]{1,0:T(8,128)(2,1)} %get-tuple-element.521), channel_id=1, source_target_pairs={{4,0},{0,4},{5,1},{1,5},{6,2},{2,6},{7,3},{3,7},{12,8},{8,12},{13,... | collective-permute-start | bytes 1572872 | tf_op jit(solution)/shard_map/g_upA_h/ppermute | solution.py:637
  499.2 32.8 %collective-permute-start.60 = (bf16[512,512]{1,0:T(8,128)(2,1)}, bf16[512,512]{1,0:T(8,128)(2,1)}, u32[]{:S(2)}, u32[]{:S(2)}) collective-permute-start(bf16[512,512]{1,0:T(8,128)(2,1)} %get-tuple-element.527), channel_id=1, source_target_pairs={{16,0},{0,16},{17,1},{1,17},{18,2},{2,18},{19,3},{3,19},{20,4},{4,... | collective-permute-start | bytes 1572872 | tf_op jit(solution)/shard_map/g_downC_x/ppermute | solution.py:637
  623.3 46.3 %collective-permute-start.77 = (bf16[4,32,2048]{2,1,0:T(8,128)(2,1)}, bf16[4,32,2048]{2,1,0:T(8,128)(2,1)S(1)}, u32[]{:S(2)}, u32[]{:S(2)}) collective-permute-start(bf16[4,32,2048]{2,1,0:T(8,128)(2,1)} %slice.55), channel_id=1, source_target_pairs={{4,0},{0,4},{5,1},{1,5},{6,2},{2,6},{7,3},{3,7},{12,8},{8,12},{13,... | collective-permute-start | bytes 1572872 | tf_op jit(solution)/shard_map/input_grad_h/ppermute | solution.py:637
  (148 other events, 1938.2 us)

commit v6 on v5

--- a/solution.py
+++ b/solution.py
@@ -210,7 +210,7 @@
     refs = Pieces(refs)
     (a, o), tokens, (qkv, probs) = refs.take(2), refs.tokens(), refs.take(2)
     weights = Merged(refs.take(2 * nh))
-    parts, (all_datt, all_dqkv, sent) = refs.parts(), refs.take(3)
+    parts, (datt_out, dqkv_out, sent, all_datt, all_dqkv) = refs.parts(), refs.take(5)
     step = pl.program_id(0)
     datt, dqkv = (v.at[pl.ds(step, 1)] for v in (all_datt, all_dqkv))
     join_tokens(tokens, datt)
@@ -243,6 +243,8 @@
         for jh in range(1, nh):
             total += dot(rows_of(dqkv, slice(jh * width, (jh + 1) * width)), weights.block(jh, d, *inward), (1, 1))
         put_parts(total.astype(BF), slice(d * depth, (d + 1) * depth), parts)
+    datt_out[...] = datt[...]
+    dqkv_out[...] = dqkv[...]
     across, both = nd // 2, width + block
 
     def every_row(ref, columns=slice(None)):
@@ -262,7 +264,9 @@
                 sent[rows, at + width : at + both] = outward[:, jh * block : (jh + 1) * block]
 
 
-def group_call(kernel, name, nh, nd, steps, blocked, whole, outs, resident=(), whole_outs=()):
+def group_call(
+    kernel, name, nh, nd, steps, blocked, whole, outs, resident=(), whole_outs=(), scratch=()
+):
     def cut(shape):
         zeros = (0,) * (len(shape) - 1)
         return pl.BlockSpec((1,) + tuple(shape[1:]), lambda i: (i,) + zeros)
@@ -280,6 +284,7 @@
         + [pl.BlockSpec(memory_space=pltpu.VMEM)] * len(whole),
         out_specs=[cut(s) for s in outs] + [stay(s) for s in whole_outs],
         out_shape=[jax.ShapeDtypeStruct(s, BF) for s in (*outs, *whole_outs)],
+        scratch_shapes=[pltpu.VMEM(shape, BF) for shape in scratch],
         compiler_params=pltpu.CompilerParams(vmem_limit_bytes=62 * 2**20),
         cost_estimate=pl.CostEstimate(flops=0, bytes_accessed=0, transcendentals=0),
     )(*resident, *blocked, *whole)
@@ -785,10 +790,8 @@
     def flat(v):
         return v.reshape(rows, v.shape[-1])
 
-    def call(kernel, name, blocked, weights, outs, resident=(), whole_outs=()):
-        return list(
-            group_call(kernel, name, nh, nd, steps, blocked, weights, outs, resident, whole_outs)
-        )
+    def call(kernel, name, blocked, weights, outs, *staying):
+        return list(group_call(kernel, name, nh, nd, steps, blocked, weights, outs, *staying))
 
     def halves(w):
         size = w.shape[0] // 2
@@ -966,15 +969,16 @@
         "attention_back",
         [datt_near[0], datt_far[0], datt_near[1], datt_far[1], qkv, probs],
         wqo,
-        parts,
+        [*parts, whole(D), whole(3 * heads)],
         (a_columns, o),
-        (whole(D), whole(3 * heads), (D // 2, 4 * heads)),
-    )
+        [(D // 2, 4 * heads)],
+        (whole(D), whole(3 * heads)),
+    )
+    down_two, up_far, ff_got, datt, dqkv, da, att_send, g_up, g_down = sync(
+        down_two, up_far, ff_got, datt, dqkv, da, att_send, g_up, g_down
+    )
+
     up_one, up_two = add_terms("g_upA_sum", [g_up[0], *up_far], 2)
-    down_two, up_one, up_two, ff_got, datt, dqkv, da, att_send, g_up, g_down = sync(
-        down_two, up_one, up_two, ff_got, datt, dqkv, da, att_send, g_up, g_down
-    )
-
     up_one = links.send_h(up_one, 1, "g_upA")
     da_got = links.send_late(da, "da")
     att_sent = links.from_core(att_send, "g_att")

time: 690 us -> 687 us (level)
    unnamed x193 -> x191, local copies, waits for them, and re-layouts: 39.4 us -> 37.3 us
  transfers between devices with their start and end apart: 78 -> 78, of which waited for: 39 -> 38; matrix products, arithmetic and copies ran while one was open for 7% -> 7% of each run, Pallas kernels for 25% -> 25%
where the time goes in v6:
time: 687 us; the launch traced here: 676 us
  waiting for transfers between devices  296 us (43%)
  Pallas kernels  199 us (29%)
  starting transfers between devices  83.6 us (12%)
  local copies, waits for them, and re-layouts  50.7 us (7%)
  other arithmetic  37.1 us (5%)
  between operations  8.77 us (1%)
    ppermute x73, waiting for transfers between devices, shifted(): lax.ppermute(v, axis, [((dst + offset) % size, dst) for dst in range(size)])  285 us
    pallas_call x5, Pallas kernels, group_call(): pl.pallas_call(lambda *refs: kernel(nh, nd, *refs), name=name, grid=(step...  113 us
    ppermute x73, starting transfers between devices, shifted(): lax.ppermute(v, axis, [((dst + offset) % size, dst) for dst in range(size)])  69.9 us
    pallas_call x7, Pallas kernels, one_step(): pl.pallas_call(kernel, name=name, grid=(1,), in_specs=[pl.BlockSpec((v.sh...  40.3 us
    unnamed x191, local copies, waits for them, and re-layouts  37.3 us
    pallas_call x10, Pallas kernels, image_call(): pl.pallas_call(kernel, name=name, grid=(steps,), in_specs=[cut(seen(v.sha...  20.8 us
    pallas_call x2, Pallas kernels, gradient(): pl.pallas_call(kernel, name=name, grid=(nh, half), in_specs=in_specs, out...  15.9 us
  transfers between devices with their start and end apart: 78, of which 38 were waited for; matrix products, arithmetic and copies ran while one was open for 7% of the time, Pallas kernels for 25%

profile of v6, /device:TPU:0, one launch (start us, length us, event | category | flops | bytes accessed | tf_op | source)
XLA Modules:
  0.0 676.4 jit_solution(14155480778249713608)
XLA Ops:
  17.5 18.2 %collective-permute-done = bf16[4,32,2048]{2,1,0:T(8,128)(2,1)} collective-permute-done((bf16[4,32,2048]{2,1,0:T(8,128)(2,1)}, bf16[4,32,2048]{2,1,0:T(8,128)(2,1)}, u32[]{:S(2)}, u32[]{:S(2)}) %collective-permute-start) | collective-permute-done | bytes 524320 | tf_op jit(solution)/shard_map/stream_h/ppermute | solution.py:642
  45.8 15.0 %collective-permute-done.2 = bf16[2,64,2048]{2,1,0:T(8,128)(2,1)S(1)} collective-permute-done((bf16[2,64,2048]{2,1,0:T(8,128)(2,1)S(1)}, bf16[2,64,2048]{2,1,0:T(8,128)(2,1)S(1)}, u32[]{:S(2)}, u32[]{:S(2)}) %collective-permute-start.2) | collective-permute-done | bytes 524320 | tf_op jit(solution)/shard_map/a0_p/ppermute | solution.py:642
  73.3 26.5 %collective-permute-done.8 = bf16[256,1024]{1,0:T(8,128)(2,1)S(1)} collective-permute-done((bf16[256,1024]{1,0:T(8,128)(2,1)S(1)}, bf16[256,1024]{1,0:T(8,128)(2,1)S(1)}, u32[]{:S(2)}, u32[]{:S(2)}) %collective-permute-start.8) | collective-permute-done | bytes 524320 | tf_op jit(solution)/shard_map/wqoB_h/ppermute | solution.py:642
  105.4 13.2 %collective-permute-done.11 = bf16[2,32,2048]{2,1,0:T(8,128)(2,1)S(1)} collective-permute-done((bf16[2,32,2048]{2,1,0:T(8,128)(2,1)S(1)}, bf16[2,32,2048]{2,1,0:T(8,128)(2,1)S(1)}, u32[]{:S(2)}, u32[]{:S(2)}) %collective-permute-start.11) | collective-permute-done | bytes 262176 | tf_op jit(solution)/shard_map/cotA_h/ppermute | solution.py:642
  122.6 13.1 %collective-permute-done.14 = bf16[2,32,2048]{2,1,0:T(8,128)(2,1)S(1)} collective-permute-done((bf16[2,32,2048]{2,1,0:T(8,128)(2,1)S(1)}, bf16[2,32,2048]{2,1,0:T(8,128)(2,1)S(1)}, u32[]{:S(2)}, u32[]{:S(2)}) %collective-permute-start.14) | collective-permute-done | bytes 262176 | tf_op jit(solution)/shard_map/cotB_h/ppermute | solution.py:642
  143.5 17.7 %attention.1 = (bf16[2,2,256,2048]{3,2,1,0:T(8,128)(2,1)}, bf16[2,2,256,1536]{3,2,1,0:T(8,128)(2,1)}, bf16[2,2,256,512]{3,2,1,0:T(8,128)(2,1)}, bf16[2,2,4,256,2...) custom-call(bf16[2,128,2048]{2,1,0:T(8,128)(2,1)} %copy-done.68, ...), custom_call_target="tpu_custom_call" | custom-call | tf_op jit(solution)/shard_map/attention/pallas_call | solution.py:278
  172.1 30.7 %collective-permute-done.22 = bf16[256,1024]{1,0:T(8,128)(2,1)S(1)} collective-permute-done((bf16[256,1024]{1,0:T(8,128)(2,1)S(1)}, bf16[256,1024]{1,0:T(8,128)(2,1)S(1)}, u32[]{:S(2)}, u32[]{:S(2)}) %collective-permute-start.22) | collective-permute-done | bytes 524320 | tf_op jit(solution)/shard_map/wuB_h/ppermute | solution.py:642
  212.6 15.3 %collective-permute-done.24.refs_4_ = bf16[2,64,2048]{2,1,0:T(8,128)(2,1)S(1)} collective-permute-done((bf16[2,64,2048]{2,1,0:T(8,128)(2,1)S(1)}, bf16[2,64,2048]{2,1,0:T(8,128)(2,1)S(1)}, u32[]{:S(2)}, u32[]{:S(2)}) %collective-permute-start.24) | collective-permute-done | bytes 524320 | tf_op jit(solution)/shard_map/att0_p/ppermute | solution.py:642
  239.8 17.6 %collective-permute-done.28 = bf16[2,64,2048]{2,1,0:T(8,128)(2,1)S(1)} collective-permute-done((bf16[2,64,2048]{2,1,0:T(8,128)(2,1)S(1)}, bf16[2,64,2048]{2,1,0:T(8,128)(2,1)S(1)}, u32[]{:S(2)}, u32[]{:S(2)}) %collective-permute-start.28) | collective-permute-done | bytes 524320 | tf_op jit(solution)/shard_map/b0_p/ppermute | solution.py:642
  267.4 8.1 %collective-permute-done.34 = bf16[512,512]{1,0:T(8,128)(2,1)S(1)} collective-permute-done((bf16[512,512]{1,0:T(8,128)(2,1)S(1)}, bf16[512,512]{1,0:T(8,128)(2,1)S(1)}, u32[]{:S(2)}, u32[]{:S(2)}) %collective-permute-start.34) | collective-permute-done | bytes 524320 | tf_op jit(solution)/shard_map/wdB1_x/ppermute | solution.py:642
  275.4 10.2 %collective-permute-done.32.refs_1_ = bf16[2,128,2048]{2,1,0:T(8,128)(2,1)S(1)} collective-permute-done((bf16[2,128,2048]{2,1,0:T(8,128)(2,1)S(1)}, bf16[2,128,2048]{2,1,0:T(8,128)(2,1)S(1)}, u32[]{:S(2)}, u32[]{:S(2)}) %collective-permute-start.32) | collective-permute-done | bytes 1048608 | tf_op jit(solution)/shard_map/b0_q/ppermute | solution.py:642
  290.6 19.5 %up.1 = (bf16[2,2,256,2048]{3,2,1,0:T(8,128)(2,1)}, bf16[2,2,256,2048]{3,2,1,0:T(8,128)(2,1)}, bf16[2,2,256,2048]{3,2,1,0:T(8,128)(2,1)}) custom-call(bf16[2,128,2048]{2,1,0:T(8,128)(2,1)} %copy-done.66, bf16[2,128,2048]{2,1,0:T(8,128)(2,1)} %copy-done.81, bf16[2,128,2048]{2,1,0:T(8,128)(2,1)} %copy-done.67, bf16[2,128,2048]{2,1,0:T(8,128)(2,1)} %copy-done.82, ...), custom_call_target="tpu_custom_call" | custom-call | tf_op jit(solution)/shard_map/up/pallas_call | solution.py:278
  315.9 26.6 %up_back.1 = (bf16[2,2,256,2048]{3,2,1,0:T(8,128)(2,1)}, bf16[2,2,256,2048]{3,2,1,0:T(8,128)(2,1)}, bf16[2,128,2048]{2,1,0:T(8,128)(2,1)}, bf16[2,128,2048]{2,1,...) custom-call(bf16[2,128,2048]{2,1,0:T(8,128)(2,1)} %pad_maximum_fusion.10.refs_0_, ...), custom_call_target="tpu_custom_call" | custom-call | tf_op jit(solution)/shard_map/up_back/pallas_call | solution.py:278
  360.5 8.0 %g_down_send.1 = bf16[2048,1024]{1,0:T(8,128)(2,1)S(1)} custom-call(bf16[1024,2048]{1,0:T(8,128)(2,1)} %bitcast.101, bf16[1024,2048]{1,0:T(8,128)(2,1)} %bitcast.109), custom_call_target="tpu_custom_call" | custom-call | tf_op jit(solution)/shard_map/g_down_send/pallas_call | solution.py:484
  377.7 9.7 %g_down_keep.1 = (bf16[512,512]{1,0:T(8,128)(2,1)}, bf16[1024,512]{1,0:T(8,128)(2,1)}, bf16[512,512]{1,0:T(8,128)(2,1)}, bf16[512,512]{1,0:T(8,128)(2,1)}, bf16[...) custom-call(bf16[1024,2048]{1,0:T(8,128)(2,1)} %bitcast.102, bf16[1024,2048]{1,0:T(8,128)(2,1)} %bitcast.110, ...), custom_call_target="tpu_custom_call" | custom-call | tf_op jit(solution)/shard_map/g_down_keep/pallas_call | solution.py:497
  422.1 14.3 %down.1 = (bf16[2,128,2048]{2,1,0:T(8,128)(2,1)}, bf16[2,128,2048]{2,1,0:T(8,128)(2,1)}, bf16[2,128,2048]{2,1,0:T(8,128)(2,1)}, bf16[2,128,2048]{2,1,0:T(8,128)(2,1)}) custom-call(bf16[2,2,256,2048]{3,2,1,0:T(8,128)(2,1)} %get-tuple-element.480.refs_0_, bf16[2,1024,512]{2,1,0:T(8,128)(2,1)} %copy-done.50, bf16[2,1024,512]{2,1,0:T(8,128)(2,1)} %copy-done.59, ...), custom_call_target="tpu_custom_call" | custom-call | tf_op jit(solution)/shard_map/down/pallas_call | solution.py:278
  436.4 9.6 %g_up_keep.1 = (bf16[512,1024]{1,0:T(8,128)(2,1)}, bf16[512,1024]{1,0:T(8,128)(2,1)}, bf16[512,1024]{1,0:T(8,128)(2,1)}, bf16[512,1024]{1,0:T(8,128)(2,1)}) custom-call(bf16[1024,2048]{1,0:T(8,128)(2,1)} %bitcast.106, bf16[1024,2048]{1,0:T(8,128)(2,1)} %bitcast.108, bf16[1024,2048]{1,0:T(8,128)(2,1)} %collective-permute-done.47.sent), custom_call_target="tpu_custom_call" | custom-call | tf_op jit(solution)/shard_map/g_up_keep/pallas_call | solution.py:497
  456.8 35.0 %attention_back.1 = (bf16[2,128,2048]{2,1,0:T(8,128)(2,1)}, bf16[2,128,2048]{2,1,0:T(8,128)(2,1)}, bf16[2,128,2048]{2,1,0:T(8,128)(2,1)}, bf16[2,128,2048]{2,1,0...) custom-call(bf16[2048,1024]{1,0:T(8,128)(2,1)} %bitcast.103, ...), custom_call_target="tpu_custom_call" | custom-call | tf_op jit(solution)/shard_map/attention_back/pallas_call | solution.py:278
  500.0 11.2 %g_att_keep.1 = (bf16[512,1024]{1,0:T(8,128)(2,1)}, bf16[512,1024]{1,0:T(8,128)(2,1)}, bf16[512,1024]{1,0:T(8,128)(2,1)}, bf16[512,1024]{1,0:T(8,128)(2,1)}) custom-call(bf16[2048,1024]{1,0:T(8,128)(2,1)} %bitcast.104, bf16[1024,1536]{1,0:T(8,128)(2,1)} %bitcast.115, bf16[1024,2048]{1,0:T(8,128)(2,1)} %bitcast.114, bf16[1024,512]{1,0:T(8,128)(2,1)} %bitcast.111, ...), custom_call_target="tpu_custom_call" | custom-call | tf_op jit(solution)/shard_map/g_att_keep/pallas_call | solution.py:497
  511.3 17.6 %collective-permute-done.59 = bf16[256,1024]{1,0:T(8,128)(2,1)S(1)} collective-permute-done((bf16[256,1024]{1,0:T(8,128)(2,1)}, bf16[256,1024]{1,0:T(8,128)(2,1)S(1)}, u32[]{:S(2)}, u32[]{:S(2)}) %collective-permute-start.59) | collective-permute-done | bytes 524320 | tf_op jit(solution)/shard_map/g_upA_h/ppermute | solution.py:642
  537.3 17.5 %collective-permute-done.61.refs_1_ = bf16[512,1024]{1,0:T(8,128)(2,1)} collective-permute-done((bf16[512,1024]{1,0:T(8,128)(2,1)}, bf16[512,1024]{1,0:T(8,128)(2,1)}, u32[]{:S(2)}, u32[]{:S(2)}) %collective-permute-start.61) | collective-permute-done | bytes 1048608 | tf_op jit(solution)/shard_map/g_attA_x/ppermute | solution.py:642
  571.0 12.6 %collective-permute-done.65 = bf16[256,1024]{1,0:T(8,128)(2,1)S(1)} collective-permute-done((bf16[256,1024]{1,0:T(8,128)(2,1)}, bf16[256,1024]{1,0:T(8,128)(2,1)S(1)}, u32[]{:S(2)}, u32[]{:S(2)}) %collective-permute-start.65) | collective-permute-done | bytes 524320 | tf_op jit(solution)/shard_map/g_attA_h/ppermute | solution.py:642
  599.5 12.3 %collective-permute-done.69 = bf16[256,1024]{1,0:T(8,128)(2,1)S(1)} collective-permute-done((bf16[256,1024]{1,0:T(8,128)(2,1)}, bf16[256,1024]{1,0:T(8,128)(2,1)S(1)}, u32[]{:S(2)}, u32[]{:S(2)}) %collective-permute-start.69) | collective-permute-done | bytes 524320 | tf_op jit(solution)/shard_map/g_attB_h/ppermute | solution.py:642
  638.4 8.8 %collective-permute-done.75 = f32[]{:T(128)} collective-permute-done((f32[]{:T(128)}, f32[]{:T(128)}, u32[]{:S(2)}, u32[]{:S(2)}) %collective-permute-start.75) | collective-permute-done | bytes 36 | tf_op jit(solution)/shard_map/norm/ppermute | solution.py:724
  (403 shorter events, 279.4 us)
Async XLA Ops:
  3.4 32.4 %collective-permute-start.1 = (bf16[512,1024]{1,0:T(8,128)(2,1)S(1)}, bf16[512,1024]{1,0:T(8,128)(2,1)}, u32[]{:S(2)}, u32[]{:S(2)}) collective-permute-start(bf16[512,1024]{1,0:T(8,128)(2,1)S(1)} %pack.1), channel_id=1, source_target_pairs={{16,0},{0,16},{17,1},{1,17},{18,2},{2,18},{19,3},{3,19},{20,4},{4,... | collective-permute-start | bytes 3145736 | tf_op jit(solution)/shard_map/wqo0_x/ppermute | solution.py:642
  35.8 31.2 %collective-permute-start.5 = (bf16[512,1024]{1,0:T(8,128)(2,1)S(1)}, bf16[512,1024]{1,0:T(8,128)(2,1)S(1)}, u32[]{:S(2)}, u32[]{:S(2)}) collective-permute-start(bf16[512,1024]{1,0:T(8,128)(2,1)S(1)} %get-tuple-element.310), channel_id=1, source_target_pairs={{16,0},{0,16},{17,1},{1,17},{18,2},{2,18},{19,3},{3,19},{20,4},{4,... | collective-permute-start | bytes 3145736 | tf_op jit(solution)/shard_map/wu0_x/ppermute | solution.py:642
  67.1 34.9 %collective-permute-start.7 = (bf16[2,128,2048]{2,1,0:T(8,128)(2,1)S(1)}, bf16[2,128,2048]{2,1,0:T(8,128)(2,1)S(1)}, u32[]{:S(2)}, u32[]{:S(2)}) collective-permute-start(bf16[2,128,2048]{2,1,0:T(8,128)(2,1)S(1)} %constant_dynamic-update-slice_fusion.2.refs_2_), channel_id=1, source_target_pairs={{2,0},{0,2},{3,1},{1,3},{6,4},{4,6},{7,5},{5,7},{10,8},{8,10},{11,... | collective-permute-start | bytes 3145736 | tf_op jit(solution)/shard_map/a1_p/ppermute | solution.py:642
  67.3 34.8 %collective-permute-start.6 = (bf16[2,128,2048]{2,1,0:T(8,128)(2,1)S(1)}, bf16[2,128,2048]{2,1,0:T(8,128)(2,1)S(1)}, u32[]{:S(2)}, u32[]{:S(2)}) collective-permute-start(bf16[2,128,2048]{2,1,0:T(8,128)(2,1)S(1)} %constant_dynamic-update-slice_fusion.refs_0_), channel_id=1, source_target_pairs={{1,0},{0,1},{3,2},{2,3},{5,4},{4,5},{7,6},{6,7},{9,8},{8,9},{11,10... | collective-permute-start | bytes 3145736 | tf_op jit(solution)/shard_map/a0_q/ppermute | solution.py:642
  70.0 29.9 %collective-permute-start.8 = (bf16[256,1024]{1,0:T(8,128)(2,1)S(1)}, bf16[256,1024]{1,0:T(8,128)(2,1)S(1)}, u32[]{:S(2)}, u32[]{:S(2)}) collective-permute-start(bf16[256,1024]{1,0:T(8,128)(2,1)S(1)} %get-tuple-element.317), channel_id=1, source_target_pairs={{4,0},{0,4},{5,1},{1,5},{6,2},{2,6},{7,3},{3,7},{12,8},{8,12},{13,... | collective-permute-start | bytes 1572872 | tf_op jit(solution)/shard_map/wqoB_h/ppermute | solution.py:642
  71.5 28.3 %collective-permute-start.9 = (bf16[256,1024]{1,0:T(8,128)(2,1)S(1)}, bf16[256,1024]{1,0:T(8,128)(2,1)S(1)}, u32[]{:S(2)}, u32[]{:S(2)}) collective-permute-start(bf16[256,1024]{1,0:T(8,128)(2,1)S(1)} %collective-permute-done.4), channel_id=1, source_target_pairs={{16,0},{0,16},{17,1},{1,17},{18,2},{2,18},{19,3},{3,19},{20,4},{4,... | collective-permute-start | bytes 1572872 | tf_op jit(solution)/shard_map/wqoA1_x/ppermute | solution.py:642
  137.1 28.9 %collective-permute-start.19 = (bf16[1024,512]{1,0:T(8,128)(2,1)}, bf16[1024,512]{1,0:T(8,128)(2,1)}, u32[]{:S(2)}, u32[]{:S(2)}) collective-permute-start(bf16[1024,512]{1,0:T(8,128)(2,1)} %get-tuple-element.371), channel_id=1, source_target_pairs={{16,0},{0,16},{17,1},{1,17},{18,2},{2,18},{19,3},{3,19},{20,4},{4,... | collective-permute-start | bytes 3145736 | tf_op jit(solution)/shard_map/wd0_x/ppermute | solution.py:642
  168.0 37.0 %collective-permute-start.23 = (bf16[2,1024,512]{2,1,0:T(8,128)(2,1)S(1)}, bf16[2,1024,512]{2,1,0:T(8,128)(2,1)S(1)}, u32[]{:S(2)}, u32[]{:S(2)}) collective-permute-start(bf16[2,1024,512]{2,1,0:T(8,128)(2,1)S(1)} %pad_maximum_fusion.3.refs_9_.refs_1_), channel_id=1, source_target_pairs={{8,0},{0,8},{9,1},{1,9},{10,2},{2,10},{11,3},{3,11},{12,4},{4,12},... | collective-permute-start | bytes 6291464 | tf_op jit(solution)/shard_map/wd0_core/ppermute | solution.py:642
  168.1 34.7 %collective-permute-start.20 = (bf16[2,128,2048]{2,1,0:T(8,128)(2,1)S(1)}, bf16[2,128,2048]{2,1,0:T(8,128)(2,1)S(1)}, u32[]{:S(2)}, u32[]{:S(2)}) collective-permute-start(bf16[2,128,2048]{2,1,0:T(8,128)(2,1)S(1)} %copy-done.90), channel_id=1, source_target_pairs={{1,0},{0,1},{3,2},{2,3},{5,4},{4,5},{7,6},{6,7},{9,8},{8,9},{11,10... | collective-permute-start | bytes 3145736 | tf_op jit(solution)/shard_map/att0_q/ppermute | solution.py:642
  168.5 36.5 %collective-permute-start.21 = (bf16[2,128,2048]{2,1,0:T(8,128)(2,1)S(1)}, bf16[2,128,2048]{2,1,0:T(8,128)(2,1)S(1)}, u32[]{:S(2)}, u32[]{:S(2)}) collective-permute-start(bf16[2,128,2048]{2,1,0:T(8,128)(2,1)S(1)} %copy-done.89), channel_id=1, source_target_pairs={{2,0},{0,2},{3,1},{1,3},{6,4},{4,6},{7,5},{5,7},{10,8},{8,10},{11,... | collective-permute-start | bytes 3145736 | tf_op jit(solution)/shard_map/att1_p/ppermute | solution.py:642
  168.5 34.3 %collective-permute-start.22 = (bf16[256,1024]{1,0:T(8,128)(2,1)S(1)}, bf16[256,1024]{1,0:T(8,128)(2,1)S(1)}, u32[]{:S(2)}, u32[]{:S(2)}) collective-permute-start(bf16[256,1024]{1,0:T(8,128)(2,1)S(1)} %copy-done.88), channel_id=1, source_target_pairs={{4,0},{0,4},{5,1},{1,5},{6,2},{2,6},{7,3},{3,7},{12,8},{8,12},{13,... | collective-permute-start | bytes 1572872 | tf_op jit(solution)/shard_map/wuB_h/ppermute | solution.py:642
  205.0 30.7 %collective-permute-start.27 = (bf16[512,1024]{1,0:T(8,128)(2,1)S(1)}, bf16[512,1024]{1,0:T(8,128)(2,1)S(1)}, u32[]{:S(2)}, u32[]{:S(2)}) collective-permute-start(bf16[512,1024]{1,0:T(8,128)(2,1)S(1)} %constant_dynamic-update-slice_fusion.4), channel_id=1, source_target_pairs={{16,0},{0,16},{17,1},{1,17},{18,2},{2,18},{19,3},{3,19},{20,4},{4,... | collective-permute-start | bytes 3145736 | tf_op jit(solution)/shard_map/wu1_x/ppermute | solution.py:642
  417.6 35.5 %collective-permute-start.49 = (bf16[2,128,2048]{2,1,0:T(8,128)(2,1)}, bf16[2,128,2048]{2,1,0:T(8,128)(2,1)}, u32[]{:S(2)}, u32[]{:S(2)}) collective-permute-start(bf16[2,128,2048]{2,1,0:T(8,128)(2,1)} %constant_dynamic-update-slice_fusion.8.refs_4_), channel_id=1, source_target_pairs={{2,0},{0,2},{3,1},{1,3},{6,4},{4,6},{7,5},{5,7},{10,8},{8,10},{11,... | collective-permute-start | bytes 3145736 | tf_op jit(solution)/shard_map/datt1_p/ppermute | solution.py:642
  417.9 28.1 %collective-permute-start.51 = (bf16[1024,512]{1,0:T(8,128)(2,1)}, bf16[1024,512]{1,0:T(8,128)(2,1)}, u32[]{:S(2)}, u32[]{:S(2)}) collective-permute-start(bf16[1024,512]{1,0:T(8,128)(2,1)} %get-tuple-element.469), channel_id=1, source_target_pairs={{16,0},{0,16},{17,1},{1,17},{18,2},{2,18},{19,3},{3,19},{20,4},{4,... | collective-permute-start | bytes 3145736 | tf_op jit(solution)/shard_map/g_downB_x/ppermute | solution.py:642
  419.4 33.8 %collective-permute-start.48 = (bf16[2,128,2048]{2,1,0:T(8,128)(2,1)}, bf16[2,128,2048]{2,1,0:T(8,128)(2,1)}, u32[]{:S(2)}, u32[]{:S(2)}) collective-permute-start(bf16[2,128,2048]{2,1,0:T(8,128)(2,1)} %constant_dynamic-update-slice_fusion.6.refs_2_), channel_id=1, source_target_pairs={{1,0},{0,1},{3,2},{2,3},{5,4},{4,5},{7,6},{6,7},{9,8},{8,9},{11,10... | collective-permute-start | bytes 3145736 | tf_op jit(solution)/shard_map/datt0_q/ppermute | solution.py:642
  420.1 31.2 %collective-permute-start.50 = (bf16[512,512]{1,0:T(8,128)(2,1)}, bf16[512,512]{1,0:T(8,128)(2,1)S(1)}, u32[]{:S(2)}, u32[]{:S(2)}) collective-permute-start(bf16[512,512]{1,0:T(8,128)(2,1)} %g_downA_sum.1), channel_id=1, source_target_pairs={{4,0},{0,4},{5,1},{1,5},{6,2},{2,6},{7,3},{3,7},{12,8},{8,12},{13,... | collective-permute-start | bytes 1572872 | tf_op jit(solution)/shard_map/g_downA_h/ppermute | solution.py:642
  453.2 38.7 %collective-permute-start.54 = (bf16[2,128,2048]{2,1,0:T(8,128)(2,1)}, bf16[2,128,2048]{2,1,0:T(8,128)(2,1)}, u32[]{:S(2)}, u32[]{:S(2)}) collective-permute-start(bf16[2,128,2048]{2,1,0:T(8,128)(2,1)} %get-tuple-element.487), channel_id=1, source_target_pairs={{1,0},{0,1},{3,2},{2,3},{5,4},{4,5},{7,6},{6,7},{9,8},{8,9},{11,10... | collective-permute-start | bytes 3145736 | tf_op jit(solution)/shard_map/ff0_q/ppermute | solution.py:642
  453.9 38.0 %collective-permute-start.55 = (bf16[2,128,2048]{2,1,0:T(8,128)(2,1)}, bf16[2,128,2048]{2,1,0:T(8,128)(2,1)}, u32[]{:S(2)}, u32[]{:S(2)}) collective-permute-start(bf16[2,128,2048]{2,1,0:T(8,128)(2,1)} %get-tuple-element.488), channel_id=1, source_target_pairs={{2,0},{0,2},{3,1},{1,3},{6,4},{4,6},{7,5},{5,7},{10,8},{8,10},{11,... | collective-permute-start | bytes 3145736 | tf_op jit(solution)/shard_map/ff1_p/ppermute | solution.py:642
  454.7 37.2 %collective-permute-start.53 = (bf16[512,1024]{1,0:T(8,128)(2,1)}, bf16[512,1024]{1,0:T(8,128)(2,1)}, u32[]{:S(2)}, u32[]{:S(2)}) collective-permute-start(bf16[512,1024]{1,0:T(8,128)(2,1)} %get-tuple-element.486), channel_id=1, source_target_pairs={{16,0},{0,16},{17,1},{1,17},{18,2},{2,18},{19,3},{3,19},{20,4},{4,... | collective-permute-start | bytes 3145736 | tf_op jit(solution)/shard_map/g_upA_x/ppermute | solution.py:642
  455.3 36.5 %collective-permute-start.52 = (bf16[512,512]{1,0:T(8,128)(2,1)}, bf16[512,512]{1,0:T(8,128)(2,1)}, u32[]{:S(2)}, u32[]{:S(2)}) collective-permute-start(bf16[512,512]{1,0:T(8,128)(2,1)} %g_downB_sum.1), channel_id=1, source_target_pairs={{4,0},{0,4},{5,1},{1,5},{6,2},{2,6},{7,3},{3,7},{12,8},{8,12},{13,... | collective-permute-start | bytes 1572872 | tf_op jit(solution)/shard_map/g_downB_h/ppermute | solution.py:642
  492.0 36.9 %collective-permute-start.56 = (bf16[2,128,2048]{2,1,0:T(8,128)(2,1)}, bf16[2,128,2048]{2,1,0:T(8,128)(2,1)}, u32[]{:S(2)}, u32[]{:S(2)}) collective-permute-start(bf16[2,128,2048]{2,1,0:T(8,128)(2,1)} %get-tuple-element.508), channel_id=1, source_target_pairs={{1,0},{0,1},{3,2},{2,3},{5,4},{4,5},{7,6},{6,7},{9,8},{8,9},{11,10... | collective-permute-start | bytes 3145736 | tf_op jit(solution)/shard_map/da0_q/ppermute | solution.py:642
  493.3 36.8 %collective-permute-start.57 = (bf16[2,128,2048]{2,1,0:T(8,128)(2,1)}, bf16[2,128,2048]{2,1,0:T(8,128)(2,1)}, u32[]{:S(2)}, u32[]{:S(2)}) collective-permute-start(bf16[2,128,2048]{2,1,0:T(8,128)(2,1)} %get-tuple-element.509), channel_id=1, source_target_pairs={{2,0},{0,2},{3,1},{1,3},{6,4},{4,6},{7,5},{5,7},{10,8},{8,10},{11,... | collective-permute-start | bytes 3145736 | tf_op jit(solution)/shard_map/da1_p/ppermute | solution.py:642
  498.6 30.3 %collective-permute-start.59 = (bf16[256,1024]{1,0:T(8,128)(2,1)}, bf16[256,1024]{1,0:T(8,128)(2,1)S(1)}, u32[]{:S(2)}, u32[]{:S(2)}) collective-permute-start(bf16[256,1024]{1,0:T(8,128)(2,1)} %get-tuple-element.521), channel_id=1, source_target_pairs={{4,0},{0,4},{5,1},{1,5},{6,2},{2,6},{7,3},{3,7},{12,8},{8,12},{13,... | collective-permute-start | bytes 1572872 | tf_op jit(solution)/shard_map/g_upA_h/ppermute | solution.py:642
  620.3 46.4 %collective-permute-start.77 = (bf16[4,32,2048]{2,1,0:T(8,128)(2,1)}, bf16[4,32,2048]{2,1,0:T(8,128)(2,1)S(1)}, u32[]{:S(2)}, u32[]{:S(2)}) collective-permute-start(bf16[4,32,2048]{2,1,0:T(8,128)(2,1)} %slice.55), channel_id=1, source_target_pairs={{4,0},{0,4},{5,1},{1,5},{6,2},{2,6},{7,3},{3,7},{12,8},{8,12},{13,... | collective-permute-start | bytes 1572872 | tf_op jit(solution)/shard_map/input_grad_h/ppermute | solution.py:642
  (147 other events, 1928.5 us)

commit v7 on v6

--- a/solution.py
+++ b/solution.py
@@ -717,7 +717,7 @@
         )
 
     def total(self, v):
-        for axis, size in (("core", 2), ("q", 2), ("x", self.X), ("p", 2), ("h", self.H)):
+        for axis, size in (("p", 2), ("core", 2), ("q", 2), ("x", self.X), ("h", self.H)):
             step = 1
             while step < size:
                 with jax.named_scope("norm"):

time: 687 us -> 685 us (level)
  no operation moved by 1% of the time
where the time goes in v7:
time: 685 us; the launch traced here: 675 us
  waiting for transfers between devices  297 us (43%)
  Pallas kernels  199 us (29%)
  starting transfers between devices  81.3 us (12%)
  local copies, waits for them, and re-layouts  50.7 us (7%)
  other arithmetic  37.1 us (5%)
  between operations  8.77 us (1%)
    ppermute x73, waiting for transfers between devices, shifted(): lax.ppermute(v, axis, [((dst + offset) % size, dst) for dst in range(size)])  284 us
    pallas_call x5, Pallas kernels, group_call(): pl.pallas_call(lambda *refs: kernel(nh, nd, *refs), name=name, grid=(step...  113 us
    ppermute x73, starting transfers between devices, shifted(): lax.ppermute(v, axis, [((dst + offset) % size, dst) for dst in range(size)])  73.1 us
    pallas_call x7, Pallas kernels, one_step(): pl.pallas_call(kernel, name=name, grid=(1,), in_specs=[pl.BlockSpec((v.sh...  40.3 us
    unnamed x191, local copies, waits for them, and re-layouts  37.3 us
    pallas_call x10, Pallas kernels, image_call(): pl.pallas_call(kernel, name=name, grid=(steps,), in_specs=[cut(seen(v.sha...  20.8 us
    pallas_call x2, Pallas kernels, gradient(): pl.pallas_call(kernel, name=name, grid=(nh, half), in_specs=in_specs, out...  15.9 us
  transfers between devices with their start and end apart: 78, of which 38 were waited for; matrix products, arithmetic and copies ran while one was open for 7% of the time, Pallas kernels for 25%

profile of v7, /device:TPU:0, one launch (start us, length us, event | category | flops | bytes accessed | tf_op | source)
XLA Modules:
  0.0 675.1 jit_solution(17881499555637720676)
XLA Ops:
  17.5 18.2 %collective-permute-done = bf16[4,32,2048]{2,1,0:T(8,128)(2,1)} collective-permute-done((bf16[4,32,2048]{2,1,0:T(8,128)(2,1)}, bf16[4,32,2048]{2,1,0:T(8,128)(2,1)}, u32[]{:S(2)}, u32[]{:S(2)}) %collective-permute-start) | collective-permute-done | bytes 524320 | tf_op jit(solution)/shard_map/stream_h/ppermute | solution.py:642
  45.8 15.0 %collective-permute-done.2 = bf16[2,64,2048]{2,1,0:T(8,128)(2,1)S(1)} collective-permute-done((bf16[2,64,2048]{2,1,0:T(8,128)(2,1)S(1)}, bf16[2,64,2048]{2,1,0:T(8,128)(2,1)S(1)}, u32[]{:S(2)}, u32[]{:S(2)}) %collective-permute-start.2) | collective-permute-done | bytes 524320 | tf_op jit(solution)/shard_map/a0_p/ppermute | solution.py:642
  73.3 26.5 %collective-permute-done.8 = bf16[256,1024]{1,0:T(8,128)(2,1)S(1)} collective-permute-done((bf16[256,1024]{1,0:T(8,128)(2,1)S(1)}, bf16[256,1024]{1,0:T(8,128)(2,1)S(1)}, u32[]{:S(2)}, u32[]{:S(2)}) %collective-permute-start.8) | collective-permute-done | bytes 524320 | tf_op jit(solution)/shard_map/wqoB_h/ppermute | solution.py:642
  105.4 13.2 %collective-permute-done.11 = bf16[2,32,2048]{2,1,0:T(8,128)(2,1)S(1)} collective-permute-done((bf16[2,32,2048]{2,1,0:T(8,128)(2,1)S(1)}, bf16[2,32,2048]{2,1,0:T(8,128)(2,1)S(1)}, u32[]{:S(2)}, u32[]{:S(2)}) %collective-permute-start.11) | collective-permute-done | bytes 262176 | tf_op jit(solution)/shard_map/cotA_h/ppermute | solution.py:642
  122.6 13.1 %collective-permute-done.14 = bf16[2,32,2048]{2,1,0:T(8,128)(2,1)S(1)} collective-permute-done((bf16[2,32,2048]{2,1,0:T(8,128)(2,1)S(1)}, bf16[2,32,2048]{2,1,0:T(8,128)(2,1)S(1)}, u32[]{:S(2)}, u32[]{:S(2)}) %collective-permute-start.14) | collective-permute-done | bytes 262176 | tf_op jit(solution)/shard_map/cotB_h/ppermute | solution.py:642
  143.5 17.7 %attention.1 = (bf16[2,2,256,2048]{3,2,1,0:T(8,128)(2,1)}, bf16[2,2,256,1536]{3,2,1,0:T(8,128)(2,1)}, bf16[2,2,256,512]{3,2,1,0:T(8,128)(2,1)}, bf16[2,2,4,256,2...) custom-call(bf16[2,128,2048]{2,1,0:T(8,128)(2,1)} %copy-done.68, ...), custom_call_target="tpu_custom_call" | custom-call | tf_op jit(solution)/shard_map/attention/pallas_call | solution.py:278
  172.1 30.7 %collective-permute-done.22 = bf16[256,1024]{1,0:T(8,128)(2,1)S(1)} collective-permute-done((bf16[256,1024]{1,0:T(8,128)(2,1)S(1)}, bf16[256,1024]{1,0:T(8,128)(2,1)S(1)}, u32[]{:S(2)}, u32[]{:S(2)}) %collective-permute-start.22) | collective-permute-done | bytes 524320 | tf_op jit(solution)/shard_map/wuB_h/ppermute | solution.py:642
  212.6 15.3 %collective-permute-done.24.refs_4_ = bf16[2,64,2048]{2,1,0:T(8,128)(2,1)S(1)} collective-permute-done((bf16[2,64,2048]{2,1,0:T(8,128)(2,1)S(1)}, bf16[2,64,2048]{2,1,0:T(8,128)(2,1)S(1)}, u32[]{:S(2)}, u32[]{:S(2)}) %collective-permute-start.24) | collective-permute-done | bytes 524320 | tf_op jit(solution)/shard_map/att0_p/ppermute | solution.py:642
  239.8 17.6 %collective-permute-done.28 = bf16[2,64,2048]{2,1,0:T(8,128)(2,1)S(1)} collective-permute-done((bf16[2,64,2048]{2,1,0:T(8,128)(2,1)S(1)}, bf16[2,64,2048]{2,1,0:T(8,128)(2,1)S(1)}, u32[]{:S(2)}, u32[]{:S(2)}) %collective-permute-start.28) | collective-permute-done | bytes 524320 | tf_op jit(solution)/shard_map/b0_p/ppermute | solution.py:642
  267.4 8.1 %collective-permute-done.34 = bf16[512,512]{1,0:T(8,128)(2,1)S(1)} collective-permute-done((bf16[512,512]{1,0:T(8,128)(2,1)S(1)}, bf16[512,512]{1,0:T(8,128)(2,1)S(1)}, u32[]{:S(2)}, u32[]{:S(2)}) %collective-permute-start.34) | collective-permute-done | bytes 524320 | tf_op jit(solution)/shard_map/wdB1_x/ppermute | solution.py:642
  275.4 10.2 %collective-permute-done.32.refs_1_ = bf16[2,128,2048]{2,1,0:T(8,128)(2,1)S(1)} collective-permute-done((bf16[2,128,2048]{2,1,0:T(8,128)(2,1)S(1)}, bf16[2,128,2048]{2,1,0:T(8,128)(2,1)S(1)}, u32[]{:S(2)}, u32[]{:S(2)}) %collective-permute-start.32) | collective-permute-done | bytes 1048608 | tf_op jit(solution)/shard_map/b0_q/ppermute | solution.py:642
  290.6 19.5 %up.1 = (bf16[2,2,256,2048]{3,2,1,0:T(8,128)(2,1)}, bf16[2,2,256,2048]{3,2,1,0:T(8,128)(2,1)}, bf16[2,2,256,2048]{3,2,1,0:T(8,128)(2,1)}) custom-call(bf16[2,128,2048]{2,1,0:T(8,128)(2,1)} %copy-done.66, bf16[2,128,2048]{2,1,0:T(8,128)(2,1)} %copy-done.81, bf16[2,128,2048]{2,1,0:T(8,128)(2,1)} %copy-done.67, bf16[2,128,2048]{2,1,0:T(8,128)(2,1)} %copy-done.82, ...), custom_call_target="tpu_custom_call" | custom-call | tf_op jit(solution)/shard_map/up/pallas_call | solution.py:278
  315.9 26.6 %up_back.1 = (bf16[2,2,256,2048]{3,2,1,0:T(8,128)(2,1)}, bf16[2,2,256,2048]{3,2,1,0:T(8,128)(2,1)}, bf16[2,128,2048]{2,1,0:T(8,128)(2,1)}, bf16[2,128,2048]{2,1,...) custom-call(bf16[2,128,2048]{2,1,0:T(8,128)(2,1)} %pad_maximum_fusion.10.refs_0_, ...), custom_call_target="tpu_custom_call" | custom-call | tf_op jit(solution)/shard_map/up_back/pallas_call | solution.py:278
  360.5 8.0 %g_down_send.1 = bf16[2048,1024]{1,0:T(8,128)(2,1)S(1)} custom-call(bf16[1024,2048]{1,0:T(8,128)(2,1)} %bitcast.101, bf16[1024,2048]{1,0:T(8,128)(2,1)} %bitcast.109), custom_call_target="tpu_custom_call" | custom-call | tf_op jit(solution)/shard_map/g_down_send/pallas_call | solution.py:484
  377.7 9.7 %g_down_keep.1 = (bf16[512,512]{1,0:T(8,128)(2,1)}, bf16[1024,512]{1,0:T(8,128)(2,1)}, bf16[512,512]{1,0:T(8,128)(2,1)}, bf16[512,512]{1,0:T(8,128)(2,1)}, bf16[...) custom-call(bf16[1024,2048]{1,0:T(8,128)(2,1)} %bitcast.102, bf16[1024,2048]{1,0:T(8,128)(2,1)} %bitcast.110, ...), custom_call_target="tpu_custom_call" | custom-call | tf_op jit(solution)/shard_map/g_down_keep/pallas_call | solution.py:497
  422.1 14.3 %down.1 = (bf16[2,128,2048]{2,1,0:T(8,128)(2,1)}, bf16[2,128,2048]{2,1,0:T(8,128)(2,1)}, bf16[2,128,2048]{2,1,0:T(8,128)(2,1)}, bf16[2,128,2048]{2,1,0:T(8,128)(2,1)}) custom-call(bf16[2,2,256,2048]{3,2,1,0:T(8,128)(2,1)} %get-tuple-element.480.refs_0_, bf16[2,1024,512]{2,1,0:T(8,128)(2,1)} %copy-done.50, bf16[2,1024,512]{2,1,0:T(8,128)(2,1)} %copy-done.59, ...), custom_call_target="tpu_custom_call" | custom-call | tf_op jit(solution)/shard_map/down/pallas_call | solution.py:278
  436.4 9.6 %g_up_keep.1 = (bf16[512,1024]{1,0:T(8,128)(2,1)}, bf16[512,1024]{1,0:T(8,128)(2,1)}, bf16[512,1024]{1,0:T(8,128)(2,1)}, bf16[512,1024]{1,0:T(8,128)(2,1)}) custom-call(bf16[1024,2048]{1,0:T(8,128)(2,1)} %bitcast.106, bf16[1024,2048]{1,0:T(8,128)(2,1)} %bitcast.108, bf16[1024,2048]{1,0:T(8,128)(2,1)} %collective-permute-done.47.sent), custom_call_target="tpu_custom_call" | custom-call | tf_op jit(solution)/shard_map/g_up_keep/pallas_call | solution.py:497
  456.8 35.0 %attention_back.1 = (bf16[2,128,2048]{2,1,0:T(8,128)(2,1)}, bf16[2,128,2048]{2,1,0:T(8,128)(2,1)}, bf16[2,128,2048]{2,1,0:T(8,128)(2,1)}, bf16[2,128,2048]{2,1,0...) custom-call(bf16[2048,1024]{1,0:T(8,128)(2,1)} %bitcast.103, ...), custom_call_target="tpu_custom_call" | custom-call | tf_op jit(solution)/shard_map/attention_back/pallas_call | solution.py:278
  500.0 11.2 %g_att_keep.1 = (bf16[512,1024]{1,0:T(8,128)(2,1)}, bf16[512,1024]{1,0:T(8,128)(2,1)}, bf16[512,1024]{1,0:T(8,128)(2,1)}, bf16[512,1024]{1,0:T(8,128)(2,1)}) custom-call(bf16[2048,1024]{1,0:T(8,128)(2,1)} %bitcast.104, bf16[1024,1536]{1,0:T(8,128)(2,1)} %bitcast.115, bf16[1024,2048]{1,0:T(8,128)(2,1)} %bitcast.114, bf16[1024,512]{1,0:T(8,128)(2,1)} %bitcast.111, ...), custom_call_target="tpu_custom_call" | custom-call | tf_op jit(solution)/shard_map/g_att_keep/pallas_call | solution.py:497
  511.3 17.6 %collective-permute-done.59 = bf16[256,1024]{1,0:T(8,128)(2,1)S(1)} collective-permute-done((bf16[256,1024]{1,0:T(8,128)(2,1)}, bf16[256,1024]{1,0:T(8,128)(2,1)S(1)}, u32[]{:S(2)}, u32[]{:S(2)}) %collective-permute-start.59) | collective-permute-done | bytes 524320 | tf_op jit(solution)/shard_map/g_upA_h/ppermute | solution.py:642
  537.3 17.5 %collective-permute-done.61.refs_1_ = bf16[512,1024]{1,0:T(8,128)(2,1)} collective-permute-done((bf16[512,1024]{1,0:T(8,128)(2,1)}, bf16[512,1024]{1,0:T(8,128)(2,1)}, u32[]{:S(2)}, u32[]{:S(2)}) %collective-permute-start.61) | collective-permute-done | bytes 1048608 | tf_op jit(solution)/shard_map/g_attA_x/ppermute | solution.py:642
  571.0 12.6 %collective-permute-done.65 = bf16[256,1024]{1,0:T(8,128)(2,1)S(1)} collective-permute-done((bf16[256,1024]{1,0:T(8,128)(2,1)}, bf16[256,1024]{1,0:T(8,128)(2,1)S(1)}, u32[]{:S(2)}, u32[]{:S(2)}) %collective-permute-start.65) | collective-permute-done | bytes 524320 | tf_op jit(solution)/shard_map/g_attA_h/ppermute | solution.py:642
  599.5 12.3 %collective-permute-done.69 = bf16[256,1024]{1,0:T(8,128)(2,1)S(1)} collective-permute-done((bf16[256,1024]{1,0:T(8,128)(2,1)}, bf16[256,1024]{1,0:T(8,128)(2,1)S(1)}, u32[]{:S(2)}, u32[]{:S(2)}) %collective-permute-start.69) | collective-permute-done | bytes 524320 | tf_op jit(solution)/shard_map/g_attB_h/ppermute | solution.py:642
  636.3 10.2 %collective-permute-done.75 = f32[]{:T(128)} collective-permute-done((f32[]{:T(128)}, f32[]{:T(128)}, u32[]{:S(2)}, u32[]{:S(2)}) %collective-permute-start.75) | collective-permute-done | bytes 36 | tf_op jit(solution)/shard_map/norm/ppermute | solution.py:724
  (403 shorter events, 276.7 us)
Async XLA Ops:
  3.4 32.4 %collective-permute-start.1 = (bf16[512,1024]{1,0:T(8,128)(2,1)S(1)}, bf16[512,1024]{1,0:T(8,128)(2,1)}, u32[]{:S(2)}, u32[]{:S(2)}) collective-permute-start(bf16[512,1024]{1,0:T(8,128)(2,1)S(1)} %pack.1), channel_id=1, source_target_pairs={{16,0},{0,16},{17,1},{1,17},{18,2},{2,18},{19,3},{3,19},{20,4},{4,... | collective-permute-start | bytes 3145736 | tf_op jit(solution)/shard_map/wqo0_x/ppermute | solution.py:642
  35.8 31.2 %collective-permute-start.5 = (bf16[512,1024]{1,0:T(8,128)(2,1)S(1)}, bf16[512,1024]{1,0:T(8,128)(2,1)S(1)}, u32[]{:S(2)}, u32[]{:S(2)}) collective-permute-start(bf16[512,1024]{1,0:T(8,128)(2,1)S(1)} %get-tuple-element.310), channel_id=1, source_target_pairs={{16,0},{0,16},{17,1},{1,17},{18,2},{2,18},{19,3},{3,19},{20,4},{4,... | collective-permute-start | bytes 3145736 | tf_op jit(solution)/shard_map/wu0_x/ppermute | solution.py:642
  67.1 34.9 %collective-permute-start.7 = (bf16[2,128,2048]{2,1,0:T(8,128)(2,1)S(1)}, bf16[2,128,2048]{2,1,0:T(8,128)(2,1)S(1)}, u32[]{:S(2)}, u32[]{:S(2)}) collective-permute-start(bf16[2,128,2048]{2,1,0:T(8,128)(2,1)S(1)} %constant_dynamic-update-slice_fusion.2.refs_2_), channel_id=1, source_target_pairs={{2,0},{0,2},{3,1},{1,3},{6,4},{4,6},{7,5},{5,7},{10,8},{8,10},{11,... | collective-permute-start | bytes 3145736 | tf_op jit(solution)/shard_map/a1_p/ppermute | solution.py:642
  67.3 34.8 %collective-permute-start.6 = (bf16[2,128,2048]{2,1,0:T(8,128)(2,1)S(1)}, bf16[2,128,2048]{2,1,0:T(8,128)(2,1)S(1)}, u32[]{:S(2)}, u32[]{:S(2)}) collective-permute-start(bf16[2,128,2048]{2,1,0:T(8,128)(2,1)S(1)} %constant_dynamic-update-slice_fusion.refs_0_), channel_id=1, source_target_pairs={{1,0},{0,1},{3,2},{2,3},{5,4},{4,5},{7,6},{6,7},{9,8},{8,9},{11,10... | collective-permute-start | bytes 3145736 | tf_op jit(solution)/shard_map/a0_q/ppermute | solution.py:642
  70.0 29.9 %collective-permute-start.8 = (bf16[256,1024]{1,0:T(8,128)(2,1)S(1)}, bf16[256,1024]{1,0:T(8,128)(2,1)S(1)}, u32[]{:S(2)}, u32[]{:S(2)}) collective-permute-start(bf16[256,1024]{1,0:T(8,128)(2,1)S(1)} %get-tuple-element.317), channel_id=1, source_target_pairs={{4,0},{0,4},{5,1},{1,5},{6,2},{2,6},{7,3},{3,7},{12,8},{8,12},{13,... | collective-permute-start | bytes 1572872 | tf_op jit(solution)/shard_map/wqoB_h/ppermute | solution.py:642
  71.5 28.3 %collective-permute-start.9 = (bf16[256,1024]{1,0:T(8,128)(2,1)S(1)}, bf16[256,1024]{1,0:T(8,128)(2,1)S(1)}, u32[]{:S(2)}, u32[]{:S(2)}) collective-permute-start(bf16[256,1024]{1,0:T(8,128)(2,1)S(1)} %collective-permute-done.4), channel_id=1, source_target_pairs={{16,0},{0,16},{17,1},{1,17},{18,2},{2,18},{19,3},{3,19},{20,4},{4,... | collective-permute-start | bytes 1572872 | tf_op jit(solution)/shard_map/wqoA1_x/ppermute | solution.py:642
  137.1 28.9 %collective-permute-start.19 = (bf16[1024,512]{1,0:T(8,128)(2,1)}, bf16[1024,512]{1,0:T(8,128)(2,1)}, u32[]{:S(2)}, u32[]{:S(2)}) collective-permute-start(bf16[1024,512]{1,0:T(8,128)(2,1)} %get-tuple-element.371), channel_id=1, source_target_pairs={{16,0},{0,16},{17,1},{1,17},{18,2},{2,18},{19,3},{3,19},{20,4},{4,... | collective-permute-start | bytes 3145736 | tf_op jit(solution)/shard_map/wd0_x/ppermute | solution.py:642
  168.0 37.0 %collective-permute-start.23 = (bf16[2,1024,512]{2,1,0:T(8,128)(2,1)S(1)}, bf16[2,1024,512]{2,1,0:T(8,128)(2,1)S(1)}, u32[]{:S(2)}, u32[]{:S(2)}) collective-permute-start(bf16[2,1024,512]{2,1,0:T(8,128)(2,1)S(1)} %pad_maximum_fusion.3.refs_9_.refs_1_), channel_id=1, source_target_pairs={{8,0},{0,8},{9,1},{1,9},{10,2},{2,10},{11,3},{3,11},{12,4},{4,12},... | collective-permute-start | bytes 6291464 | tf_op jit(solution)/shard_map/wd0_core/ppermute | solution.py:642
  168.1 34.7 %collective-permute-start.20 = (bf16[2,128,2048]{2,1,0:T(8,128)(2,1)S(1)}, bf16[2,128,2048]{2,1,0:T(8,128)(2,1)S(1)}, u32[]{:S(2)}, u32[]{:S(2)}) collective-permute-start(bf16[2,128,2048]{2,1,0:T(8,128)(2,1)S(1)} %copy-done.90), channel_id=1, source_target_pairs={{1,0},{0,1},{3,2},{2,3},{5,4},{4,5},{7,6},{6,7},{9,8},{8,9},{11,10... | collective-permute-start | bytes 3145736 | tf_op jit(solution)/shard_map/att0_q/ppermute | solution.py:642
  168.5 36.5 %collective-permute-start.21 = (bf16[2,128,2048]{2,1,0:T(8,128)(2,1)S(1)}, bf16[2,128,2048]{2,1,0:T(8,128)(2,1)S(1)}, u32[]{:S(2)}, u32[]{:S(2)}) collective-permute-start(bf16[2,128,2048]{2,1,0:T(8,128)(2,1)S(1)} %copy-done.89), channel_id=1, source_target_pairs={{2,0},{0,2},{3,1},{1,3},{6,4},{4,6},{7,5},{5,7},{10,8},{8,10},{11,... | collective-permute-start | bytes 3145736 | tf_op jit(solution)/shard_map/att1_p/ppermute | solution.py:642
  168.5 34.3 %collective-permute-start.22 = (bf16[256,1024]{1,0:T(8,128)(2,1)S(1)}, bf16[256,1024]{1,0:T(8,128)(2,1)S(1)}, u32[]{:S(2)}, u32[]{:S(2)}) collective-permute-start(bf16[256,1024]{1,0:T(8,128)(2,1)S(1)} %copy-done.88), channel_id=1, source_target_pairs={{4,0},{0,4},{5,1},{1,5},{6,2},{2,6},{7,3},{3,7},{12,8},{8,12},{13,... | collective-permute-start | bytes 1572872 | tf_op jit(solution)/shard_map/wuB_h/ppermute | solution.py:642
  205.0 30.7 %collective-permute-start.27 = (bf16[512,1024]{1,0:T(8,128)(2,1)S(1)}, bf16[512,1024]{1,0:T(8,128)(2,1)S(1)}, u32[]{:S(2)}, u32[]{:S(2)}) collective-permute-start(bf16[512,1024]{1,0:T(8,128)(2,1)S(1)} %constant_dynamic-update-slice_fusion.4), channel_id=1, source_target_pairs={{16,0},{0,16},{17,1},{1,17},{18,2},{2,18},{19,3},{3,19},{20,4},{4,... | collective-permute-start | bytes 3145736 | tf_op jit(solution)/shard_map/wu1_x/ppermute | solution.py:642
  417.6 35.5 %collective-permute-start.49 = (bf16[2,128,2048]{2,1,0:T(8,128)(2,1)}, bf16[2,128,2048]{2,1,0:T(8,128)(2,1)}, u32[]{:S(2)}, u32[]{:S(2)}) collective-permute-start(bf16[2,128,2048]{2,1,0:T(8,128)(2,1)} %constant_dynamic-update-slice_fusion.8.refs_4_), channel_id=1, source_target_pairs={{2,0},{0,2},{3,1},{1,3},{6,4},{4,6},{7,5},{5,7},{10,8},{8,10},{11,... | collective-permute-start | bytes 3145736 | tf_op jit(solution)/shard_map/datt1_p/ppermute | solution.py:642
  417.9 28.1 %collective-permute-start.51 = (bf16[1024,512]{1,0:T(8,128)(2,1)}, bf16[1024,512]{1,0:T(8,128)(2,1)}, u32[]{:S(2)}, u32[]{:S(2)}) collective-permute-start(bf16[1024,512]{1,0:T(8,128)(2,1)} %get-tuple-element.469), channel_id=1, source_target_pairs={{16,0},{0,16},{17,1},{1,17},{18,2},{2,18},{19,3},{3,19},{20,4},{4,... | collective-permute-start | bytes 3145736 | tf_op jit(solution)/shard_map/g_downB_x/ppermute | solution.py:642
  419.4 33.8 %collective-permute-start.48 = (bf16[2,128,2048]{2,1,0:T(8,128)(2,1)}, bf16[2,128,2048]{2,1,0:T(8,128)(2,1)}, u32[]{:S(2)}, u32[]{:S(2)}) collective-permute-start(bf16[2,128,2048]{2,1,0:T(8,128)(2,1)} %constant_dynamic-update-slice_fusion.6.refs_2_), channel_id=1, source_target_pairs={{1,0},{0,1},{3,2},{2,3},{5,4},{4,5},{7,6},{6,7},{9,8},{8,9},{11,10... | collective-permute-start | bytes 3145736 | tf_op jit(solution)/shard_map/datt0_q/ppermute | solution.py:642
  420.1 31.2 %collective-permute-start.50 = (bf16[512,512]{1,0:T(8,128)(2,1)}, bf16[512,512]{1,0:T(8,128)(2,1)S(1)}, u32[]{:S(2)}, u32[]{:S(2)}) collective-permute-start(bf16[512,512]{1,0:T(8,128)(2,1)} %g_downA_sum.1), channel_id=1, source_target_pairs={{4,0},{0,4},{5,1},{1,5},{6,2},{2,6},{7,3},{3,7},{12,8},{8,12},{13,... | collective-permute-start | bytes 1572872 | tf_op jit(solution)/shard_map/g_downA_h/ppermute | solution.py:642
  453.2 38.7 %collective-permute-start.54 = (bf16[2,128,2048]{2,1,0:T(8,128)(2,1)}, bf16[2,128,2048]{2,1,0:T(8,128)(2,1)}, u32[]{:S(2)}, u32[]{:S(2)}) collective-permute-start(bf16[2,128,2048]{2,1,0:T(8,128)(2,1)} %get-tuple-element.487), channel_id=1, source_target_pairs={{1,0},{0,1},{3,2},{2,3},{5,4},{4,5},{7,6},{6,7},{9,8},{8,9},{11,10... | collective-permute-start | bytes 3145736 | tf_op jit(solution)/shard_map/ff0_q/ppermute | solution.py:642
  453.9 38.0 %collective-permute-start.55 = (bf16[2,128,2048]{2,1,0:T(8,128)(2,1)}, bf16[2,128,2048]{2,1,0:T(8,128)(2,1)}, u32[]{:S(2)}, u32[]{:S(2)}) collective-permute-start(bf16[2,128,2048]{2,1,0:T(8,128)(2,1)} %get-tuple-element.488), channel_id=1, source_target_pairs={{2,0},{0,2},{3,1},{1,3},{6,4},{4,6},{7,5},{5,7},{10,8},{8,10},{11,... | collective-permute-start | bytes 3145736 | tf_op jit(solution)/shard_map/ff1_p/ppermute | solution.py:642
  454.7 37.2 %collective-permute-start.53 = (bf16[512,1024]{1,0:T(8,128)(2,1)}, bf16[512,1024]{1,0:T(8,128)(2,1)}, u32[]{:S(2)}, u32[]{:S(2)}) collective-permute-start(bf16[512,1024]{1,0:T(8,128)(2,1)} %get-tuple-element.486), channel_id=1, source_target_pairs={{16,0},{0,16},{17,1},{1,17},{18,2},{2,18},{19,3},{3,19},{20,4},{4,... | collective-permute-start | bytes 3145736 | tf_op jit(solution)/shard_map/g_upA_x/ppermute | solution.py:642
  455.3 36.5 %collective-permute-start.52 = (bf16[512,512]{1,0:T(8,128)(2,1)}, bf16[512,512]{1,0:T(8,128)(2,1)}, u32[]{:S(2)}, u32[]{:S(2)}) collective-permute-start(bf16[512,512]{1,0:T(8,128)(2,1)} %g_downB_sum.1), channel_id=1, source_target_pairs={{4,0},{0,4},{5,1},{1,5},{6,2},{2,6},{7,3},{3,7},{12,8},{8,12},{13,... | collective-permute-start | bytes 1572872 | tf_op jit(solution)/shard_map/g_downB_h/ppermute | solution.py:642
  492.0 36.9 %collective-permute-start.56 = (bf16[2,128,2048]{2,1,0:T(8,128)(2,1)}, bf16[2,128,2048]{2,1,0:T(8,128)(2,1)}, u32[]{:S(2)}, u32[]{:S(2)}) collective-permute-start(bf16[2,128,2048]{2,1,0:T(8,128)(2,1)} %get-tuple-element.508), channel_id=1, source_target_pairs={{1,0},{0,1},{3,2},{2,3},{5,4},{4,5},{7,6},{6,7},{9,8},{8,9},{11,10... | collective-permute-start | bytes 3145736 | tf_op jit(solution)/shard_map/da0_q/ppermute | solution.py:642
  493.3 36.8 %collective-permute-start.57 = (bf16[2,128,2048]{2,1,0:T(8,128)(2,1)}, bf16[2,128,2048]{2,1,0:T(8,128)(2,1)}, u32[]{:S(2)}, u32[]{:S(2)}) collective-permute-start(bf16[2,128,2048]{2,1,0:T(8,128)(2,1)} %get-tuple-element.509), channel_id=1, source_target_pairs={{2,0},{0,2},{3,1},{1,3},{6,4},{4,6},{7,5},{5,7},{10,8},{8,10},{11,... | collective-permute-start | bytes 3145736 | tf_op jit(solution)/shard_map/da1_p/ppermute | solution.py:642
  498.6 30.3 %collective-permute-start.59 = (bf16[256,1024]{1,0:T(8,128)(2,1)}, bf16[256,1024]{1,0:T(8,128)(2,1)S(1)}, u32[]{:S(2)}, u32[]{:S(2)}) collective-permute-start(bf16[256,1024]{1,0:T(8,128)(2,1)} %get-tuple-element.521), channel_id=1, source_target_pairs={{4,0},{0,4},{5,1},{1,5},{6,2},{2,6},{7,3},{3,7},{12,8},{8,12},{13,... | collective-permute-start | bytes 1572872 | tf_op jit(solution)/shard_map/g_upA_h/ppermute | solution.py:642
  620.7 45.3 %collective-permute-start.77 = (bf16[4,32,2048]{2,1,0:T(8,128)(2,1)}, bf16[4,32,2048]{2,1,0:T(8,128)(2,1)S(1)}, u32[]{:S(2)}, u32[]{:S(2)}) collective-permute-start(bf16[4,32,2048]{2,1,0:T(8,128)(2,1)} %slice.55), channel_id=1, source_target_pairs={{4,0},{0,4},{5,1},{1,5},{6,2},{2,6},{7,3},{3,7},{12,8},{8,12},{13,... | collective-permute-start | bytes 1572872 | tf_op jit(solution)/shard_map/input_grad_h/ppermute | solution.py:642
  (147 other events, 1925.5 us)
